TPU v7x, 256 devices: a whole 4x4x8 slice. The times are simulated.
256 devices in a mesh: blk: 64 (over y, z, x_lo), feat: 4 (over x_hi, core).
Axes of the slice: x: 4 (x_hi: 2, x_lo: 2; x = x_hi * 2 + x_lo), y: 4, z: 8, core: 2. Of those that a mesh axis runs over, the one named last changes fastest.
Arguments:
- image: bfloat16 [11264, 1152], P('blk', 'feat'), may hold values from -6 to 6
- text: bfloat16 [11264, 1152], P('blk', 'feat'), may hold values from -6 to 6
- scale: float32 [], replicated, may hold values from 0.05 to 0.12
- bias: float32 [], replicated, may hold values from -7 to -4
Outputs:
- image_grad: float32 [11264, 1152], P('blk', 'feat')
- text_grad: float32 [11264, 1152], P('blk', 'feat')
All inputs are finite; a program needn't handle non-finite values.
Results may differ from a plain program's by a relative error of at most 0.0013.
Values may be sent and summed in bfloat16 or wider, within the bound.
No kernel may reach another device: no remote copies, remote signals or barrier semaphores. Data moves between devices by JAX's collectives and lax.ppermute only.
A program may use at most 64 MiB of HBM per device.

v0:
```python
import jax
import jax.numpy as jnp
from jax import lax
from jax.sharding import PartitionSpec as P


def from_behind(block, axis, distance):
    devices = range(lax.axis_size(axis))
    route = [((i - distance) % len(devices), i) for i in devices]
    return lax.ppermute(block, axis, route)


def pair_grads(image_all, current, scale, bias, diag_start, own):
    dots = lax.dot_general(
        image_all, current, (((1,), (1,)), ((), ())), preferred_element_type=jnp.float32
    )
    logit = scale * dots + bias
    if own:
        row_index = lax.broadcasted_iota(jnp.int32, logit.shape, 0)
        col_index = diag_start + lax.broadcasted_iota(jnp.int32, logit.shape, 1)
        value = jnp.where(row_index == col_index, -jax.nn.sigmoid(-logit), jax.nn.sigmoid(logit))
    else:
        value = jax.nn.sigmoid(logit)
    slope = value.astype(jnp.bfloat16)
    image_add = jnp.dot(slope, current, preferred_element_type=jnp.float32)
    text_add = lax.dot_general(
        slope, image_all, (((0,), (0,)), ((), ())), preferred_element_type=jnp.float32
    )
    return (image_add, text_add)


def pass_both(current, accum):
    return (
        from_behind(current.astype(jnp.float32), "blk", 1).astype(current.dtype),
        from_behind(accum, "blk", 1),
    )


def shards(image, text, scale, bias):
    block_count = lax.axis_size("blk")
    image_all = lax.all_gather(image, "feat", axis=1, tiled=True)
    quarter = lax.all_to_all(text, "feat", split_axis=0, concat_axis=1, tiled=True)
    rows_q = quarter.shape[0]
    diag_start = lax.axis_index("feat") * rows_q
    image_acc, text_acc = pair_grads(image_all, quarter, scale, bias, diag_start, True)

    def visit(step, carry):
        current, accum, grad_img = carry
        current, accum = pass_both(current, accum)
        image_add, text_add = pair_grads(image_all, current, scale, bias, 0, False)
        return (current, accum + text_add, grad_img + image_add)

    current, text_acc, image_acc = lax.fori_loop(
        1, block_count, visit, (quarter, text_acc, image_acc)
    )
    text_acc = from_behind(text_acc, "blk", 1)
    image_grad = scale * lax.psum_scatter(image_acc, "feat", scatter_dimension=1, tiled=True)
    text_grad = lax.all_to_all(scale * text_acc, "feat", split_axis=1, concat_axis=0, tiled=True)
    return (image_grad, text_grad)


def solution(mesh):
    in_specs = (P("blk", "feat"), P("blk", "feat"), P(), P())
    out_specs = (P("blk", "feat"), P("blk", "feat"))
    return jax.shard_map(shards, mesh=mesh, in_specs=in_specs, out_specs=out_specs, check_vma=False)
```

profile of v0, /device:TPU:8, one launch (start us, length us, event | category | flops | bytes accessed | tf_op | source)
XLA Modules:
  0.0 872.0 jit_solution(9749662576289194764)
XLA Ops:
  14.4 9.5 %all-gather = bf16[4,288,176]{1,2,0:T(8,128)(2,1)S(1)} all-gather(bf16[1,288,176]{1,2,0:T(8,128)(2,1)} %bitcast.39), channel_id=1, replica_groups=mesh['blk'=64,'feat'=4] {'feat'}, dimensions={0}, use_global_device_ids=true | all-gather | bytes 506880 | tf_op jit(solution)/shard_map/all_gather | solution.py:41
  25.5 740.3 %while.14 = (s32[]{:T(128)}, bf16[44,1152]{1,0:T(8,128)(2,1)S(1)}, f32[44,1152]{1,0:T(8,128)S(1)}, f32[176,1152]{1,0:T(8,128)S(1)}, f32[]{:T(128)}, /*index=5*/bf16[176,1152]{1,0:T(8,128)(2,1)S(1)}, f32[]{:T(128)}, s32[]{:T(128)}) while((s32[]{:T(128)}, bf16[44,1152]{1,0:T(8,128)(2,1)S(1)}, f32[44,1152]{1,0:T(8,128)S(1)}, ...), condition=%wide.region_1.2_spmd, body=%wide.region_0.1_spmd.sunk | while | flops 53826432 | bytes 4507181 | solution.py:53
  40.2 8.7 collective-permute-done
  52.8 8.9 %collective-permute-done = bf16[44,1152]{1,0:T(8,128)(2,1)S(1)} collective-permute-done((bf16[44,1152]{1,0:T(8,128)(2,1)S(1)}, bf16[44,1152]{1,0:T(8,128)(2,1)S(1)}, u32[]{:S(2)}, u32[]{:S(2)}) %collective-permute-start) | collective-permute-done | bytes 101408 | tf_op jit(solution)/shard_map/while/body/eval_jaxpr/ppermute | solution.py:10
  64.7 8.2 collective-permute-done
  132.4 8.8 %collective-permute-done = bf16[44,1152]{1,0:T(8,128)(2,1)S(1)} collective-permute-done((bf16[44,1152]{1,0:T(8,128)(2,1)S(1)}, bf16[44,1152]{1,0:T(8,128)(2,1)S(1)}, u32[]{:S(2)}, u32[]{:S(2)}) %collective-permute-start) | collective-permute-done | bytes 101408 | tf_op jit(solution)/shard_map/while/body/eval_jaxpr/ppermute | solution.py:10
  146.1 8.8 %collective-permute-done = bf16[44,1152]{1,0:T(8,128)(2,1)S(1)} collective-permute-done((bf16[44,1152]{1,0:T(8,128)(2,1)S(1)}, bf16[44,1152]{1,0:T(8,128)(2,1)S(1)}, u32[]{:S(2)}, u32[]{:S(2)}) %collective-permute-start) | collective-permute-done | bytes 101408 | tf_op jit(solution)/shard_map/while/body/eval_jaxpr/ppermute | solution.py:10
  158.9 8.9 %collective-permute-done = bf16[44,1152]{1,0:T(8,128)(2,1)S(1)} collective-permute-done((bf16[44,1152]{1,0:T(8,128)(2,1)S(1)}, bf16[44,1152]{1,0:T(8,128)(2,1)S(1)}, u32[]{:S(2)}, u32[]{:S(2)}) %collective-permute-start) | collective-permute-done | bytes 101408 | tf_op jit(solution)/shard_map/while/body/eval_jaxpr/ppermute | solution.py:10
  170.9 8.3 collective-permute-done
  238.5 8.8 %collective-permute-done = bf16[44,1152]{1,0:T(8,128)(2,1)S(1)} collective-permute-done((bf16[44,1152]{1,0:T(8,128)(2,1)S(1)}, bf16[44,1152]{1,0:T(8,128)(2,1)S(1)}, u32[]{:S(2)}, u32[]{:S(2)}) %collective-permute-start) | collective-permute-done | bytes 101408 | tf_op jit(solution)/shard_map/while/body/eval_jaxpr/ppermute | solution.py:10
  252.2 8.8 %collective-permute-done = bf16[44,1152]{1,0:T(8,128)(2,1)S(1)} collective-permute-done((bf16[44,1152]{1,0:T(8,128)(2,1)S(1)}, bf16[44,1152]{1,0:T(8,128)(2,1)S(1)}, u32[]{:S(2)}, u32[]{:S(2)}) %collective-permute-start) | collective-permute-done | bytes 101408 | tf_op jit(solution)/shard_map/while/body/eval_jaxpr/ppermute | solution.py:10
  265.1 8.9 %collective-permute-done = bf16[44,1152]{1,0:T(8,128)(2,1)S(1)} collective-permute-done((bf16[44,1152]{1,0:T(8,128)(2,1)S(1)}, bf16[44,1152]{1,0:T(8,128)(2,1)S(1)}, u32[]{:S(2)}, u32[]{:S(2)}) %collective-permute-start) | collective-permute-done | bytes 101408 | tf_op jit(solution)/shard_map/while/body/eval_jaxpr/ppermute | solution.py:10
  277.1 8.3 collective-permute-done
  344.5 8.8 %collective-permute-done = bf16[44,1152]{1,0:T(8,128)(2,1)S(1)} collective-permute-done((bf16[44,1152]{1,0:T(8,128)(2,1)S(1)}, bf16[44,1152]{1,0:T(8,128)(2,1)S(1)}, u32[]{:S(2)}, u32[]{:S(2)}) %collective-permute-start) | collective-permute-done | bytes 101408 | tf_op jit(solution)/shard_map/while/body/eval_jaxpr/ppermute | solution.py:10
  358.4 8.8 %collective-permute-done = bf16[44,1152]{1,0:T(8,128)(2,1)S(1)} collective-permute-done((bf16[44,1152]{1,0:T(8,128)(2,1)S(1)}, bf16[44,1152]{1,0:T(8,128)(2,1)S(1)}, u32[]{:S(2)}, u32[]{:S(2)}) %collective-permute-start) | collective-permute-done | bytes 101408 | tf_op jit(solution)/shard_map/while/body/eval_jaxpr/ppermute | solution.py:10
  371.3 8.9 %collective-permute-done = bf16[44,1152]{1,0:T(8,128)(2,1)S(1)} collective-permute-done((bf16[44,1152]{1,0:T(8,128)(2,1)S(1)}, bf16[44,1152]{1,0:T(8,128)(2,1)S(1)}, u32[]{:S(2)}, u32[]{:S(2)}) %collective-permute-start) | collective-permute-done | bytes 101408 | tf_op jit(solution)/shard_map/while/body/eval_jaxpr/ppermute | solution.py:10
  383.5 8.4 collective-permute-done
  450.7 8.8 %collective-permute-done = bf16[44,1152]{1,0:T(8,128)(2,1)S(1)} collective-permute-done((bf16[44,1152]{1,0:T(8,128)(2,1)S(1)}, bf16[44,1152]{1,0:T(8,128)(2,1)S(1)}, u32[]{:S(2)}, u32[]{:S(2)}) %collective-permute-start) | collective-permute-done | bytes 101408 | tf_op jit(solution)/shard_map/while/body/eval_jaxpr/ppermute | solution.py:10
  464.6 8.8 %collective-permute-done = bf16[44,1152]{1,0:T(8,128)(2,1)S(1)} collective-permute-done((bf16[44,1152]{1,0:T(8,128)(2,1)S(1)}, bf16[44,1152]{1,0:T(8,128)(2,1)S(1)}, u32[]{:S(2)}, u32[]{:S(2)}) %collective-permute-start) | collective-permute-done | bytes 101408 | tf_op jit(solution)/shard_map/while/body/eval_jaxpr/ppermute | solution.py:10
  477.7 8.9 %collective-permute-done = bf16[44,1152]{1,0:T(8,128)(2,1)S(1)} collective-permute-done((bf16[44,1152]{1,0:T(8,128)(2,1)S(1)}, bf16[44,1152]{1,0:T(8,128)(2,1)S(1)}, u32[]{:S(2)}, u32[]{:S(2)}) %collective-permute-start) | collective-permute-done | bytes 101408 | tf_op jit(solution)/shard_map/while/body/eval_jaxpr/ppermute | solution.py:10
  490.0 8.6 collective-permute-done
  556.9 8.7 collective-permute-done
  570.7 8.8 %collective-permute-done = bf16[44,1152]{1,0:T(8,128)(2,1)S(1)} collective-permute-done((bf16[44,1152]{1,0:T(8,128)(2,1)S(1)}, bf16[44,1152]{1,0:T(8,128)(2,1)S(1)}, u32[]{:S(2)}, u32[]{:S(2)}) %collective-permute-start) | collective-permute-done | bytes 101408 | tf_op jit(solution)/shard_map/while/body/eval_jaxpr/ppermute | solution.py:10
  583.8 8.9 %collective-permute-done = bf16[44,1152]{1,0:T(8,128)(2,1)S(1)} collective-permute-done((bf16[44,1152]{1,0:T(8,128)(2,1)S(1)}, bf16[44,1152]{1,0:T(8,128)(2,1)S(1)}, u32[]{:S(2)}, u32[]{:S(2)}) %collective-permute-start) | collective-permute-done | bytes 101408 | tf_op jit(solution)/shard_map/while/body/eval_jaxpr/ppermute | solution.py:10
  596.1 8.6 collective-permute-done
  663.1 8.7 collective-permute-done
  676.9 8.8 %collective-permute-done = bf16[44,1152]{1,0:T(8,128)(2,1)S(1)} collective-permute-done((bf16[44,1152]{1,0:T(8,128)(2,1)S(1)}, bf16[44,1152]{1,0:T(8,128)(2,1)S(1)}, u32[]{:S(2)}, u32[]{:S(2)}) %collective-permute-start) | collective-permute-done | bytes 101408 | tf_op jit(solution)/shard_map/while/body/eval_jaxpr/ppermute | solution.py:10
  690.0 8.9 %collective-permute-done = bf16[44,1152]{1,0:T(8,128)(2,1)S(1)} collective-permute-done((bf16[44,1152]{1,0:T(8,128)(2,1)S(1)}, bf16[44,1152]{1,0:T(8,128)(2,1)S(1)}, u32[]{:S(2)}, u32[]{:S(2)}) %collective-permute-start) | collective-permute-done | bytes 101408 | tf_op jit(solution)/shard_map/while/body/eval_jaxpr/ppermute | solution.py:10
  702.3 8.8 %collective-permute-done = bf16[44,1152]{1,0:T(8,128)(2,1)S(1)} collective-permute-done((bf16[44,1152]{1,0:T(8,128)(2,1)S(1)}, bf16[44,1152]{1,0:T(8,128)(2,1)S(1)}, u32[]{:S(2)}, u32[]{:S(2)}) %collective-permute-start) | collective-permute-done | bytes 101408 | tf_op jit(solution)/shard_map/while/body/eval_jaxpr/ppermute | solution.py:10
  767.3 8.9 %collective-permute-done.2 = f32[44,1152]{1,0:T(8,128)S(1)} collective-permute-done((f32[44,1152]{1,0:T(8,128)S(1)}, f32[44,1152]{1,0:T(8,128)S(1)}, u32[]{:S(2)}, u32[]{:S(2)}) %collective-permute-start.2) | collective-permute-done | bytes 202784 | tf_op jit(solution)/shard_map/ppermute | solution.py:10
  776.5 12.7 %all_to_all.38 = f32[44,4,288]{2,0,1:T(8,128)S(1)} all-to-all(f32[44,4,288]{2,0,1:T(8,128)S(1)} %copy.18), channel_id=1, replica_groups=mesh['blk'=64,'feat'=4] {'feat'}, dimensions={1} | all-to-all | bytes 405504 | tf_op jit(solution)/shard_map/all_to_all | solution.py:58
  789.9 73.4 %reduce-scatter.4.cloned.1.call-done = f32[288,176]{1,0:T(8,128)} async-done(((f32[1152,176]{1,0:T(8,128)}), f32[288,176]{1,0:T(8,128)}) %reduce-scatter.4.cloned.1.call-update) | async-done | bytes 202768
  (498 shorter events, 513.6 us)
Async XLA Ops:
  8.8 15.7 %all-to-all-start = ((bf16[4,44,288]{2,1,0:T(8,128)(2,1)}), bf16[4,44,288]{2,1,0:T(8,128)(2,1)S(1)}, u32[]{:S(2)}, u32[]{:S(2)}) async-start(bf16[4,44,288]{2,1,0:T(8,128)(2,1)} %all_to_all.28), calls=%async_computation | async-start | bytes 294912 | tf_op jit(solution)/shard_map/all_to_all | solution.py:42
  13.1 850.3 %reduce-scatter.4.cloned.1.call-start = ((), (), s32[]{:S(2)}) async-start(), calls=%async_computation.3 | async-start | bytes 1474560
  26.2 13.5 %collective-permute-start.1 = (f32[44,1152]{1,0:T(8,128)S(1)}, f32[44,1152]{1,0:T(8,128)S(1)}, u32[]{:S(2)}, u32[]{:S(2)}) collective-permute-start(f32[44,1152]{1,0:T(8,128)S(1)} %get-tuple-element.109), channel_id=1, source_target_pairs={{252,0},{0,4},{4,8},{8,12},{12,16},{16,20},{20,24},{24,28},{28,32}... | collective-permute-start | bytes 608264 | tf_op jit(solution)/shard_map/while/body/eval_jaxpr/ppermute | solution.py:10
  40.0 12.5 %collective-permute-start.1 = (f32[44,1152]{1,0:T(8,128)S(1)}, f32[44,1152]{1,0:T(8,128)S(1)}, u32[]{:S(2)}, u32[]{:S(2)}) collective-permute-start(f32[44,1152]{1,0:T(8,128)S(1)} %get-tuple-element.109), channel_id=1, source_target_pairs={{252,0},{0,4},{4,8},{8,12},{12,16},{16,20},{20,24},{24,28},{28,32}... | collective-permute-start | bytes 608264 | tf_op jit(solution)/shard_map/while/body/eval_jaxpr/ppermute | solution.py:10
  52.7 11.6 %collective-permute-start.1 = (f32[44,1152]{1,0:T(8,128)S(1)}, f32[44,1152]{1,0:T(8,128)S(1)}, u32[]{:S(2)}, u32[]{:S(2)}) collective-permute-start(f32[44,1152]{1,0:T(8,128)S(1)} %get-tuple-element.109), channel_id=1, source_target_pairs={{252,0},{0,4},{4,8},{8,12},{12,16},{16,20},{20,24},{24,28},{28,32}... | collective-permute-start | bytes 608264 | tf_op jit(solution)/shard_map/while/body/eval_jaxpr/ppermute | solution.py:10
  107.3 11.6 %collective-permute-start.1 = (f32[44,1152]{1,0:T(8,128)S(1)}, f32[44,1152]{1,0:T(8,128)S(1)}, u32[]{:S(2)}, u32[]{:S(2)}) collective-permute-start(f32[44,1152]{1,0:T(8,128)S(1)} %get-tuple-element.109), channel_id=1, source_target_pairs={{252,0},{0,4},{4,8},{8,12},{12,16},{16,20},{20,24},{24,28},{28,32}... | collective-permute-start | bytes 608264 | tf_op jit(solution)/shard_map/while/body/eval_jaxpr/ppermute | solution.py:10
  119.2 12.8 %collective-permute-start.1 = (f32[44,1152]{1,0:T(8,128)S(1)}, f32[44,1152]{1,0:T(8,128)S(1)}, u32[]{:S(2)}, u32[]{:S(2)}) collective-permute-start(f32[44,1152]{1,0:T(8,128)S(1)} %get-tuple-element.109), channel_id=1, source_target_pairs={{252,0},{0,4},{4,8},{8,12},{12,16},{16,20},{20,24},{24,28},{28,32}... | collective-permute-start | bytes 608264 | tf_op jit(solution)/shard_map/while/body/eval_jaxpr/ppermute | solution.py:10
  132.3 13.4 %collective-permute-start.1 = (f32[44,1152]{1,0:T(8,128)S(1)}, f32[44,1152]{1,0:T(8,128)S(1)}, u32[]{:S(2)}, u32[]{:S(2)}) collective-permute-start(f32[44,1152]{1,0:T(8,128)S(1)} %get-tuple-element.109), channel_id=1, source_target_pairs={{252,0},{0,4},{4,8},{8,12},{12,16},{16,20},{20,24},{24,28},{28,32}... | collective-permute-start | bytes 608264 | tf_op jit(solution)/shard_map/while/body/eval_jaxpr/ppermute | solution.py:10
  146.0 12.5 %collective-permute-start.1 = (f32[44,1152]{1,0:T(8,128)S(1)}, f32[44,1152]{1,0:T(8,128)S(1)}, u32[]{:S(2)}, u32[]{:S(2)}) collective-permute-start(f32[44,1152]{1,0:T(8,128)S(1)} %get-tuple-element.109), channel_id=1, source_target_pairs={{252,0},{0,4},{4,8},{8,12},{12,16},{16,20},{20,24},{24,28},{28,32}... | collective-permute-start | bytes 608264 | tf_op jit(solution)/shard_map/while/body/eval_jaxpr/ppermute | solution.py:10
  158.8 11.6 %collective-permute-start.1 = (f32[44,1152]{1,0:T(8,128)S(1)}, f32[44,1152]{1,0:T(8,128)S(1)}, u32[]{:S(2)}, u32[]{:S(2)}) collective-permute-start(f32[44,1152]{1,0:T(8,128)S(1)} %get-tuple-element.109), channel_id=1, source_target_pairs={{252,0},{0,4},{4,8},{8,12},{12,16},{16,20},{20,24},{24,28},{28,32}... | collective-permute-start | bytes 608264 | tf_op jit(solution)/shard_map/while/body/eval_jaxpr/ppermute | solution.py:10
  213.4 11.6 %collective-permute-start.1 = (f32[44,1152]{1,0:T(8,128)S(1)}, f32[44,1152]{1,0:T(8,128)S(1)}, u32[]{:S(2)}, u32[]{:S(2)}) collective-permute-start(f32[44,1152]{1,0:T(8,128)S(1)} %get-tuple-element.109), channel_id=1, source_target_pairs={{252,0},{0,4},{4,8},{8,12},{12,16},{16,20},{20,24},{24,28},{28,32}... | collective-permute-start | bytes 608264 | tf_op jit(solution)/shard_map/while/body/eval_jaxpr/ppermute | solution.py:10
  225.3 12.7 %collective-permute-start.1 = (f32[44,1152]{1,0:T(8,128)S(1)}, f32[44,1152]{1,0:T(8,128)S(1)}, u32[]{:S(2)}, u32[]{:S(2)}) collective-permute-start(f32[44,1152]{1,0:T(8,128)S(1)} %get-tuple-element.109), channel_id=1, source_target_pairs={{252,0},{0,4},{4,8},{8,12},{12,16},{16,20},{20,24},{24,28},{28,32}... | collective-permute-start | bytes 608264 | tf_op jit(solution)/shard_map/while/body/eval_jaxpr/ppermute | solution.py:10
  238.4 13.4 %collective-permute-start.1 = (f32[44,1152]{1,0:T(8,128)S(1)}, f32[44,1152]{1,0:T(8,128)S(1)}, u32[]{:S(2)}, u32[]{:S(2)}) collective-permute-start(f32[44,1152]{1,0:T(8,128)S(1)} %get-tuple-element.109), channel_id=1, source_target_pairs={{252,0},{0,4},{4,8},{8,12},{12,16},{16,20},{20,24},{24,28},{28,32}... | collective-permute-start | bytes 608264 | tf_op jit(solution)/shard_map/while/body/eval_jaxpr/ppermute | solution.py:10
  252.1 12.6 %collective-permute-start.1 = (f32[44,1152]{1,0:T(8,128)S(1)}, f32[44,1152]{1,0:T(8,128)S(1)}, u32[]{:S(2)}, u32[]{:S(2)}) collective-permute-start(f32[44,1152]{1,0:T(8,128)S(1)} %get-tuple-element.109), channel_id=1, source_target_pairs={{252,0},{0,4},{4,8},{8,12},{12,16},{16,20},{20,24},{24,28},{28,32}... | collective-permute-start | bytes 608264 | tf_op jit(solution)/shard_map/while/body/eval_jaxpr/ppermute | solution.py:10
  265.0 11.7 %collective-permute-start.1 = (f32[44,1152]{1,0:T(8,128)S(1)}, f32[44,1152]{1,0:T(8,128)S(1)}, u32[]{:S(2)}, u32[]{:S(2)}) collective-permute-start(f32[44,1152]{1,0:T(8,128)S(1)} %get-tuple-element.109), channel_id=1, source_target_pairs={{252,0},{0,4},{4,8},{8,12},{12,16},{16,20},{20,24},{24,28},{28,32}... | collective-permute-start | bytes 608264 | tf_op jit(solution)/shard_map/while/body/eval_jaxpr/ppermute | solution.py:10
  319.7 11.5 %collective-permute-start.1 = (f32[44,1152]{1,0:T(8,128)S(1)}, f32[44,1152]{1,0:T(8,128)S(1)}, u32[]{:S(2)}, u32[]{:S(2)}) collective-permute-start(f32[44,1152]{1,0:T(8,128)S(1)} %get-tuple-element.109), channel_id=1, source_target_pairs={{252,0},{0,4},{4,8},{8,12},{12,16},{16,20},{20,24},{24,28},{28,32}... | collective-permute-start | bytes 608264 | tf_op jit(solution)/shard_map/while/body/eval_jaxpr/ppermute | solution.py:10
  331.5 12.7 %collective-permute-start.1 = (f32[44,1152]{1,0:T(8,128)S(1)}, f32[44,1152]{1,0:T(8,128)S(1)}, u32[]{:S(2)}, u32[]{:S(2)}) collective-permute-start(f32[44,1152]{1,0:T(8,128)S(1)} %get-tuple-element.109), channel_id=1, source_target_pairs={{252,0},{0,4},{4,8},{8,12},{12,16},{16,20},{20,24},{24,28},{28,32}... | collective-permute-start | bytes 608264 | tf_op jit(solution)/shard_map/while/body/eval_jaxpr/ppermute | solution.py:10
  344.4 13.5 %collective-permute-start.1 = (f32[44,1152]{1,0:T(8,128)S(1)}, f32[44,1152]{1,0:T(8,128)S(1)}, u32[]{:S(2)}, u32[]{:S(2)}) collective-permute-start(f32[44,1152]{1,0:T(8,128)S(1)} %get-tuple-element.109), channel_id=1, source_target_pairs={{252,0},{0,4},{4,8},{8,12},{12,16},{16,20},{20,24},{24,28},{28,32}... | collective-permute-start | bytes 608264 | tf_op jit(solution)/shard_map/while/body/eval_jaxpr/ppermute | solution.py:10
  358.3 12.7 %collective-permute-start.1 = (f32[44,1152]{1,0:T(8,128)S(1)}, f32[44,1152]{1,0:T(8,128)S(1)}, u32[]{:S(2)}, u32[]{:S(2)}) collective-permute-start(f32[44,1152]{1,0:T(8,128)S(1)} %get-tuple-element.109), channel_id=1, source_target_pairs={{252,0},{0,4},{4,8},{8,12},{12,16},{16,20},{20,24},{24,28},{28,32}... | collective-permute-start | bytes 608264 | tf_op jit(solution)/shard_map/while/body/eval_jaxpr/ppermute | solution.py:10
  371.3 11.8 %collective-permute-start.1 = (f32[44,1152]{1,0:T(8,128)S(1)}, f32[44,1152]{1,0:T(8,128)S(1)}, u32[]{:S(2)}, u32[]{:S(2)}) collective-permute-start(f32[44,1152]{1,0:T(8,128)S(1)} %get-tuple-element.109), channel_id=1, source_target_pairs={{252,0},{0,4},{4,8},{8,12},{12,16},{16,20},{20,24},{24,28},{28,32}... | collective-permute-start | bytes 608264 | tf_op jit(solution)/shard_map/while/body/eval_jaxpr/ppermute | solution.py:10
  437.7 12.5 %collective-permute-start.1 = (f32[44,1152]{1,0:T(8,128)S(1)}, f32[44,1152]{1,0:T(8,128)S(1)}, u32[]{:S(2)}, u32[]{:S(2)}) collective-permute-start(f32[44,1152]{1,0:T(8,128)S(1)} %get-tuple-element.109), channel_id=1, source_target_pairs={{252,0},{0,4},{4,8},{8,12},{12,16},{16,20},{20,24},{24,28},{28,32}... | collective-permute-start | bytes 608264 | tf_op jit(solution)/shard_map/while/body/eval_jaxpr/ppermute | solution.py:10
  450.6 13.7 %collective-permute-start.1 = (f32[44,1152]{1,0:T(8,128)S(1)}, f32[44,1152]{1,0:T(8,128)S(1)}, u32[]{:S(2)}, u32[]{:S(2)}) collective-permute-start(f32[44,1152]{1,0:T(8,128)S(1)} %get-tuple-element.109), channel_id=1, source_target_pairs={{252,0},{0,4},{4,8},{8,12},{12,16},{16,20},{20,24},{24,28},{28,32}... | collective-permute-start | bytes 608264 | tf_op jit(solution)/shard_map/while/body/eval_jaxpr/ppermute | solution.py:10
  464.5 12.8 %collective-permute-start.1 = (f32[44,1152]{1,0:T(8,128)S(1)}, f32[44,1152]{1,0:T(8,128)S(1)}, u32[]{:S(2)}, u32[]{:S(2)}) collective-permute-start(f32[44,1152]{1,0:T(8,128)S(1)} %get-tuple-element.109), channel_id=1, source_target_pairs={{252,0},{0,4},{4,8},{8,12},{12,16},{16,20},{20,24},{24,28},{28,32}... | collective-permute-start | bytes 608264 | tf_op jit(solution)/shard_map/while/body/eval_jaxpr/ppermute | solution.py:10
  477.6 12.0 %collective-permute-start.1 = (f32[44,1152]{1,0:T(8,128)S(1)}, f32[44,1152]{1,0:T(8,128)S(1)}, u32[]{:S(2)}, u32[]{:S(2)}) collective-permute-start(f32[44,1152]{1,0:T(8,128)S(1)} %get-tuple-element.109), channel_id=1, source_target_pairs={{252,0},{0,4},{4,8},{8,12},{12,16},{16,20},{20,24},{24,28},{28,32}... | collective-permute-start | bytes 608264 | tf_op jit(solution)/shard_map/while/body/eval_jaxpr/ppermute | solution.py:10
  544.1 12.4 %collective-permute-start.1 = (f32[44,1152]{1,0:T(8,128)S(1)}, f32[44,1152]{1,0:T(8,128)S(1)}, u32[]{:S(2)}, u32[]{:S(2)}) collective-permute-start(f32[44,1152]{1,0:T(8,128)S(1)} %get-tuple-element.109), channel_id=1, source_target_pairs={{252,0},{0,4},{4,8},{8,12},{12,16},{16,20},{20,24},{24,28},{28,32}... | collective-permute-start | bytes 608264 | tf_op jit(solution)/shard_map/while/body/eval_jaxpr/ppermute | solution.py:10
  556.8 13.5 %collective-permute-start.1 = (f32[44,1152]{1,0:T(8,128)S(1)}, f32[44,1152]{1,0:T(8,128)S(1)}, u32[]{:S(2)}, u32[]{:S(2)}) collective-permute-start(f32[44,1152]{1,0:T(8,128)S(1)} %get-tuple-element.109), channel_id=1, source_target_pairs={{252,0},{0,4},{4,8},{8,12},{12,16},{16,20},{20,24},{24,28},{28,32}... | collective-permute-start | bytes 608264 | tf_op jit(solution)/shard_map/while/body/eval_jaxpr/ppermute | solution.py:10
  570.6 12.8 %collective-permute-start.1 = (f32[44,1152]{1,0:T(8,128)S(1)}, f32[44,1152]{1,0:T(8,128)S(1)}, u32[]{:S(2)}, u32[]{:S(2)}) collective-permute-start(f32[44,1152]{1,0:T(8,128)S(1)} %get-tuple-element.109), channel_id=1, source_target_pairs={{252,0},{0,4},{4,8},{8,12},{12,16},{16,20},{20,24},{24,28},{28,32}... | collective-permute-start | bytes 608264 | tf_op jit(solution)/shard_map/while/body/eval_jaxpr/ppermute | solution.py:10
  583.8 12.0 %collective-permute-start.1 = (f32[44,1152]{1,0:T(8,128)S(1)}, f32[44,1152]{1,0:T(8,128)S(1)}, u32[]{:S(2)}, u32[]{:S(2)}) collective-permute-start(f32[44,1152]{1,0:T(8,128)S(1)} %get-tuple-element.109), channel_id=1, source_target_pairs={{252,0},{0,4},{4,8},{8,12},{12,16},{16,20},{20,24},{24,28},{28,32}... | collective-permute-start | bytes 608264 | tf_op jit(solution)/shard_map/while/body/eval_jaxpr/ppermute | solution.py:10
  650.3 12.4 %collective-permute-start.1 = (f32[44,1152]{1,0:T(8,128)S(1)}, f32[44,1152]{1,0:T(8,128)S(1)}, u32[]{:S(2)}, u32[]{:S(2)}) collective-permute-start(f32[44,1152]{1,0:T(8,128)S(1)} %get-tuple-element.109), channel_id=1, source_target_pairs={{252,0},{0,4},{4,8},{8,12},{12,16},{16,20},{20,24},{24,28},{28,32}... | collective-permute-start | bytes 608264 | tf_op jit(solution)/shard_map/while/body/eval_jaxpr/ppermute | solution.py:10
  663.0 13.5 %collective-permute-start.1 = (f32[44,1152]{1,0:T(8,128)S(1)}, f32[44,1152]{1,0:T(8,128)S(1)}, u32[]{:S(2)}, u32[]{:S(2)}) collective-permute-start(f32[44,1152]{1,0:T(8,128)S(1)} %get-tuple-element.109), channel_id=1, source_target_pairs={{252,0},{0,4},{4,8},{8,12},{12,16},{16,20},{20,24},{24,28},{28,32}... | collective-permute-start | bytes 608264 | tf_op jit(solution)/shard_map/while/body/eval_jaxpr/ppermute | solution.py:10
  676.8 12.8 %collective-permute-start.1 = (f32[44,1152]{1,0:T(8,128)S(1)}, f32[44,1152]{1,0:T(8,128)S(1)}, u32[]{:S(2)}, u32[]{:S(2)}) collective-permute-start(f32[44,1152]{1,0:T(8,128)S(1)} %get-tuple-element.109), channel_id=1, source_target_pairs={{252,0},{0,4},{4,8},{8,12},{12,16},{16,20},{20,24},{24,28},{28,32}... | collective-permute-start | bytes 608264 | tf_op jit(solution)/shard_map/while/body/eval_jaxpr/ppermute | solution.py:10
  689.9 12.0 %collective-permute-start.1 = (f32[44,1152]{1,0:T(8,128)S(1)}, f32[44,1152]{1,0:T(8,128)S(1)}, u32[]{:S(2)}, u32[]{:S(2)}) collective-permute-start(f32[44,1152]{1,0:T(8,128)S(1)} %get-tuple-element.109), channel_id=1, source_target_pairs={{252,0},{0,4},{4,8},{8,12},{12,16},{16,20},{20,24},{24,28},{28,32}... | collective-permute-start | bytes 608264 | tf_op jit(solution)/shard_map/while/body/eval_jaxpr/ppermute | solution.py:10
  (97 other events, 879.4 us)
Sparse Core Ops, SparseCore 0:
  767.3 95.9 reduce-scatter.3
where the time goes:
time: 874 us; the launch traced here: 872 us
  waiting for transfers between devices  673 us (77%)
  matrix products  133 us (15%)
  blocking collectives  22.2 us (3%)
  starting transfers between devices  18.3 us (2%)
  between operations  15.4 us (2%)
    ppermute x127, waiting for transfers between devices, from_behind(): return lax.ppermute(block, axis, route)  600 us
    dot_general x64, matrix products, pair_grads(): lax.dot_general(image_all, current, (((1,), (1,)), ((), ())), preferred_e...  100 us
    unnamed x2, waiting for transfers between devices  73.4 us
    dot_general x64, matrix products, pair_grads(): image_add = jnp.dot(slope, current, preferred_element_type=jnp.float32)  19.7 us
  transfers between devices with their start and end apart: 129, of which 128 were waited for; matrix products, arithmetic and copies ran while one was open for 14% of the time, Pallas kernels for 0%

commit v1 on v0

v1 whole, which is shorter than its diff:
```python
import jax
import jax.numpy as jnp
from jax import lax
from jax.experimental import pallas as pl
from jax.experimental.pallas import tpu as pltpu
from jax.sharding import Mesh
from jax.sharding import PartitionSpec as P

AXES = ("y", "z", "l", "h", "c")
SIZES = {"y": 4, "z": 8, "l": 2, "h": 2, "c": 2}
ROWS = 88
SLOT = 96
QUART = 288
HALF = 576
WIDE = 640
F32 = jnp.float32
BF16 = jnp.bfloat16
F16 = jnp.float16
VMEM = pl.BlockSpec(memory_space=pltpu.VMEM)
SMEM = pl.BlockSpec(memory_space=pltpu.SMEM)


def shape(dims, dtype):
    return jax.ShapeDtypeStruct(dims, dtype)


def call(kernel, outs, *args, smem=0, scratch=(), flops=0, mib=32):
    specs = [VMEM] * (len(args) - smem) + [SMEM] * smem
    moved = sum(a.size * a.dtype.itemsize for a in (*args, *outs))
    return pl.pallas_call(
        kernel,
        out_shape=outs,
        in_specs=specs,
        out_specs=[VMEM] * len(outs),
        scratch_shapes=list(scratch),
        compiler_params=pltpu.CompilerParams(vmem_limit_bytes=mib * 2**20),
        cost_estimate=pl.CostEstimate(flops=flops, bytes_accessed=moved, transcendentals=0),
    )(*args)


def flip(x, axis, mask):
    axes = axis if isinstance(axis, tuple) else (axis,)
    count = 1
    for a in axes:
        count *= SIZES[a]
    return lax.ppermute(x, axis, [(i, i ^ mask) for i in range(count)])


def split_kernel(image, text, image_keep, image_send, text_keep, text_send):
    for source, axis, keep, send in (
        (image, "h", image_keep, image_send),
        (text, "c", text_keep, text_send),
    ):
        low = lax.axis_index(axis) == 0
        x = source[...].astype(F32)
        first, second = x[:ROWS], x[ROWS:]
        keep[...] = jnp.where(low, first, second).astype(BF16)
        send[...] = jnp.where(low, second, first).astype(BF16)


def join_kernel(keep, recv, piece):
    joined = jnp.concatenate(
        [keep[...].astype(F32), recv[...].astype(F32), jnp.zeros((ROWS, WIDE - HALF), F32)], axis=1
    )
    piece[...] = jnp.concatenate([joined, jnp.zeros((SLOT - ROWS, WIDE), F32)], axis=0).astype(BF16)


def scaled(x):
    most = jnp.max(jnp.max(jnp.abs(x), axis=0, keepdims=True), axis=1, keepdims=True)
    power = jnp.floor(jnp.log2(jnp.maximum(most, 1e-30)))
    lane = lax.broadcasted_iota(jnp.int32, x.shape, 1)
    return jnp.where(lane < HALF, x * jnp.exp2(13.0 - power), power)


def unscaled(p):
    return p * jnp.exp2(p[:1, HALF : HALF + 1] - 13.0)


def pair_kernel(*refs):
    image_own, image_swap, text = refs[0:4], refs[4:8], refs[8:12]
    scale_ref, bias_ref = refs[12:14]
    keep, send, text_own = refs[14:17]
    text_out = refs[17:20]
    images, texts, slope, text_sum = refs[20:24]
    scale, bias = scale_ref[0], bias_ref[0]
    zeros = jnp.zeros((SLOT, WIDE - HALF), BF16)
    for k in range(4):
        for p in range(2):
            rows = pl.ds(SLOT * (2 * k + p), SLOT)
            images[rows, 0:WIDE] = image_own[k][p]
            images[rows, WIDE:] = image_swap[k][p]
            a, b = text[k][2 * p], text[k][2 * p + 1]
            texts[rows, 0:WIDE] = jnp.concatenate([a[:, :QUART], b[:, :QUART], zeros], axis=1)
            texts[rows, WIDE:] = jnp.concatenate([a[:, QUART:HALF], b[:, QUART:HALF], zeros], axis=1)
    own = lax.axis_index("h") == lax.axis_index("c")
    for j in range(3):
        cols = pl.ds(256 * j, 256)
        dots = lax.dot_general(
            images[...], texts[cols, :], (((1,), (1,)), ((), ())), preferred_element_type=F32
        )
        logit = scale * dots + bias
        if j == 0:
            row = lax.broadcasted_iota(jnp.int32, logit.shape, 0)
            col = lax.broadcasted_iota(jnp.int32, logit.shape, 1)
            paired = (row == col) & (row < ROWS) & own
            value = jnp.where(paired, -jax.nn.sigmoid(-logit), jax.nn.sigmoid(logit))
        else:
            value = jax.nn.sigmoid(logit)
        value = value.astype(BF16)
        slope[:, cols] = value
        text_sum[cols, :] = lax.dot_general(
            value, images[...], (((0,), (0,)), ((), ())), preferred_element_type=F32
        )
    add = jnp.dot(slope[...], texts[...], preferred_element_type=F32)
    for s in range(8):
        keep[s] = add[SLOT * s : SLOT * (s + 1), :WIDE]
        send[s] = add[SLOT * s : SLOT * (s + 1), WIDE:]
    pad = jnp.zeros((SLOT, WIDE - HALF), F32)
    for e in range(4):
        parts = []
        for p in range(2):
            x = text_sum[pl.ds(SLOT * (2 * e + p), SLOT), :]
            for d in range(2):
                low, high = x[:, QUART * d : QUART * (d + 1)], x[:, WIDE + QUART * d : WIDE + QUART * (d + 1)]
                parts.append(jnp.concatenate([low, high, pad], axis=1))
        if e == 0:
            for n in range(4):
                text_own[n] = parts[n]
        else:
            for n in range(4):
                text_out[e - 1][n] = scaled(parts[n])


def image_first_kernel(keep, recv, own, *outs):
    for s in range(8):
        x = keep[s] + recv[s]
        if s < 2:
            own[s] = x
        else:
            outs[s // 2 - 1][s % 2] = scaled(x)


def text_second_kernel(own, r1, r2, r3, kept, *outs):
    for n in range(4):
        x = own[n] + unscaled(r1[n]) + unscaled(r2[n]) + unscaled(r3[n])
        if n == 0:
            kept[...] = x
        else:
            outs[n - 1][...] = scaled(x)


def image_second_kernel(own, r1, r2, r3, kept, out):
    for n in range(2):
        x = own[n] + unscaled(r1[n]) + unscaled(r2[n]) + unscaled(r3[n])
        if n == 0:
            kept[...] = x
        else:
            out[...] = scaled(x)


def last_kernel(*refs):
    *parts, scale, keep, send = refs
    x = parts[0][...]
    for part in parts[1:]:
        x = x + unscaled(part[...])
    x = scale[0] * x[:ROWS]
    keep[...] = x[:, :QUART]
    send[...] = x[:, QUART:HALF]


def place_kernel(image_keep, image_recv, text_keep, text_recv, image_out, text_out):
    for axis, keep, recv, out in (
        ("h", image_keep, image_recv, image_out),
        ("c", text_keep, text_recv, text_out),
    ):
        low = lax.axis_index(axis) == 0
        a, b = keep[...], recv[...]
        out[:ROWS] = jnp.where(low, a, b)
        out[ROWS:] = jnp.where(low, b, a)


def shards(image, text, scale, bias):
    scale, bias = scale.reshape(1), bias.reshape(1)
    half = shape((ROWS, QUART), BF16)
    image_keep, image_send, text_keep, text_send = call(split_kernel, [half] * 4, image, text)
    image_recv = flip(image_send, "h", 1)
    text_recv = flip(text_send, "c", 1)
    piece = [shape((SLOT, WIDE), BF16)]
    (text_piece,) = call(join_kernel, piece, text_keep, text_recv)
    (image_piece,) = call(join_kernel, piece, image_keep, image_recv)

    x_axes = ("l", "h")
    texts = jnp.stack([text_piece] + [flip(text_piece, x_axes, n) for n in (1, 2, 3)])
    images = jnp.stack([image_piece, flip(image_piece, "z", 1)])
    text_all = [texts] + [flip(texts, "y", n) for n in (1, 2, 3)]
    image_all = [images] + [flip(images, "z", n) for n in (2, 4, 6)]
    image_swap = [flip(x, "c", 1) for x in image_all]

    big = shape((8, SLOT, WIDE), F32)
    four, two, one = (shape((*d, SLOT, WIDE), F32) for d in ((4,), (2,), ()))
    keep, send, text_own, *text_out = call(
        pair_kernel,
        [big, big, four, four, four, four],
        *image_all,
        *image_swap,
        *text_all,
        scale,
        bias,
        smem=2,
        scratch=[
            pltpu.VMEM((8 * SLOT, 2 * WIDE), BF16),
            pltpu.VMEM((8 * SLOT, 2 * WIDE), BF16),
            pltpu.VMEM((8 * SLOT, 8 * SLOT), BF16),
            pltpu.VMEM((8 * SLOT, 2 * WIDE), F32),
        ],
        flops=6 * 704 * 704 * 1152,
        mib=56,
    )

    def across(x, axis, mask):
        return flip(x.astype(F16), axis, mask).astype(F32)

    recv = flip(send, "c", 1)
    text_in = [across(x, "y", n) for n, x in zip((1, 2, 3), text_out)]
    image_own, *image_out = call(image_first_kernel, [two] * 4, keep, recv)
    image_in = [across(x, "z", n) for n, x in zip((2, 4, 6), image_out)]
    text_own, *text_out = call(text_second_kernel, [one] * 4, text_own, *text_in)
    text_in = [across(x, x_axes, n) for n, x in zip((1, 2, 3), text_out)]
    image_own, image_out = call(image_second_kernel, [one] * 2, image_own, *image_in)
    image_in = across(image_out, "z", 1)
    part = [shape((ROWS, QUART), F32)] * 2
    image_keep, image_send = call(last_kernel, part, image_own, image_in, scale, smem=1)
    image_recv = flip(image_send, "h", 1)
    text_keep, text_send = call(last_kernel, part, text_own, *text_in, scale, smem=1)
    text_recv = flip(text_send, "c", 1)
    grads = [shape((2 * ROWS, QUART), F32)] * 2
    return tuple(call(place_kernel, grads, image_keep, image_recv, text_keep, text_recv))


def solution(mesh):
    fine = Mesh(mesh.devices.reshape([SIZES[a] for a in AXES]), AXES)
    spec = P(("y", "z", "l"), ("h", "c"))
    return jax.shard_map(
        shards, mesh=fine, in_specs=(spec, spec, P(), P()), out_specs=(spec, spec), check_vma=False
    )
```

time: 874 us -> 134 us (0.15)
  waiting for transfers between devices: 673 us -> 66.8 us
  matrix products: 133 us -> 0 us
  starting transfers between devices: 18.3 us -> 45.6 us
  blocking collectives: 22.2 us -> 0 us
  Pallas kernels: 0 us -> 13.1 us
  between operations: 15.4 us -> 2.32 us
    ppermute x127 -> x29, waiting for transfers between devices: 600 us -> 66.8 us  [flip(): return lax.ppermute(x, axis, [(i, i ^ mask) for i in range(count)])]
    dot_general x192 -> x0, matrix products: 133 us -> none  [the longest x64 100 us: pair_grads(): lax.dot_general(image_all, current, (((1,), (1,)), ((), ())), preferred_e...]
    unnamed x2 -> x0, waiting for transfers between devices: 73.4 us -> none
    ppermute x127 -> x29, starting transfers between devices: 14 us -> 45.6 us  [flip(): return lax.ppermute(x, axis, [(i, i ^ mask) for i in range(count)])]
    pallas_call x0 -> x10, Pallas kernels: none -> 13.1 us  [call(): pl.pallas_call(kernel, out_shape=outs, in_specs=specs, out_specs=[VMEM] *...]
    all_to_all x1 -> x0, blocking collectives: 12.7 us -> none  [shards(): lax.all_to_all(scale * text_acc, 'feat', split_axis=1, concat_axis=0, til...]
    all_gather x1 -> x0, blocking collectives: 9.51 us -> none  [shards(): image_all = lax.all_gather(image, 'feat', axis=1, tiled=True)]
  transfers between devices with their start and end apart: 129 -> 29, of which waited for: 128 -> 12; matrix products, arithmetic and copies ran while one was open for 14% -> 3% of each run, Pallas kernels for 0% -> 1%
where the time goes in v1:
time: 134 us
  waiting for transfers between devices  66.8 us (50%)
  starting transfers between devices  45.6 us (34%)
  Pallas kernels  13.1 us (10%)
  other arithmetic  3.37 us (3%)
  local copies, waits for them, and re-layouts  2.6 us (2%)
  between operations  2.32 us (2%)
    ppermute x29, waiting for transfers between devices, flip(): return lax.ppermute(x, axis, [(i, i ^ mask) for i in range(count)])  66.8 us
    ppermute x29, starting transfers between devices, flip(): return lax.ppermute(x, axis, [(i, i ^ mask) for i in range(count)])  45.6 us
    pallas_call x10, Pallas kernels, call(): pl.pallas_call(kernel, out_shape=outs, in_specs=specs, out_specs=[VMEM] *...  13.1 us
    convert_element_type x20, other arithmetic, across(): return flip(x.astype(F16), axis, mask).astype(F32)  3.26 us
  transfers between devices with their start and end apart: 29, of which 12 were waited for; matrix products, arithmetic and copies ran while one was open for 3% of the time, Pallas kernels for 1%

profile of v1, /device:TPU:8, one launch (start us, length us, event | category | flops | bytes accessed | tf_op | source)
XLA Modules:
  0.0 133.8 jit_solution(8597100812718852798)
XLA Ops:
  1.5 0.9 copy-done.3
  2.5 3.1 %collective-permute-start = (bf16[88,288]{1,0:T(8,128)(2,1)S(1)}, bf16[88,288]{1,0:T(8,128)(2,1)S(1)}, u32[]{:S(2)}, u32[]{:S(2)}) collective-permute-start(bf16[88,288]{1,0:T(8,128)(2,1)S(1)} %get-tuple-element.27), channel_id=1, source_target_pairs={{0,2},{2,0},{1,3},{3,1},{4,6},{6,4},{5,7},{7,5},{8,10},{10,8},{9,1... | collective-permute-start | bytes 152072 | tf_op jit(solution)/shard_map/ppermute | solution.py:46
  5.6 2.8 %collective-permute-done.recv = bf16[88,288]{1,0:T(8,128)(2,1)S(1)} collective-permute-done((bf16[88,288]{1,0:T(8,128)(2,1)S(1)}, bf16[88,288]{1,0:T(8,128)(2,1)S(1)}, u32[]{:S(2)}, u32[]{:S(2)}) %collective-permute-start) | collective-permute-done | bytes 50720 | tf_op jit(solution)/shard_map/ppermute | solution.py:46
  8.5 2.0 %collective-permute-start.1 = (bf16[96,640]{1,0:T(8,128)(2,1)S(1)}, bf16[96,640]{1,0:T(8,128)(2,1)S(1)}, u32[]{:S(2)}, u32[]{:S(2)}) collective-permute-start(bf16[96,640]{1,0:T(8,128)(2,1)S(1)} %shard_map.60), channel_id=1, source_target_pairs={{0,8},{8,0},{16,24},{24,16},{32,40},{40,32},{48,56},{56,48},{1,9},... | collective-permute-start | bytes 368648 | tf_op jit(solution)/shard_map/ppermute | solution.py:46
  10.5 1.3 collective-permute-done.9.recv
  11.8 2.8 %collective-permute-start.12 = (bf16[96,640]{1,0:T(8,128)(2,1)S(1)}, bf16[96,640]{1,0:T(8,128)(2,1)S(1)}, u32[]{:S(2)}, u32[]{:S(2)}) collective-permute-start(bf16[96,640]{1,0:T(8,128)(2,1)S(1)} %shard_map.61), channel_id=1, source_target_pairs={{0,6},{2,4},{4,2},{6,0},{1,7},{3,5},{5,3},{7,1},{8,14},{10,12},{12... | collective-permute-start | bytes 368648 | tf_op jit(solution)/shard_map/ppermute | solution.py:46
  14.9 1.7 %collective-permute-start.10 = (bf16[96,640]{1,0:T(8,128)(2,1)S(1)}, bf16[96,640]{1,0:T(8,128)(2,1)S(1)}, u32[]{:S(2)}, u32[]{:S(2)}) collective-permute-start(bf16[96,640]{1,0:T(8,128)(2,1)S(1)} %shard_map.61), channel_id=1, source_target_pairs={{0,2},{2,0},{4,6},{6,4},{1,3},{3,1},{5,7},{7,5},{8,10},{10,8},{12,... | collective-permute-start | bytes 368648 | tf_op jit(solution)/shard_map/ppermute | solution.py:46
  16.7 5.5 %collective-permute-start.4 = (bf16[2,96,640]{2,1,0:T(8,128)(2,1)S(1)}, bf16[2,96,640]{2,1,0:T(8,128)(2,1)S(1)}, u32[]{:S(2)}, u32[]{:S(2)}) collective-permute-start(bf16[2,96,640]{2,1,0:T(8,128)(2,1)S(1)} %pad_maximum_fusion.1.refs_0_), channel_id=1, source_target_pairs={{0,48},{8,56},{16,32},{24,40},{32,16},{40,24},{48,0},{56,8},{1,49}... | collective-permute-start | bytes 737288 | tf_op jit(solution)/shard_map/ppermute | solution.py:46
  22.2 2.6 %collective-permute-start.3 = (bf16[2,96,640]{2,1,0:T(8,128)(2,1)S(1)}, bf16[2,96,640]{2,1,0:T(8,128)(2,1)S(1)}, u32[]{:S(2)}, u32[]{:S(2)}) collective-permute-start(bf16[2,96,640]{2,1,0:T(8,128)(2,1)S(1)} %pad_maximum_fusion.1.refs_0_), channel_id=1, source_target_pairs={{0,32},{8,40},{16,48},{24,56},{32,0},{40,8},{48,16},{56,24},{1,33}... | collective-permute-start | bytes 737288 | tf_op jit(solution)/shard_map/ppermute | solution.py:46
  24.8 1.5 %collective-permute-start.2 = (bf16[2,96,640]{2,1,0:T(8,128)(2,1)S(1)}, bf16[2,96,640]{2,1,0:T(8,128)(2,1)S(1)}, u32[]{:S(2)}, u32[]{:S(2)}) collective-permute-start(bf16[2,96,640]{2,1,0:T(8,128)(2,1)S(1)} %pad_maximum_fusion.1.refs_0_), channel_id=1, source_target_pairs={{0,16},{8,24},{16,0},{24,8},{32,48},{40,56},{48,32},{56,40},{1,17}... | collective-permute-start | bytes 737288 | tf_op jit(solution)/shard_map/ppermute | solution.py:46
  26.4 1.7 %collective-permute-start.15 = (bf16[4,96,640]{2,1,0:T(8,128)(2,1)S(1)}, bf16[4,96,640]{2,1,0:T(8,128)(2,1)S(1)}, u32[]{:S(2)}, u32[]{:S(2)}) collective-permute-start(bf16[4,96,640]{2,1,0:T(8,128)(2,1)S(1)} %pad_maximum_fusion.refs_8_), channel_id=1, source_target_pairs={{0,192},{64,128},{128,64},{192,0},{1,193},{65,129},{129,65},{193,1... | collective-permute-start | bytes 1474568 | tf_op jit(solution)/shard_map/ppermute | solution.py:46
  28.1 14.6 %collective-permute-done.4.refs_3_ = bf16[2,96,640]{2,1,0:T(8,128)(2,1)S(1)} collective-permute-done((bf16[2,96,640]{2,1,0:T(8,128)(2,1)S(1)}, bf16[2,96,640]{2,1,0:T(8,128)(2,1)S(1)}, u32[]{:S(2)}, u32[]{:S(2)}) %collective-permute-start.4) | collective-permute-done | bytes 245792 | tf_op jit(solution)/shard_map/ppermute | solution.py:46
  42.7 2.4 %collective-permute-start.14 = (bf16[4,96,640]{2,1,0:T(8,128)(2,1)S(1)}, bf16[4,96,640]{2,1,0:T(8,128)(2,1)S(1)}, u32[]{:S(2)}, u32[]{:S(2)}) collective-permute-start(bf16[4,96,640]{2,1,0:T(8,128)(2,1)S(1)} %pad_maximum_fusion.refs_8_), channel_id=1, source_target_pairs={{0,128},{64,192},{128,0},{192,64},{1,129},{65,193},{129,1},{193,65... | collective-permute-start | bytes 1474568 | tf_op jit(solution)/shard_map/ppermute | solution.py:46
  45.1 1.3 %collective-permute-start.13 = (bf16[4,96,640]{2,1,0:T(8,128)(2,1)S(1)}, bf16[4,96,640]{2,1,0:T(8,128)(2,1)S(1)}, u32[]{:S(2)}, u32[]{:S(2)}) collective-permute-start(bf16[4,96,640]{2,1,0:T(8,128)(2,1)S(1)} %pad_maximum_fusion.refs_8_), channel_id=1, source_target_pairs={{0,64},{64,0},{128,192},{192,128},{1,65},{65,1},{129,193},{193,129... | collective-permute-start | bytes 1474568 | tf_op jit(solution)/shard_map/ppermute | solution.py:46
  46.4 1.4 %collective-permute-done.2.refs_1_ = bf16[2,96,640]{2,1,0:T(8,128)(2,1)S(1)} collective-permute-done((bf16[2,96,640]{2,1,0:T(8,128)(2,1)S(1)}, bf16[2,96,640]{2,1,0:T(8,128)(2,1)S(1)}, u32[]{:S(2)}, u32[]{:S(2)}) %collective-permute-start.2) | collective-permute-done | bytes 245792 | tf_op jit(solution)/shard_map/ppermute | solution.py:46
  49.8 8.5 %collective-permute-done.14.refs_10_ = bf16[4,96,640]{2,1,0:T(8,128)(2,1)S(1)} collective-permute-done((bf16[4,96,640]{2,1,0:T(8,128)(2,1)S(1)}, bf16[4,96,640]{2,1,0:T(8,128)(2,1)S(1)}, u32[]{:S(2)}, u32[]{:S(2)}) %collective-permute-start.14) | collective-permute-done | bytes 491552 | tf_op jit(solution)/shard_map/ppermute | solution.py:46
  58.3 10.2 %collective-permute-done.13.refs_9_ = bf16[4,96,640]{2,1,0:T(8,128)(2,1)S(1)} collective-permute-done((bf16[4,96,640]{2,1,0:T(8,128)(2,1)S(1)}, bf16[4,96,640]{2,1,0:T(8,128)(2,1)S(1)}, u32[]{:S(2)}, u32[]{:S(2)}) %collective-permute-start.13) | collective-permute-done | bytes 491552 | tf_op jit(solution)/shard_map/ppermute | solution.py:46
  69.3 10.3 %shard_map.62 = (f32[8,96,640]{2,1,0:T(8,128)}, f32[8,96,640]{2,1,0:T(8,128)}, f32[4,96,640]{2,1,0:T(8,128)}, f32[4,96,640]{2,1,0:T(8,128)}, f32[4,96,640]{2,1,0:T(8,128)}, /*index=5*/f32[4,96,640]{2,1,0:T(8,128)}) custom-call(bf16[2,96,640]{2,1,0:T(8,128)(2,1)} %copy-done.6, bf16[2,96,640]{2,1,0:T(8,128)(2,1)} %copy-done.13, ...), custom_call_target="tpu_custom_call" | custom-call | flops 3425697792 | bytes 11796488 | tf_op jit(solution)/shard_map/pallas_call | solution.py:30
  79.8 1.4 %convert_element_type.72 = f16[4,96,640]{2,1,0:T(8,128)(2,1)S(1)} convert(f32[4,96,640]{2,1,0:T(8,128)} %get-tuple-element.43) | non-fusion elementwise | flops 245760 | bytes 1474560 | tf_op jit(solution)/shard_map/convert_element_type | solution.py:221
  81.7 1.3 convert_element_type.70
  83.0 2.4 %collective-permute-start.23 = (f16[4,96,640]{2,1,0:T(8,128)(2,1)S(1)}, f16[4,96,640]{2,1,0:T(8,128)(2,1)S(1)}, u32[]{:S(2)}, u32[]{:S(2)}) collective-permute-start(f16[4,96,640]{2,1,0:T(8,128)(2,1)S(1)} %convert_element_type.70), channel_id=1, source_target_pairs={{0,128},{64,192},{128,0},{192,64},{1,129},{65,193},{129,1},{193,65... | collective-permute-start | bytes 1474568 | tf_op jit(solution)/shard_map/ppermute | solution.py:46
  85.4 1.4 %collective-permute-start.22 = (f16[4,96,640]{2,1,0:T(8,128)(2,1)S(1)}, f16[4,96,640]{2,1,0:T(8,128)(2,1)S(1)}, u32[]{:S(2)}, u32[]{:S(2)}) collective-permute-start(f16[4,96,640]{2,1,0:T(8,128)(2,1)S(1)} %convert_element_type.68), channel_id=1, source_target_pairs={{0,64},{64,0},{128,192},{192,128},{1,65},{65,1},{129,193},{193,129... | collective-permute-start | bytes 1474568 | tf_op jit(solution)/shard_map/ppermute | solution.py:46
  87.3 4.7 %collective-permute-start.19 = (f16[2,96,640]{2,1,0:T(8,128)(2,1)S(1)}, f16[2,96,640]{2,1,0:T(8,128)(2,1)S(1)}, u32[]{:S(2)}, u32[]{:S(2)}) collective-permute-start(f16[2,96,640]{2,1,0:T(8,128)(2,1)S(1)} %convert_element_type.64), channel_id=1, source_target_pairs={{0,48},{8,56},{16,32},{24,40},{32,16},{40,24},{48,0},{56,8},{1,49}... | collective-permute-start | bytes 737288 | tf_op jit(solution)/shard_map/ppermute | solution.py:46
  92.0 1.6 %collective-permute-start.18 = (f16[2,96,640]{2,1,0:T(8,128)(2,1)S(1)}, f16[2,96,640]{2,1,0:T(8,128)(2,1)S(1)}, u32[]{:S(2)}, u32[]{:S(2)}) collective-permute-start(f16[2,96,640]{2,1,0:T(8,128)(2,1)S(1)} %convert_element_type.62), channel_id=1, source_target_pairs={{0,32},{8,40},{16,48},{24,56},{32,0},{40,8},{48,16},{56,24},{1,33}... | collective-permute-start | bytes 737288 | tf_op jit(solution)/shard_map/ppermute | solution.py:46
  93.6 11.8 %collective-permute-done.24 = f16[4,96,640]{2,1,0:T(8,128)(2,1)S(1)} collective-permute-done((f16[4,96,640]{2,1,0:T(8,128)(2,1)S(1)}, f16[4,96,640]{2,1,0:T(8,128)(2,1)S(1)}, u32[]{:S(2)}, u32[]{:S(2)}) %collective-permute-start.24) | collective-permute-done | bytes 491552 | tf_op jit(solution)/shard_map/ppermute | solution.py:46
  105.4 2.6 %collective-permute-start.17 = (f16[2,96,640]{2,1,0:T(8,128)(2,1)S(1)}, f16[2,96,640]{2,1,0:T(8,128)(2,1)S(1)}, u32[]{:S(2)}, u32[]{:S(2)}) collective-permute-start(f16[2,96,640]{2,1,0:T(8,128)(2,1)S(1)} %convert_element_type.60), channel_id=1, source_target_pairs={{0,16},{8,24},{16,0},{24,8},{32,48},{40,56},{48,32},{56,40},{1,17}... | collective-permute-start | bytes 737288 | tf_op jit(solution)/shard_map/ppermute | solution.py:46
  109.3 2.8 %collective-permute-start.27 = (f16[96,640]{1,0:T(8,128)(2,1)S(1)}, f16[96,640]{1,0:T(8,128)(2,1)S(1)}, u32[]{:S(2)}, u32[]{:S(2)}) collective-permute-start(f16[96,640]{1,0:T(8,128)(2,1)S(1)} %convert_element_type.78), channel_id=1, source_target_pairs={{0,6},{2,4},{4,2},{6,0},{1,7},{3,5},{5,3},{7,1},{8,14},{10,12},{12... | collective-permute-start | bytes 368648 | tf_op jit(solution)/shard_map/ppermute | solution.py:46
  112.1 1.9 %collective-permute-start.25 = (f16[96,640]{1,0:T(8,128)(2,1)S(1)}, f16[96,640]{1,0:T(8,128)(2,1)S(1)}, u32[]{:S(2)}, u32[]{:S(2)}) collective-permute-start(f16[96,640]{1,0:T(8,128)(2,1)S(1)} %convert_element_type.74), channel_id=1, source_target_pairs={{0,2},{2,0},{4,6},{6,4},{1,3},{3,1},{5,7},{7,5},{8,10},{10,8},{12,... | collective-permute-start | bytes 368648 | tf_op jit(solution)/shard_map/ppermute | solution.py:46
  114.1 6.2 %collective-permute-done.17 = f16[2,96,640]{2,1,0:T(8,128)(2,1)S(1)} collective-permute-done((f16[2,96,640]{2,1,0:T(8,128)(2,1)S(1)}, f16[2,96,640]{2,1,0:T(8,128)(2,1)S(1)}, u32[]{:S(2)}, u32[]{:S(2)}) %collective-permute-start.17) | collective-permute-done | bytes 245792 | tf_op jit(solution)/shard_map/ppermute | solution.py:46
  121.7 4.4 %collective-permute-done.20 = f16[96,640]{1,0:T(8,128)(2,1)S(1)} collective-permute-done((f16[96,640]{1,0:T(8,128)(2,1)S(1)}, f16[96,640]{1,0:T(8,128)(2,1)S(1)}, u32[]{:S(2)}, u32[]{:S(2)}) %collective-permute-start.20) | collective-permute-done | bytes 122912 | tf_op jit(solution)/shard_map/ppermute | solution.py:46
  126.3 1.5 %collective-permute-start.21 = (f32[88,288]{1,0:T(8,128)S(1)}, f32[88,288]{1,0:T(8,128)S(1)}, u32[]{:S(2)}, u32[]{:S(2)}) collective-permute-start(f32[88,288]{1,0:T(8,128)S(1)} %get-tuple-element.39), channel_id=1, source_target_pairs={{0,2},{2,0},{1,3},{3,1},{4,6},{6,4},{5,7},{7,5},{8,10},{10,8},{9,1... | collective-permute-start | bytes 304136 | tf_op jit(solution)/shard_map/ppermute | solution.py:46
  127.8 5.1 %collective-permute-done.21.image_recv = f32[88,288]{1,0:T(8,128)S(1)} collective-permute-done((f32[88,288]{1,0:T(8,128)S(1)}, f32[88,288]{1,0:T(8,128)S(1)}, u32[]{:S(2)}, u32[]{:S(2)}) %collective-permute-start.21) | collective-permute-done | bytes 101408 | tf_op jit(solution)/shard_map/ppermute | solution.py:46
  (88 shorter events, 7.8 us)
Async XLA Ops:
  2.5 5.9 %collective-permute-start = (bf16[88,288]{1,0:T(8,128)(2,1)S(1)}, bf16[88,288]{1,0:T(8,128)(2,1)S(1)}, u32[]{:S(2)}, u32[]{:S(2)}) collective-permute-start(bf16[88,288]{1,0:T(8,128)(2,1)S(1)} %get-tuple-element.27), channel_id=1, source_target_pairs={{0,2},{2,0},{1,3},{3,1},{4,6},{6,4},{5,7},{7,5},{8,10},{10,8},{9,1... | collective-permute-start | bytes 152072 | tf_op jit(solution)/shard_map/ppermute | solution.py:46
  8.5 8.1 %collective-permute-start.1 = (bf16[96,640]{1,0:T(8,128)(2,1)S(1)}, bf16[96,640]{1,0:T(8,128)(2,1)S(1)}, u32[]{:S(2)}, u32[]{:S(2)}) collective-permute-start(bf16[96,640]{1,0:T(8,128)(2,1)S(1)} %shard_map.60), channel_id=1, source_target_pairs={{0,8},{8,0},{16,24},{24,16},{32,40},{40,32},{48,56},{56,48},{1,9},... | collective-permute-start | bytes 368648 | tf_op jit(solution)/shard_map/ppermute | solution.py:46
  10.5 1.3 collective-permute-start.9
  11.8 10.3 %collective-permute-start.12 = (bf16[96,640]{1,0:T(8,128)(2,1)S(1)}, bf16[96,640]{1,0:T(8,128)(2,1)S(1)}, u32[]{:S(2)}, u32[]{:S(2)}) collective-permute-start(bf16[96,640]{1,0:T(8,128)(2,1)S(1)} %shard_map.61), channel_id=1, source_target_pairs={{0,6},{2,4},{4,2},{6,0},{1,7},{3,5},{5,3},{7,1},{8,14},{10,12},{12... | collective-permute-start | bytes 368648 | tf_op jit(solution)/shard_map/ppermute | solution.py:46
  14.7 10.1 %collective-permute-start.11 = (bf16[96,640]{1,0:T(8,128)(2,1)S(1)}, bf16[96,640]{1,0:T(8,128)(2,1)S(1)}, u32[]{:S(2)}, u32[]{:S(2)}) collective-permute-start(bf16[96,640]{1,0:T(8,128)(2,1)S(1)} %shard_map.61), channel_id=1, source_target_pairs={{0,4},{2,6},{4,0},{6,2},{1,5},{3,7},{5,1},{7,3},{8,12},{10,14},{12... | collective-permute-start | bytes 368648 | tf_op jit(solution)/shard_map/ppermute | solution.py:46
  14.9 11.4 %collective-permute-start.10 = (bf16[96,640]{1,0:T(8,128)(2,1)S(1)}, bf16[96,640]{1,0:T(8,128)(2,1)S(1)}, u32[]{:S(2)}, u32[]{:S(2)}) collective-permute-start(bf16[96,640]{1,0:T(8,128)(2,1)S(1)} %shard_map.61), channel_id=1, source_target_pairs={{0,2},{2,0},{4,6},{6,4},{1,3},{3,1},{5,7},{7,5},{8,10},{10,8},{12,... | collective-permute-start | bytes 368648 | tf_op jit(solution)/shard_map/ppermute | solution.py:46
  16.7 51.8 %copy-start.6 = (bf16[2,96,640]{2,1,0:T(8,128)(2,1)}, bf16[2,96,640]{2,1,0:T(8,128)(2,1)S(1)}, u32[]{:S(2)}) copy-start(bf16[2,96,640]{2,1,0:T(8,128)(2,1)S(1)} %pad_maximum_fusion.1.refs_0_) | copy-start | bytes 737284
  16.7 26.0 %collective-permute-start.4 = (bf16[2,96,640]{2,1,0:T(8,128)(2,1)S(1)}, bf16[2,96,640]{2,1,0:T(8,128)(2,1)S(1)}, u32[]{:S(2)}, u32[]{:S(2)}) collective-permute-start(bf16[2,96,640]{2,1,0:T(8,128)(2,1)S(1)} %pad_maximum_fusion.1.refs_0_), channel_id=1, source_target_pairs={{0,48},{8,56},{16,32},{24,40},{32,16},{40,24},{48,0},{56,8},{1,49}... | collective-permute-start | bytes 737288 | tf_op jit(solution)/shard_map/ppermute | solution.py:46
  22.2 20.5 %collective-permute-start.5 = (bf16[2,96,640]{2,1,0:T(8,128)(2,1)S(1)}, bf16[2,96,640]{2,1,0:T(8,128)(2,1)S(1)}, u32[]{:S(2)}, u32[]{:S(2)}) collective-permute-start(bf16[2,96,640]{2,1,0:T(8,128)(2,1)S(1)} %pad_maximum_fusion.1.refs_0_), channel_id=1, source_target_pairs={{0,1},{1,0},{2,3},{3,2},{4,5},{5,4},{6,7},{7,6},{8,9},{9,8},{10,11... | collective-permute-start | bytes 737288 | tf_op jit(solution)/shard_map/ppermute | solution.py:46
  22.2 22.9 %collective-permute-start.3 = (bf16[2,96,640]{2,1,0:T(8,128)(2,1)S(1)}, bf16[2,96,640]{2,1,0:T(8,128)(2,1)S(1)}, u32[]{:S(2)}, u32[]{:S(2)}) collective-permute-start(bf16[2,96,640]{2,1,0:T(8,128)(2,1)S(1)} %pad_maximum_fusion.1.refs_0_), channel_id=1, source_target_pairs={{0,32},{8,40},{16,48},{24,56},{32,0},{40,8},{48,16},{56,24},{1,33}... | collective-permute-start | bytes 737288 | tf_op jit(solution)/shard_map/ppermute | solution.py:46
  24.8 23.0 %collective-permute-start.2 = (bf16[2,96,640]{2,1,0:T(8,128)(2,1)S(1)}, bf16[2,96,640]{2,1,0:T(8,128)(2,1)S(1)}, u32[]{:S(2)}, u32[]{:S(2)}) collective-permute-start(bf16[2,96,640]{2,1,0:T(8,128)(2,1)S(1)} %pad_maximum_fusion.1.refs_0_), channel_id=1, source_target_pairs={{0,16},{8,24},{16,0},{24,8},{32,48},{40,56},{48,32},{56,40},{1,17}... | collective-permute-start | bytes 737288 | tf_op jit(solution)/shard_map/ppermute | solution.py:46
  26.4 42.1 %copy-start.5 = (bf16[4,96,640]{2,1,0:T(8,128)(2,1)}, bf16[4,96,640]{2,1,0:T(8,128)(2,1)S(1)}, u32[]{:S(2)}) copy-start(bf16[4,96,640]{2,1,0:T(8,128)(2,1)S(1)} %pad_maximum_fusion.refs_8_) | copy-start | bytes 1474564
  26.4 23.4 %collective-permute-start.15 = (bf16[4,96,640]{2,1,0:T(8,128)(2,1)S(1)}, bf16[4,96,640]{2,1,0:T(8,128)(2,1)S(1)}, u32[]{:S(2)}, u32[]{:S(2)}) collective-permute-start(bf16[4,96,640]{2,1,0:T(8,128)(2,1)S(1)} %pad_maximum_fusion.refs_8_), channel_id=1, source_target_pairs={{0,192},{64,128},{128,64},{192,0},{1,193},{65,129},{129,65},{193,1... | collective-permute-start | bytes 1474568 | tf_op jit(solution)/shard_map/ppermute | solution.py:46
  42.7 25.8 %copy-start.10 = (bf16[2,96,640]{2,1,0:T(8,128)(2,1)}, bf16[2,96,640]{2,1,0:T(8,128)(2,1)S(1)}, u32[]{:S(2)}) copy-start(bf16[2,96,640]{2,1,0:T(8,128)(2,1)S(1)} %collective-permute-done.4.refs_3_) | copy-start | bytes 737284
  42.7 5.1 %collective-permute-start.8 = (bf16[2,96,640]{2,1,0:T(8,128)(2,1)S(1)}, bf16[2,96,640]{2,1,0:T(8,128)(2,1)S(1)}, u32[]{:S(2)}, u32[]{:S(2)}) collective-permute-start(bf16[2,96,640]{2,1,0:T(8,128)(2,1)S(1)} %collective-permute-done.4.refs_3_), channel_id=1, source_target_pairs={{0,1},{1,0},{2,3},{3,2},{4,5},{5,4},{6,7},{7,6},{8,9},{9,8},{10,11... | collective-permute-start | bytes 737288 | tf_op jit(solution)/shard_map/ppermute | solution.py:46
  42.7 15.6 %collective-permute-start.14 = (bf16[4,96,640]{2,1,0:T(8,128)(2,1)S(1)}, bf16[4,96,640]{2,1,0:T(8,128)(2,1)S(1)}, u32[]{:S(2)}, u32[]{:S(2)}) collective-permute-start(bf16[4,96,640]{2,1,0:T(8,128)(2,1)S(1)} %pad_maximum_fusion.refs_8_), channel_id=1, source_target_pairs={{0,128},{64,192},{128,0},{192,64},{1,129},{65,193},{129,1},{193,65... | collective-permute-start | bytes 1474568 | tf_op jit(solution)/shard_map/ppermute | solution.py:46
  45.1 23.4 %collective-permute-start.13 = (bf16[4,96,640]{2,1,0:T(8,128)(2,1)S(1)}, bf16[4,96,640]{2,1,0:T(8,128)(2,1)S(1)}, u32[]{:S(2)}, u32[]{:S(2)}) collective-permute-start(bf16[4,96,640]{2,1,0:T(8,128)(2,1)S(1)} %pad_maximum_fusion.refs_8_), channel_id=1, source_target_pairs={{0,64},{64,0},{128,192},{192,128},{1,65},{65,1},{129,193},{193,129... | collective-permute-start | bytes 1474568 | tf_op jit(solution)/shard_map/ppermute | solution.py:46
  47.8 1.8 %collective-permute-start.7 = (bf16[2,96,640]{2,1,0:T(8,128)(2,1)S(1)}, bf16[2,96,640]{2,1,0:T(8,128)(2,1)}, u32[]{:S(2)}, u32[]{:S(2)}) collective-permute-start(bf16[2,96,640]{2,1,0:T(8,128)(2,1)S(1)} %collective-permute-done.3.refs_2_), channel_id=1, source_target_pairs={{0,1},{1,0},{2,3},{3,2},{4,5},{5,4},{6,7},{7,6},{8,9},{9,8},{10,11... | collective-permute-start | bytes 737288 | tf_op jit(solution)/shard_map/ppermute | solution.py:46
  47.8 2.0 %collective-permute-start.6 = (bf16[2,96,640]{2,1,0:T(8,128)(2,1)S(1)}, bf16[2,96,640]{2,1,0:T(8,128)(2,1)}, u32[]{:S(2)}, u32[]{:S(2)}) collective-permute-start(bf16[2,96,640]{2,1,0:T(8,128)(2,1)S(1)} %collective-permute-done.2.refs_1_), channel_id=1, source_target_pairs={{0,1},{1,0},{2,3},{3,2},{4,5},{5,4},{6,7},{7,6},{8,9},{9,8},{10,11... | collective-permute-start | bytes 737288 | tf_op jit(solution)/shard_map/ppermute | solution.py:46
  79.6 7.2 %collective-permute-start.16 = (f32[8,96,640]{2,1,0:T(8,128)}, f32[8,96,640]{2,1,0:T(8,128)S(1)}, u32[]{:S(2)}, u32[]{:S(2)}) collective-permute-start(f32[8,96,640]{2,1,0:T(8,128)} %get-tuple-element.31), channel_id=1, source_target_pairs={{0,1},{1,0},{2,3},{3,2},{4,5},{5,4},{6,7},{7,6},{8,9},{9,8},{10,11... | collective-permute-start | bytes 5898248 | tf_op jit(solution)/shard_map/ppermute | solution.py:46
  81.2 24.2 %collective-permute-start.24 = (f16[4,96,640]{2,1,0:T(8,128)(2,1)S(1)}, f16[4,96,640]{2,1,0:T(8,128)(2,1)S(1)}, u32[]{:S(2)}, u32[]{:S(2)}) collective-permute-start(f16[4,96,640]{2,1,0:T(8,128)(2,1)S(1)} %convert_element_type.72), channel_id=1, source_target_pairs={{0,192},{64,128},{128,64},{192,0},{1,193},{65,129},{129,65},{193,1... | collective-permute-start | bytes 1474568 | tf_op jit(solution)/shard_map/ppermute | solution.py:46
  83.0 25.1 %collective-permute-start.23 = (f16[4,96,640]{2,1,0:T(8,128)(2,1)S(1)}, f16[4,96,640]{2,1,0:T(8,128)(2,1)S(1)}, u32[]{:S(2)}, u32[]{:S(2)}) collective-permute-start(f16[4,96,640]{2,1,0:T(8,128)(2,1)S(1)} %convert_element_type.70), channel_id=1, source_target_pairs={{0,128},{64,192},{128,0},{192,64},{1,129},{65,193},{129,1},{193,65... | collective-permute-start | bytes 1474568 | tf_op jit(solution)/shard_map/ppermute | solution.py:46
  85.4 23.2 %collective-permute-start.22 = (f16[4,96,640]{2,1,0:T(8,128)(2,1)S(1)}, f16[4,96,640]{2,1,0:T(8,128)(2,1)S(1)}, u32[]{:S(2)}, u32[]{:S(2)}) collective-permute-start(f16[4,96,640]{2,1,0:T(8,128)(2,1)S(1)} %convert_element_type.68), channel_id=1, source_target_pairs={{0,64},{64,0},{128,192},{192,128},{1,65},{65,1},{129,193},{193,129... | collective-permute-start | bytes 1474568 | tf_op jit(solution)/shard_map/ppermute | solution.py:46
  87.3 24.8 %collective-permute-start.19 = (f16[2,96,640]{2,1,0:T(8,128)(2,1)S(1)}, f16[2,96,640]{2,1,0:T(8,128)(2,1)S(1)}, u32[]{:S(2)}, u32[]{:S(2)}) collective-permute-start(f16[2,96,640]{2,1,0:T(8,128)(2,1)S(1)} %convert_element_type.64), channel_id=1, source_target_pairs={{0,48},{8,56},{16,32},{24,40},{32,16},{40,24},{48,0},{56,8},{1,49}... | collective-permute-start | bytes 737288 | tf_op jit(solution)/shard_map/ppermute | solution.py:46
  92.0 22.1 %collective-permute-start.18 = (f16[2,96,640]{2,1,0:T(8,128)(2,1)S(1)}, f16[2,96,640]{2,1,0:T(8,128)(2,1)S(1)}, u32[]{:S(2)}, u32[]{:S(2)}) collective-permute-start(f16[2,96,640]{2,1,0:T(8,128)(2,1)S(1)} %convert_element_type.62), channel_id=1, source_target_pairs={{0,32},{8,40},{16,48},{24,56},{32,0},{40,8},{48,16},{56,24},{1,33}... | collective-permute-start | bytes 737288 | tf_op jit(solution)/shard_map/ppermute | solution.py:46
  105.4 14.9 %collective-permute-start.17 = (f16[2,96,640]{2,1,0:T(8,128)(2,1)S(1)}, f16[2,96,640]{2,1,0:T(8,128)(2,1)S(1)}, u32[]{:S(2)}, u32[]{:S(2)}) collective-permute-start(f16[2,96,640]{2,1,0:T(8,128)(2,1)S(1)} %convert_element_type.60), channel_id=1, source_target_pairs={{0,16},{8,24},{16,0},{24,8},{32,48},{40,56},{48,32},{56,40},{1,17}... | collective-permute-start | bytes 737288 | tf_op jit(solution)/shard_map/ppermute | solution.py:46
  109.3 12.0 %collective-permute-start.27 = (f16[96,640]{1,0:T(8,128)(2,1)S(1)}, f16[96,640]{1,0:T(8,128)(2,1)S(1)}, u32[]{:S(2)}, u32[]{:S(2)}) collective-permute-start(f16[96,640]{1,0:T(8,128)(2,1)S(1)} %convert_element_type.78), channel_id=1, source_target_pairs={{0,6},{2,4},{4,2},{6,0},{1,7},{3,5},{5,3},{7,1},{8,14},{10,12},{12... | collective-permute-start | bytes 368648 | tf_op jit(solution)/shard_map/ppermute | solution.py:46
  112.1 9.1 %collective-permute-start.26 = (f16[96,640]{1,0:T(8,128)(2,1)S(1)}, f16[96,640]{1,0:T(8,128)(2,1)S(1)}, u32[]{:S(2)}, u32[]{:S(2)}) collective-permute-start(f16[96,640]{1,0:T(8,128)(2,1)S(1)} %convert_element_type.76), channel_id=1, source_target_pairs={{0,4},{2,6},{4,0},{6,2},{1,5},{3,7},{5,1},{7,3},{8,12},{10,14},{12... | collective-permute-start | bytes 368648 | tf_op jit(solution)/shard_map/ppermute | solution.py:46
  112.1 9.2 %collective-permute-start.25 = (f16[96,640]{1,0:T(8,128)(2,1)S(1)}, f16[96,640]{1,0:T(8,128)(2,1)S(1)}, u32[]{:S(2)}, u32[]{:S(2)}) collective-permute-start(f16[96,640]{1,0:T(8,128)(2,1)S(1)} %convert_element_type.74), channel_id=1, source_target_pairs={{0,2},{2,0},{4,6},{6,4},{1,3},{3,1},{5,7},{7,5},{8,10},{10,8},{12,... | collective-permute-start | bytes 368648 | tf_op jit(solution)/shard_map/ppermute | solution.py:46
  120.8 5.3 %collective-permute-start.20 = (f16[96,640]{1,0:T(8,128)(2,1)S(1)}, f16[96,640]{1,0:T(8,128)(2,1)S(1)}, u32[]{:S(2)}, u32[]{:S(2)}) collective-permute-start(f16[96,640]{1,0:T(8,128)(2,1)S(1)} %convert_element_type.66), channel_id=1, source_target_pairs={{0,8},{8,0},{16,24},{24,16},{32,40},{40,32},{48,56},{56,48},{1,9},... | collective-permute-start | bytes 368648 | tf_op jit(solution)/shard_map/ppermute | solution.py:46
  121.6 6.3 %collective-permute-start.28 = (f32[88,288]{1,0:T(8,128)S(1)}, f32[88,288]{1,0:T(8,128)S(1)}, u32[]{:S(2)}, u32[]{:S(2)}) collective-permute-start(f32[88,288]{1,0:T(8,128)S(1)} %get-tuple-element.49), channel_id=1, source_target_pairs={{0,1},{1,0},{2,3},{3,2},{4,5},{5,4},{6,7},{7,6},{8,9},{9,8},{10,11... | collective-permute-start | bytes 304136 | tf_op jit(solution)/shard_map/ppermute | solution.py:46
  126.3 6.6 %collective-permute-start.21 = (f32[88,288]{1,0:T(8,128)S(1)}, f32[88,288]{1,0:T(8,128)S(1)}, u32[]{:S(2)}, u32[]{:S(2)}) collective-permute-start(f32[88,288]{1,0:T(8,128)S(1)} %get-tuple-element.39), channel_id=1, source_target_pairs={{0,2},{2,0},{1,3},{3,1},{4,6},{6,4},{5,7},{7,5},{8,10},{10,8},{9,1... | collective-permute-start | bytes 304136 | tf_op jit(solution)/shard_map/ppermute | solution.py:46
  (12 other events, 151.8 us)

commit v2 on v1

v2 whole, which is shorter than its diff:
```python
import jax
import jax.numpy as jnp
from jax import lax
from jax.experimental import pallas as pl
from jax.experimental.pallas import tpu as pltpu
from jax.sharding import Mesh
from jax.sharding import PartitionSpec as P

AXES = ("y", "z", "l", "h", "c")
SIZES = {"y": 4, "z": 8, "l": 2, "h": 2, "c": 2}
ROWS = 88
SLOT = 96
CUT = 48
FAR = 240
QUART = 288
HALF = 576
WIDE = 640
X = ("l", "h")
F32 = jnp.float32
BF16 = jnp.bfloat16
F16 = jnp.float16
VMEM = pl.BlockSpec(memory_space=pltpu.VMEM)
SMEM = pl.BlockSpec(memory_space=pltpu.SMEM)


def shape(dims, dtype):
    return jax.ShapeDtypeStruct(dims, dtype)


def call(kernel, outs, *args, smem=0, scratch=(), flops=0, mib=32):
    specs = [VMEM] * (len(args) - smem) + [SMEM] * smem
    moved = sum(a.size * a.dtype.itemsize for a in (*args, *outs))
    return pl.pallas_call(
        kernel,
        out_shape=outs,
        in_specs=specs,
        out_specs=[VMEM] * len(outs),
        scratch_shapes=list(scratch),
        compiler_params=pltpu.CompilerParams(vmem_limit_bytes=mib * 2**20),
        cost_estimate=pl.CostEstimate(flops=flops, bytes_accessed=moved, transcendentals=0),
    )(*args)


def flip(x, axis, mask):
    count = 4 if axis == X else SIZES[axis]
    return lax.ppermute(x, axis, [(i, i ^ mask) for i in range(count)])


def behind(x, axis, distance):
    count = SIZES[axis]
    return lax.ppermute(x, axis, [(i, (i + distance) % count) for i in range(count)])


def together(*xs):
    return lax.optimization_barrier(xs)


def split_kernel(image, text, image_keep, image_send, text_keep, text_send):
    for source, axis, keep, send in (
        (image, "h", image_keep, image_send),
        (text, "c", text_keep, text_send),
    ):
        low = lax.axis_index(axis) == 0
        x = source[...].astype(F32)
        first, second = x[:ROWS], x[ROWS:]
        keep[...] = jnp.where(low, first, second).astype(BF16)
        send[...] = jnp.where(low, second, first).astype(BF16)


def joined(a, b):
    x = jnp.concatenate([a, b, jnp.zeros((ROWS, WIDE - HALF), F32)], axis=1)
    return jnp.concatenate([x, jnp.zeros((SLOT - ROWS, WIDE), F32)], axis=0).astype(BF16)


def piece_kernel(keep, recv, out):
    out[...] = joined(keep[...].astype(F32), recv[...].astype(F32))


def stack_kernel(*refs):
    for n, ref in enumerate(refs[:-1]):
        refs[-1][n] = ref[...]


def image_near_kernel(own, below, above, near, up, down):
    x, a, b = own[...], below[...], above[...]
    for out, parts in ((near, (x, a, b)), (up, (x, b, a[:CUT])), (down, (x, a, b[CUT:]))):
        for n, part in enumerate(parts):
            out[pl.ds(SLOT * n, part.shape[0]), :] = part


def scaled(x):
    most = jnp.max(jnp.max(jnp.abs(x), axis=0, keepdims=True), axis=1, keepdims=True)
    power = jnp.floor(jnp.log2(jnp.maximum(most, 1e-30)))
    lane = lax.broadcasted_iota(jnp.int32, x.shape, 1)
    return jnp.where(lane < HALF, x * jnp.exp2(13.0 - power), power)


def unscaled(p):
    return p * jnp.exp2(p[:1, HALF : HALF + 1] - 13.0)


def slope_kernel(*refs):
    halves, text = (refs[0:3], refs[3:6]), refs[6:10]
    scale_ref, bias_ref = refs[10:12]
    keep, send, slope, images = refs[12:16]
    texts = refs[16]
    scale, bias = scale_ref[0], bias_ref[0]
    zeros = jnp.zeros((SLOT, WIDE - HALF), BF16)
    for c, (near, below, above) in enumerate(halves):
        lanes = pl.ds(WIDE * c, WIDE)
        for first, source, count in (
            (0, near, 3 * SLOT),
            (3 * SLOT, below, 2 * SLOT),
            (5 * SLOT, above, 2 * SLOT),
        ):
            images[pl.ds(first, count), lanes] = source[:count, :]
        images[pl.ds(7 * SLOT, CUT), lanes] = below[2 * SLOT :, :]
        images[pl.ds(7 * SLOT + CUT, CUT), lanes] = above[2 * SLOT :, :]
    for s in range(8):
        rows = pl.ds(SLOT * s, SLOT)
        a, b = text[s // 4 * 2][s % 4], text[s // 4 * 2 + 1][s % 4]
        texts[rows, 0:WIDE] = jnp.concatenate([a[:, :QUART], b[:, :QUART], zeros], axis=1)
        texts[rows, WIDE:] = jnp.concatenate([a[:, QUART:HALF], b[:, QUART:HALF], zeros], axis=1)
    own = lax.axis_index("h") == lax.axis_index("c")
    for j in range(3):
        cols = pl.ds(256 * j, 256)
        dots = lax.dot_general(
            images[...], texts[cols, :], (((1,), (1,)), ((), ())), preferred_element_type=F32
        )
        logit = scale * dots + bias
        value = jax.nn.sigmoid(logit)
        if j == 0:
            top = logit[:SLOT]
            row = lax.broadcasted_iota(jnp.int32, top.shape, 0)
            col = lax.broadcasted_iota(jnp.int32, top.shape, 1)
            paired = (col == row) & (row < ROWS) & own
            top = jnp.where(paired, -jax.nn.sigmoid(-top), value[:SLOT])
            value = jnp.concatenate([top, value[SLOT:]], axis=0)
        slope[:, cols] = value.astype(BF16)
    add = jnp.dot(slope[...], texts[...], preferred_element_type=F32)
    for s in range(8):
        keep[s] = add[SLOT * s : SLOT * (s + 1), :WIDE]
        send[s] = add[SLOT * s : SLOT * (s + 1), WIDE:]


def text_kernel(slope, images, own, *outs):
    total = lax.dot_general(
        slope[...], images[...], (((0,), (0,)), ((), ())), preferred_element_type=F32
    )
    pad = jnp.zeros((SLOT, WIDE - HALF), F32)
    for s in range(8):
        x = total[SLOT * s : SLOT * (s + 1), :]
        for d in range(2):
            low, high = x[:, QUART * d : QUART * (d + 1)], x[:, WIDE + QUART * d : WIDE + QUART * (d + 1)]
            part = jnp.concatenate([low, high, pad], axis=1)
            m = s // 4 * 2 + d
            if m == 0:
                own[s % 4] = part
            else:
                outs[m - 1][s % 4] = scaled(part)


def image_first_kernel(keep, recv, own, below, above):
    for s in range(8):
        x = keep[s] + recv[s]
        if s < 3:
            own[s] = x
        elif s < 7:
            out = below if s < 5 else above
            out[pl.ds(SLOT * ((s - 3) % 2), SLOT), :] = scaled(x)
        else:
            x = scaled(x)
            below[pl.ds(2 * SLOT, CUT), :] = x[:CUT]
            above[pl.ds(2 * SLOT, CUT), :] = x[CUT:]


def image_sum_kernel(own, from_above, from_below, kept, below, above):
    a = [unscaled(from_above[n * SLOT : min((n + 1) * SLOT, FAR), :]) for n in range(3)]
    b = [unscaled(from_below[n * SLOT : min((n + 1) * SLOT, FAR), :]) for n in range(3)]
    kept[...] = own[0] + a[0] + b[0]
    x = own[1] + b[1]
    below[...] = scaled(jnp.concatenate([x[:CUT] + a[2], x[CUT:]], axis=0))
    x = own[2] + a[1]
    above[...] = scaled(jnp.concatenate([x[:CUT], x[CUT:] + b[2]], axis=0))


def text_sum_kernel(own, r1, r2, r3, kept, *outs):
    for n in range(4):
        x = own[n] + unscaled(r1[n]) + unscaled(r2[n]) + unscaled(r3[n])
        if n == 0:
            kept[...] = x
        else:
            outs[n - 1][...] = scaled(x)


def last_kernel(*refs):
    own, *parts, scale, keep, send = refs
    x = own[...]
    for part in parts:
        x = x + unscaled(part[...])
    x = scale[0] * x[:ROWS]
    keep[...] = x[:, :QUART]
    send[...] = x[:, QUART:HALF]


def place_kernel(image_keep, image_recv, text_keep, text_recv, image_out, text_out):
    for axis, keep, recv, out in (
        ("h", image_keep, image_recv, image_out),
        ("c", text_keep, text_recv, text_out),
    ):
        low = lax.axis_index(axis) == 0
        a, b = keep[...], recv[...]
        out[:ROWS] = jnp.where(low, a, b)
        out[ROWS:] = jnp.where(low, b, a)


def shards(image, text, scale, bias):
    scale, bias = scale.reshape(1), bias.reshape(1)
    half = shape((ROWS, QUART), BF16)
    image_keep, image_send, text_keep, text_send = call(split_kernel, [half] * 4, image, text, mib=4)
    text_recv = flip(text_send, "c", 1)
    piece = [shape((SLOT, WIDE), BF16)]
    (text,) = call(piece_kernel, piece, text_keep, text_recv, mib=4)

    four = [text] + [flip(text, "y", n) for n in (1, 2, 3)]
    image_recv = flip(image_send, "h", 1)
    (image,) = call(piece_kernel, piece, image_keep, image_recv, mib=4)
    (four,) = call(stack_kernel, [shape((4, SLOT, WIDE), BF16)], *four, mib=4)
    four, image = together(four, image)
    texts = [four] + [flip(four, X, n) for n in (1, 2, 3)]
    near, up, down = call(
        image_near_kernel,
        [shape((n, WIDE), BF16) for n in (3 * SLOT, FAR, FAR)],
        image,
        behind(image, "z", 3),
        behind(image, "z", -3),
        mib=4,
    )
    images = [near, behind(up, "z", 1), behind(down, "z", -1)]
    *images, t0, t1, t2, t3 = together(*images, *texts)
    texts = [t0, t1, t2, t3]
    swapped = [flip(x, "c", 1) for x in images]

    big, quad, three, one = (shape((*d, SLOT, WIDE), F32) for d in ((8,), (4,), (3,), ()))
    far = shape((FAR, WIDE), F32)
    keep, send, slope, images = call(
        slope_kernel,
        [big, big, shape((8 * SLOT, 8 * SLOT), BF16), shape((8 * SLOT, 2 * WIDE), BF16)],
        *images,
        *swapped,
        *texts,
        scale,
        bias,
        smem=2,
        scratch=[pltpu.VMEM((8 * SLOT, 2 * WIDE), BF16)],
        flops=4 * 704 * 704 * 1152,
        mib=16,
    )
    recv = flip(send, "c", 1)
    text_own, *text_out = call(text_kernel, [quad] * 4, slope, images, flops=2 * 704 * 704 * 1152, mib=12)
    image_own, below, above = call(image_first_kernel, [three, far, far], keep, recv, mib=12)
    below, above, *text_out = together(below, above, *text_out)

    def across(x, move, axis, n):
        return move(x.astype(F16), axis, n).astype(F32)

    text_in = [across(x, flip, X, n) for n, x in enumerate(text_out, 1)]
    image_in = [across(below, behind, "z", -1), across(above, behind, "z", 1)]
    image_own, below, above = call(image_sum_kernel, [one] * 3, image_own, *image_in, mib=8)
    below, above = across(below, behind, "z", -3), across(above, behind, "z", 3)
    below, above, *text_in = together(below, above, *text_in)
    text_own, *text_out = call(text_sum_kernel, [one] * 4, text_own, *text_in, mib=12)
    text_in = [across(x, flip, "y", n) for n, x in enumerate(text_out, 1)]
    image_in = [below, above]
    part = [shape((ROWS, QUART), F32)] * 2
    image_keep, image_send = call(last_kernel, part, image_own, *image_in, scale, smem=1, mib=4)
    image_recv = flip(image_send, "h", 1)
    text_keep, text_send = call(last_kernel, part, text_own, *text_in, scale, smem=1, mib=4)
    text_recv = flip(text_send, "c", 1)
    grads = [shape((2 * ROWS, QUART), F32)] * 2
    return tuple(call(place_kernel, grads, image_keep, image_recv, text_keep, text_recv, mib=4))


def solution(mesh):
    fine = Mesh(mesh.devices.reshape([SIZES[a] for a in AXES]), AXES)
    spec = P(("y", "z", "l"), ("h", "c"))
    return jax.shard_map(
        shards, mesh=fine, in_specs=(spec, spec, P(), P()), out_specs=(spec, spec), check_vma=False
    )
```

time: 134 us -> 98.8 us (0.74)
  the two profiles are of different devices: /device:TPU:8 before, /device:TPU:97 now
where the time goes in v2:
time: 98.8 us; the launch traced here: 98.7 us
  starting transfers between devices  49.2 us (50%)
  waiting for transfers between devices  35.2 us (36%)
  Pallas kernels  9.57 us (10%)
  between operations  2.2 us (2%)
  local copies, waits for them, and re-layouts  1.8 us (2%)
    ppermute x20, starting transfers between devices, flip(): return lax.ppermute(x, axis, [(i, i ^ mask) for i in range(count)])  34.2 us
    ppermute x8, waiting for transfers between devices, behind(): lax.ppermute(x, axis, [(i, (i + distance) % count) for i in range(count)])  25.5 us
    ppermute x8, starting transfers between devices, behind(): lax.ppermute(x, axis, [(i, (i + distance) % count) for i in range(count)])  15.1 us
    ppermute x20, waiting for transfers between devices, flip(): return lax.ppermute(x, axis, [(i, i ^ mask) for i in range(count)])  9.67 us
    pallas_call x13, Pallas kernels, call(): pl.pallas_call(kernel, out_shape=outs, in_specs=specs, out_specs=[VMEM] *...  9.57 us
  transfers between devices with their start and end apart: 28, of which 18 were waited for; matrix products, arithmetic and copies ran while one was open for 0% of the time, Pallas kernels for 3%

profile of v2, /device:TPU:97, one launch (start us, length us, event | category | flops | bytes accessed | tf_op | source)
XLA Modules:
  0.0 98.7 jit_solution(5926224770609252166)
XLA Ops:
  0.6 0.9 copy-done
  1.5 0.9 copy-done.1
  3.3 0.9 collective-permute-done.recv
  4.3 2.8 %collective-permute-start.3 = (bf16[96,640]{1,0:T(8,128)(2,1)S(1)}, bf16[96,640]{1,0:T(8,128)(2,1)S(1)}, u32[]{:S(2)}, u32[]{:S(2)}) collective-permute-start(bf16[96,640]{1,0:T(8,128)(2,1)S(1)} %shard_map.60.refs_0_), channel_id=1, source_target_pairs={{0,192},{64,128},{128,64},{192,0},{1,193},{65,129},{129,65},{193,1... | collective-permute-start | bytes 368648 | tf_op jit(solution)/shard_map/ppermute | solution.py:46
  7.8 2.7 %collective-permute-start.4 = (bf16[88,288]{1,0:T(8,128)(2,1)S(1)}, bf16[88,288]{1,0:T(8,128)(2,1)S(1)}, u32[]{:S(2)}, u32[]{:S(2)}) collective-permute-start(bf16[88,288]{1,0:T(8,128)(2,1)S(1)} %get-tuple-element.53), channel_id=1, source_target_pairs={{0,2},{2,0},{1,3},{3,1},{4,6},{6,4},{5,7},{7,5},{8,10},{10,8},{9,1... | collective-permute-start | bytes 152072 | tf_op jit(solution)/shard_map/ppermute | solution.py:46
  10.5 2.2 %collective-permute-done.4.recv = bf16[88,288]{1,0:T(8,128)(2,1)S(1)} collective-permute-done((bf16[88,288]{1,0:T(8,128)(2,1)S(1)}, bf16[88,288]{1,0:T(8,128)(2,1)S(1)}, u32[]{:S(2)}, u32[]{:S(2)}) %collective-permute-start.4) | collective-permute-done | bytes 50720 | tf_op jit(solution)/shard_map/ppermute | solution.py:46
  13.4 2.6 %collective-permute-start.11 = (bf16[4,96,640]{2,1,0:T(8,128)(2,1)S(1)}, bf16[4,96,640]{2,1,0:T(8,128)(2,1)S(1)}, u32[]{:S(2)}, u32[]{:S(2)}) collective-permute-start(bf16[4,96,640]{2,1,0:T(8,128)(2,1)S(1)} %shard_map.61.refs_6_), channel_id=1, source_target_pairs={{0,6},{2,4},{4,2},{6,0},{1,7},{3,5},{5,3},{7,1},{8,14},{10,12},{12... | collective-permute-start | bytes 1474568 | tf_op jit(solution)/shard_map/ppermute | solution.py:46
  16.0 1.4 %collective-permute-start.9 = (bf16[4,96,640]{2,1,0:T(8,128)(2,1)S(1)}, bf16[4,96,640]{2,1,0:T(8,128)(2,1)S(1)}, u32[]{:S(2)}, u32[]{:S(2)}) collective-permute-start(bf16[4,96,640]{2,1,0:T(8,128)(2,1)S(1)} %shard_map.61.refs_6_), channel_id=1, source_target_pairs={{0,2},{2,0},{4,6},{6,4},{1,3},{3,1},{5,7},{7,5},{8,10},{10,8},{12,... | collective-permute-start | bytes 1474568 | tf_op jit(solution)/shard_map/ppermute | solution.py:46
  17.8 4.1 %collective-permute-start.5 = (bf16[96,640]{1,0:T(8,128)(2,1)S(1)}, bf16[96,640]{1,0:T(8,128)(2,1)S(1)}, u32[]{:S(2)}, u32[]{:S(2)}) collective-permute-start(bf16[96,640]{1,0:T(8,128)(2,1)S(1)} %shard_map.62.own), channel_id=1, source_target_pairs={{0,24},{8,32},{16,40},{24,48},{32,56},{40,0},{48,8},{56,16},{1,25}... | collective-permute-start | bytes 368648 | tf_op jit(solution)/shard_map/ppermute | solution.py:51
  21.9 2.4 %collective-permute-done.6.above = bf16[96,640]{1,0:T(8,128)(2,1)S(1)} collective-permute-done((bf16[96,640]{1,0:T(8,128)(2,1)S(1)}, bf16[96,640]{1,0:T(8,128)(2,1)S(1)}, u32[]{:S(2)}, u32[]{:S(2)}) %collective-permute-start.6) | collective-permute-done | bytes 122912 | tf_op jit(solution)/shard_map/ppermute | solution.py:51
  24.3 1.0 collective-permute-done.5.below
  25.3 3.2 %collective-permute-start.7 = (bf16[240,640]{1,0:T(8,128)(2,1)S(1)}, bf16[240,640]{1,0:T(8,128)(2,1)S(1)}, u32[]{:S(2)}, u32[]{:S(2)}) collective-permute-start(bf16[240,640]{1,0:T(8,128)(2,1)S(1)} %get-tuple-element.56), channel_id=1, source_target_pairs={{0,8},{8,16},{16,24},{24,32},{32,40},{40,48},{48,56},{56,0},{1,9},... | collective-permute-start | bytes 921608 | tf_op jit(solution)/shard_map/ppermute | solution.py:51
  28.6 2.1 %collective-permute-start.8 = (bf16[240,640]{1,0:T(8,128)(2,1)S(1)}, bf16[240,640]{1,0:T(8,128)(2,1)S(1)}, u32[]{:S(2)}, u32[]{:S(2)}) collective-permute-start(bf16[240,640]{1,0:T(8,128)(2,1)S(1)} %get-tuple-element.57), channel_id=1, source_target_pairs={{0,56},{8,0},{16,8},{24,16},{32,24},{40,32},{48,40},{56,48},{1,57}... | collective-permute-start | bytes 921608 | tf_op jit(solution)/shard_map/ppermute | solution.py:51
  30.7 4.4 %collective-permute-done.7.refs_1_ = bf16[240,640]{1,0:T(8,128)(2,1)S(1)} collective-permute-done((bf16[240,640]{1,0:T(8,128)(2,1)S(1)}, bf16[240,640]{1,0:T(8,128)(2,1)S(1)}, u32[]{:S(2)}, u32[]{:S(2)}) %collective-permute-start.7) | collective-permute-done | bytes 307232 | tf_op jit(solution)/shard_map/ppermute | solution.py:51
  35.1 1.2 %collective-permute-done.8.refs_2_ = bf16[240,640]{1,0:T(8,128)(2,1)S(1)} collective-permute-done((bf16[240,640]{1,0:T(8,128)(2,1)S(1)}, bf16[240,640]{1,0:T(8,128)(2,1)S(1)}, u32[]{:S(2)}, u32[]{:S(2)}) %collective-permute-start.8) | collective-permute-done | bytes 307232 | tf_op jit(solution)/shard_map/ppermute | solution.py:51
  36.9 4.4 %collective-permute-start.12 = (bf16[288,640]{1,0:T(8,128)(2,1)S(1)}, bf16[288,640]{1,0:T(8,128)(2,1)S(1)}, u32[]{:S(2)}, u32[]{:S(2)}) collective-permute-start(bf16[288,640]{1,0:T(8,128)(2,1)S(1)} %get-tuple-element.59.refs_0_), channel_id=1, source_target_pairs={{0,1},{1,0},{2,3},{3,2},{4,5},{5,4},{6,7},{7,6},{8,9},{9,8},{10,11... | collective-permute-start | bytes 1105928 | tf_op jit(solution)/shard_map/ppermute | solution.py:46
  43.6 4.5 %shard_map.64 = (f32[8,96,640]{2,1,0:T(8,128)S(1)}, f32[8,96,640]{2,1,0:T(8,128)S(1)}, bf16[768,768]{1,0:T(8,128)(2,1)S(1)}, bf16[768,1280]{1,0:T(8,128)(2,1)S(1)}) custom-call(bf16[288,640]{1,0:T(8,128)(2,1)S(1)} %get-tuple-element.59.refs_0_, bf16[240,640]{1,0:T(8,128)(2,1)S(1)} %collective-permute-done.7.refs_1_, ...), custom_call_target="tpu_custom_call" | custom-call | flops 2283798528 | bytes 11010056 | tf_op jit(solution)/shard_map/pallas_call | solution.py:33
  48.6 2.1 %shard_map.66 = (f32[4,96,640]{2,1,0:T(8,128)S(1)}, f32[4,96,640]{2,1,0:T(8,128)S(1)}, f32[4,96,640]{2,1,0:T(8,128)S(1)}, f32[4,96,640]{2,1,0:T(8,128)S(1)}) custom-call(bf16[768,768]{1,0:T(8,128)(2,1)S(1)} %get-tuple-element.71.slope, bf16[768,1280]{1,0:T(8,128)(2,1)S(1)} %get-tuple-element.72.images), custom_call_target="tpu_custom_call" | custom-call | flops 1141899264 | bytes 7077888 | tf_op jit(solution)/shard_map/pallas_call | solution.py:33
  50.7 1.5 %collective-permute-done.15.recv = f32[8,96,640]{2,1,0:T(8,128)S(1)} collective-permute-done((f32[8,96,640]{2,1,0:T(8,128)S(1)}, f32[8,96,640]{2,1,0:T(8,128)S(1)}, u32[]{:S(2)}, u32[]{:S(2)}) %collective-permute-start.15) | collective-permute-done | bytes 1966112 | tf_op jit(solution)/shard_map/ppermute | solution.py:46
  52.7 2.6 %collective-permute-start.22 = (f16[4,96,640]{2,1,0:T(8,128)(2,1)S(1)}, f16[4,96,640]{2,1,0:T(8,128)(2,1)S(1)}, u32[]{:S(2)}, u32[]{:S(2)}) collective-permute-start(f16[4,96,640]{2,1,0:T(8,128)(2,1)S(1)} %convert_element_type.72), channel_id=1, source_target_pairs={{0,6},{2,4},{4,2},{6,0},{1,7},{3,5},{5,3},{7,1},{8,14},{10,12},{12... | collective-permute-start | bytes 1474568 | tf_op jit(solution)/shard_map/ppermute | solution.py:46
  55.3 1.5 %collective-permute-start.20 = (f16[4,96,640]{2,1,0:T(8,128)(2,1)S(1)}, f16[4,96,640]{2,1,0:T(8,128)(2,1)S(1)}, u32[]{:S(2)}, u32[]{:S(2)}) collective-permute-start(f16[4,96,640]{2,1,0:T(8,128)(2,1)S(1)} %convert_element_type.68), channel_id=1, source_target_pairs={{0,2},{2,0},{4,6},{6,4},{1,3},{3,1},{5,7},{7,5},{8,10},{10,8},{12,... | collective-permute-start | bytes 1474568 | tf_op jit(solution)/shard_map/ppermute | solution.py:46
  56.8 1.8 %collective-permute-start.17 = (f16[240,640]{1,0:T(8,128)(2,1)S(1)}, f16[240,640]{1,0:T(8,128)(2,1)S(1)}, u32[]{:S(2)}, u32[]{:S(2)}) collective-permute-start(f16[240,640]{1,0:T(8,128)(2,1)S(1)} %convert_element_type.62), channel_id=1, source_target_pairs={{0,8},{8,16},{16,24},{24,32},{32,40},{40,48},{48,56},{56,0},{1,9},... | collective-permute-start | bytes 921608 | tf_op jit(solution)/shard_map/ppermute | solution.py:51
  58.7 5.7 %collective-permute-done.17 = f16[240,640]{1,0:T(8,128)(2,1)S(1)} collective-permute-done((f16[240,640]{1,0:T(8,128)(2,1)S(1)}, f16[240,640]{1,0:T(8,128)(2,1)S(1)}, u32[]{:S(2)}, u32[]{:S(2)}) %collective-permute-start.17) | collective-permute-done | bytes 307232 | tf_op jit(solution)/shard_map/ppermute | solution.py:51
  64.5 2.7 %collective-permute-done.16 = f16[240,640]{1,0:T(8,128)(2,1)S(1)} collective-permute-done((f16[240,640]{1,0:T(8,128)(2,1)S(1)}, f16[240,640]{1,0:T(8,128)(2,1)S(1)}, u32[]{:S(2)}, u32[]{:S(2)}) %collective-permute-start.16) | collective-permute-done | bytes 307232 | tf_op jit(solution)/shard_map/ppermute | solution.py:51
  67.6 2.8 %collective-permute-start.19 = (f16[96,640]{1,0:T(8,128)(2,1)S(1)}, f16[96,640]{1,0:T(8,128)(2,1)S(1)}, u32[]{:S(2)}, u32[]{:S(2)}) collective-permute-start(f16[96,640]{1,0:T(8,128)(2,1)S(1)} %convert_element_type.66), channel_id=1, source_target_pairs={{0,24},{8,32},{16,40},{24,48},{32,56},{40,0},{48,8},{56,16},{1,25}... | collective-permute-start | bytes 368648 | tf_op jit(solution)/shard_map/ppermute | solution.py:51
  71.1 2.5 %collective-permute-done.19 = f16[96,640]{1,0:T(8,128)(2,1)S(1)} collective-permute-done((f16[96,640]{1,0:T(8,128)(2,1)S(1)}, f16[96,640]{1,0:T(8,128)(2,1)S(1)}, u32[]{:S(2)}, u32[]{:S(2)}) %collective-permute-start.19) | collective-permute-done | bytes 122912 | tf_op jit(solution)/shard_map/ppermute | solution.py:51
  73.6 5.5 %collective-permute-done.18 = f16[96,640]{1,0:T(8,128)(2,1)S(1)} collective-permute-done((f16[96,640]{1,0:T(8,128)(2,1)S(1)}, f16[96,640]{1,0:T(8,128)(2,1)S(1)}, u32[]{:S(2)}, u32[]{:S(2)}) %collective-permute-start.18) | collective-permute-done | bytes 122912 | tf_op jit(solution)/shard_map/ppermute | solution.py:51
  80.0 4.0 %collective-permute-start.26 = (f16[96,640]{1,0:T(8,128)(2,1)S(1)}, f16[96,640]{1,0:T(8,128)(2,1)S(1)}, u32[]{:S(2)}, u32[]{:S(2)}) collective-permute-start(f16[96,640]{1,0:T(8,128)(2,1)S(1)} %convert_element_type.78), channel_id=1, source_target_pairs={{0,192},{64,128},{128,64},{192,0},{1,193},{65,129},{129,65},{193,1... | collective-permute-start | bytes 368648 | tf_op jit(solution)/shard_map/ppermute | solution.py:46
  85.0 1.7 %collective-permute-start.23 = (f32[88,288]{1,0:T(8,128)S(1)}, f32[88,288]{1,0:T(8,128)S(1)}, u32[]{:S(2)}, u32[]{:S(2)}) collective-permute-start(f32[88,288]{1,0:T(8,128)S(1)} %get-tuple-element.87), channel_id=1, source_target_pairs={{0,2},{2,0},{1,3},{3,1},{4,6},{6,4},{5,7},{7,5},{8,10},{10,8},{9,1... | collective-permute-start | bytes 304136 | tf_op jit(solution)/shard_map/ppermute | solution.py:46
  87.1 2.1 %collective-permute-done.25 = f16[96,640]{1,0:T(8,128)(2,1)S(1)} collective-permute-done((f16[96,640]{1,0:T(8,128)(2,1)S(1)}, f16[96,640]{1,0:T(8,128)(2,1)S(1)}, u32[]{:S(2)}, u32[]{:S(2)}) %collective-permute-start.25) | collective-permute-done | bytes 122912 | tf_op jit(solution)/shard_map/ppermute | solution.py:46
  89.5 7.3 %collective-permute-start.27 = (f32[88,288]{1,0:T(8,128)S(1)}, f32[88,288]{1,0:T(8,128)S(1)}, u32[]{:S(2)}, u32[]{:S(2)}) collective-permute-start(f32[88,288]{1,0:T(8,128)S(1)} %get-tuple-element.97), channel_id=1, source_target_pairs={{0,1},{1,0},{2,3},{3,2},{4,5},{5,4},{6,7},{7,6},{8,9},{9,8},{10,11... | collective-permute-start | bytes 304136 | tf_op jit(solution)/shard_map/ppermute | solution.py:46
  96.8 1.0 %collective-permute-done.27.text_recv = f32[88,288]{1,0:T(8,128)S(1)} collective-permute-done((f32[88,288]{1,0:T(8,128)S(1)}, f32[88,288]{1,0:T(8,128)S(1)}, u32[]{:S(2)}, u32[]{:S(2)}) %collective-permute-start.27) | collective-permute-done | bytes 101408 | tf_op jit(solution)/shard_map/ppermute | solution.py:46
  (61 shorter events, 9.9 us)
Async XLA Ops:
  0.6 0.9 copy-start
  1.5 0.9 copy-start.1
  2.5 1.7 %collective-permute-start = (bf16[88,288]{1,0:T(8,128)(2,1)S(1)}, bf16[88,288]{1,0:T(8,128)(2,1)S(1)}, u32[]{:S(2)}, u32[]{:S(2)}) collective-permute-start(bf16[88,288]{1,0:T(8,128)(2,1)S(1)} %get-tuple-element.51), channel_id=1, source_target_pairs={{0,1},{1,0},{2,3},{3,2},{4,5},{5,4},{6,7},{7,6},{8,9},{9,8},{10,11... | collective-permute-start | bytes 152072 | tf_op jit(solution)/shard_map/ppermute | solution.py:46
  4.3 8.5 %collective-permute-start.3 = (bf16[96,640]{1,0:T(8,128)(2,1)S(1)}, bf16[96,640]{1,0:T(8,128)(2,1)S(1)}, u32[]{:S(2)}, u32[]{:S(2)}) collective-permute-start(bf16[96,640]{1,0:T(8,128)(2,1)S(1)} %shard_map.60.refs_0_), channel_id=1, source_target_pairs={{0,192},{64,128},{128,64},{192,0},{1,193},{65,129},{129,65},{193,1... | collective-permute-start | bytes 368648 | tf_op jit(solution)/shard_map/ppermute | solution.py:46
  7.1 5.7 %collective-permute-start.2 = (bf16[96,640]{1,0:T(8,128)(2,1)S(1)}, bf16[96,640]{1,0:T(8,128)(2,1)S(1)}, u32[]{:S(2)}, u32[]{:S(2)}) collective-permute-start(bf16[96,640]{1,0:T(8,128)(2,1)S(1)} %shard_map.60.refs_0_), channel_id=1, source_target_pairs={{0,128},{64,192},{128,0},{192,64},{1,129},{65,193},{129,1},{193,65... | collective-permute-start | bytes 368648 | tf_op jit(solution)/shard_map/ppermute | solution.py:46
  7.5 6.0 %collective-permute-start.1 = (bf16[96,640]{1,0:T(8,128)(2,1)S(1)}, bf16[96,640]{1,0:T(8,128)(2,1)S(1)}, u32[]{:S(2)}, u32[]{:S(2)}) collective-permute-start(bf16[96,640]{1,0:T(8,128)(2,1)S(1)} %shard_map.60.refs_0_), channel_id=1, source_target_pairs={{0,64},{64,0},{128,192},{192,128},{1,65},{65,1},{129,193},{193,129... | collective-permute-start | bytes 368648 | tf_op jit(solution)/shard_map/ppermute | solution.py:46
  7.8 4.9 %collective-permute-start.4 = (bf16[88,288]{1,0:T(8,128)(2,1)S(1)}, bf16[88,288]{1,0:T(8,128)(2,1)S(1)}, u32[]{:S(2)}, u32[]{:S(2)}) collective-permute-start(bf16[88,288]{1,0:T(8,128)(2,1)S(1)} %get-tuple-element.53), channel_id=1, source_target_pairs={{0,2},{2,0},{1,3},{3,1},{4,6},{6,4},{5,7},{7,5},{8,10},{10,8},{9,1... | collective-permute-start | bytes 152072 | tf_op jit(solution)/shard_map/ppermute | solution.py:46
  13.4 22.9 %collective-permute-start.11 = (bf16[4,96,640]{2,1,0:T(8,128)(2,1)S(1)}, bf16[4,96,640]{2,1,0:T(8,128)(2,1)S(1)}, u32[]{:S(2)}, u32[]{:S(2)}) collective-permute-start(bf16[4,96,640]{2,1,0:T(8,128)(2,1)S(1)} %shard_map.61.refs_6_), channel_id=1, source_target_pairs={{0,6},{2,4},{4,2},{6,0},{1,7},{3,5},{5,3},{7,1},{8,14},{10,12},{12... | collective-permute-start | bytes 1474568 | tf_op jit(solution)/shard_map/ppermute | solution.py:46
  16.0 20.4 %collective-permute-start.10 = (bf16[4,96,640]{2,1,0:T(8,128)(2,1)S(1)}, bf16[4,96,640]{2,1,0:T(8,128)(2,1)S(1)}, u32[]{:S(2)}, u32[]{:S(2)}) collective-permute-start(bf16[4,96,640]{2,1,0:T(8,128)(2,1)S(1)} %shard_map.61.refs_6_), channel_id=1, source_target_pairs={{0,4},{2,6},{4,0},{6,2},{1,5},{3,7},{5,1},{7,3},{8,12},{10,14},{12... | collective-permute-start | bytes 1474568 | tf_op jit(solution)/shard_map/ppermute | solution.py:46
  16.0 20.8 %collective-permute-start.9 = (bf16[4,96,640]{2,1,0:T(8,128)(2,1)S(1)}, bf16[4,96,640]{2,1,0:T(8,128)(2,1)S(1)}, u32[]{:S(2)}, u32[]{:S(2)}) collective-permute-start(bf16[4,96,640]{2,1,0:T(8,128)(2,1)S(1)} %shard_map.61.refs_6_), channel_id=1, source_target_pairs={{0,2},{2,0},{4,6},{6,4},{1,3},{3,1},{5,7},{7,5},{8,10},{10,8},{12,... | collective-permute-start | bytes 1474568 | tf_op jit(solution)/shard_map/ppermute | solution.py:46
  17.4 6.9 %collective-permute-start.6 = (bf16[96,640]{1,0:T(8,128)(2,1)S(1)}, bf16[96,640]{1,0:T(8,128)(2,1)S(1)}, u32[]{:S(2)}, u32[]{:S(2)}) collective-permute-start(bf16[96,640]{1,0:T(8,128)(2,1)S(1)} %shard_map.62.own), channel_id=1, source_target_pairs={{0,40},{8,48},{16,56},{24,0},{32,8},{40,16},{48,24},{56,32},{1,41}... | collective-permute-start | bytes 368648 | tf_op jit(solution)/shard_map/ppermute | solution.py:51
  17.8 7.5 %collective-permute-start.5 = (bf16[96,640]{1,0:T(8,128)(2,1)S(1)}, bf16[96,640]{1,0:T(8,128)(2,1)S(1)}, u32[]{:S(2)}, u32[]{:S(2)}) collective-permute-start(bf16[96,640]{1,0:T(8,128)(2,1)S(1)} %shard_map.62.own), channel_id=1, source_target_pairs={{0,24},{8,32},{16,40},{24,48},{32,56},{40,0},{48,8},{56,16},{1,25}... | collective-permute-start | bytes 368648 | tf_op jit(solution)/shard_map/ppermute | solution.py:51
  25.3 9.8 %collective-permute-start.7 = (bf16[240,640]{1,0:T(8,128)(2,1)S(1)}, bf16[240,640]{1,0:T(8,128)(2,1)S(1)}, u32[]{:S(2)}, u32[]{:S(2)}) collective-permute-start(bf16[240,640]{1,0:T(8,128)(2,1)S(1)} %get-tuple-element.56), channel_id=1, source_target_pairs={{0,8},{8,16},{16,24},{24,32},{32,40},{40,48},{48,56},{56,0},{1,9},... | collective-permute-start | bytes 921608 | tf_op jit(solution)/shard_map/ppermute | solution.py:51
  28.6 7.8 %collective-permute-start.8 = (bf16[240,640]{1,0:T(8,128)(2,1)S(1)}, bf16[240,640]{1,0:T(8,128)(2,1)S(1)}, u32[]{:S(2)}, u32[]{:S(2)}) collective-permute-start(bf16[240,640]{1,0:T(8,128)(2,1)S(1)} %get-tuple-element.57), channel_id=1, source_target_pairs={{0,56},{8,0},{16,8},{24,16},{32,24},{40,32},{48,40},{56,48},{1,57}... | collective-permute-start | bytes 921608 | tf_op jit(solution)/shard_map/ppermute | solution.py:51
  36.9 6.8 %collective-permute-start.12 = (bf16[288,640]{1,0:T(8,128)(2,1)S(1)}, bf16[288,640]{1,0:T(8,128)(2,1)S(1)}, u32[]{:S(2)}, u32[]{:S(2)}) collective-permute-start(bf16[288,640]{1,0:T(8,128)(2,1)S(1)} %get-tuple-element.59.refs_0_), channel_id=1, source_target_pairs={{0,1},{1,0},{2,3},{3,2},{4,5},{5,4},{6,7},{7,6},{8,9},{9,8},{10,11... | collective-permute-start | bytes 1105928 | tf_op jit(solution)/shard_map/ppermute | solution.py:46
  41.3 1.9 %collective-permute-start.13 = (bf16[240,640]{1,0:T(8,128)(2,1)S(1)}, bf16[240,640]{1,0:T(8,128)(2,1)}, u32[]{:S(2)}, u32[]{:S(2)}) collective-permute-start(bf16[240,640]{1,0:T(8,128)(2,1)S(1)} %collective-permute-done.7.refs_1_), channel_id=1, source_target_pairs={{0,1},{1,0},{2,3},{3,2},{4,5},{5,4},{6,7},{7,6},{8,9},{9,8},{10,11... | collective-permute-start | bytes 921608 | tf_op jit(solution)/shard_map/ppermute | solution.py:46
  41.4 2.2 %collective-permute-start.14 = (bf16[240,640]{1,0:T(8,128)(2,1)S(1)}, bf16[240,640]{1,0:T(8,128)(2,1)}, u32[]{:S(2)}, u32[]{:S(2)}) collective-permute-start(bf16[240,640]{1,0:T(8,128)(2,1)S(1)} %collective-permute-done.8.refs_2_), channel_id=1, source_target_pairs={{0,1},{1,0},{2,3},{3,2},{4,5},{5,4},{6,7},{7,6},{8,9},{9,8},{10,11... | collective-permute-start | bytes 921608 | tf_op jit(solution)/shard_map/ppermute | solution.py:46
  48.1 4.1 %collective-permute-start.15 = (f32[8,96,640]{2,1,0:T(8,128)S(1)}, f32[8,96,640]{2,1,0:T(8,128)S(1)}, u32[]{:S(2)}, u32[]{:S(2)}) collective-permute-start(f32[8,96,640]{2,1,0:T(8,128)S(1)} %get-tuple-element.67), channel_id=1, source_target_pairs={{0,1},{1,0},{2,3},{3,2},{4,5},{5,4},{6,7},{7,6},{8,9},{9,8},{10,11... | collective-permute-start | bytes 5898248 | tf_op jit(solution)/shard_map/ppermute | solution.py:46
  52.7 26.5 %collective-permute-start.22 = (f16[4,96,640]{2,1,0:T(8,128)(2,1)S(1)}, f16[4,96,640]{2,1,0:T(8,128)(2,1)S(1)}, u32[]{:S(2)}, u32[]{:S(2)}) collective-permute-start(f16[4,96,640]{2,1,0:T(8,128)(2,1)S(1)} %convert_element_type.72), channel_id=1, source_target_pairs={{0,6},{2,4},{4,2},{6,0},{1,7},{3,5},{5,3},{7,1},{8,14},{10,12},{12... | collective-permute-start | bytes 1474568 | tf_op jit(solution)/shard_map/ppermute | solution.py:46
  55.2 24.0 %collective-permute-start.21 = (f16[4,96,640]{2,1,0:T(8,128)(2,1)S(1)}, f16[4,96,640]{2,1,0:T(8,128)(2,1)S(1)}, u32[]{:S(2)}, u32[]{:S(2)}) collective-permute-start(f16[4,96,640]{2,1,0:T(8,128)(2,1)S(1)} %convert_element_type.70), channel_id=1, source_target_pairs={{0,4},{2,6},{4,0},{6,2},{1,5},{3,7},{5,1},{7,3},{8,12},{10,14},{12... | collective-permute-start | bytes 1474568 | tf_op jit(solution)/shard_map/ppermute | solution.py:46
  55.3 24.0 %collective-permute-start.20 = (f16[4,96,640]{2,1,0:T(8,128)(2,1)S(1)}, f16[4,96,640]{2,1,0:T(8,128)(2,1)S(1)}, u32[]{:S(2)}, u32[]{:S(2)}) collective-permute-start(f16[4,96,640]{2,1,0:T(8,128)(2,1)S(1)} %convert_element_type.68), channel_id=1, source_target_pairs={{0,2},{2,0},{4,6},{6,4},{1,3},{3,1},{5,7},{7,5},{8,10},{10,8},{12,... | collective-permute-start | bytes 1474568 | tf_op jit(solution)/shard_map/ppermute | solution.py:46
  56.8 7.6 %collective-permute-start.17 = (f16[240,640]{1,0:T(8,128)(2,1)S(1)}, f16[240,640]{1,0:T(8,128)(2,1)S(1)}, u32[]{:S(2)}, u32[]{:S(2)}) collective-permute-start(f16[240,640]{1,0:T(8,128)(2,1)S(1)} %convert_element_type.62), channel_id=1, source_target_pairs={{0,8},{8,16},{16,24},{24,32},{32,40},{40,48},{48,56},{56,0},{1,9},... | collective-permute-start | bytes 921608 | tf_op jit(solution)/shard_map/ppermute | solution.py:51
  58.6 8.6 %collective-permute-start.16 = (f16[240,640]{1,0:T(8,128)(2,1)S(1)}, f16[240,640]{1,0:T(8,128)(2,1)S(1)}, u32[]{:S(2)}, u32[]{:S(2)}) collective-permute-start(f16[240,640]{1,0:T(8,128)(2,1)S(1)} %convert_element_type.60), channel_id=1, source_target_pairs={{0,56},{8,0},{16,8},{24,16},{32,24},{40,32},{48,40},{56,48},{1,57}... | collective-permute-start | bytes 921608 | tf_op jit(solution)/shard_map/ppermute | solution.py:51
  67.6 5.9 %collective-permute-start.19 = (f16[96,640]{1,0:T(8,128)(2,1)S(1)}, f16[96,640]{1,0:T(8,128)(2,1)S(1)}, u32[]{:S(2)}, u32[]{:S(2)}) collective-permute-start(f16[96,640]{1,0:T(8,128)(2,1)S(1)} %convert_element_type.66), channel_id=1, source_target_pairs={{0,24},{8,32},{16,40},{24,48},{32,56},{40,0},{48,8},{56,16},{1,25}... | collective-permute-start | bytes 368648 | tf_op jit(solution)/shard_map/ppermute | solution.py:51
  70.4 8.7 %collective-permute-start.18 = (f16[96,640]{1,0:T(8,128)(2,1)S(1)}, f16[96,640]{1,0:T(8,128)(2,1)S(1)}, u32[]{:S(2)}, u32[]{:S(2)}) collective-permute-start(f16[96,640]{1,0:T(8,128)(2,1)S(1)} %convert_element_type.64), channel_id=1, source_target_pairs={{0,40},{8,48},{16,56},{24,0},{32,8},{40,16},{48,24},{56,32},{1,41}... | collective-permute-start | bytes 368648 | tf_op jit(solution)/shard_map/ppermute | solution.py:51
  80.0 7.2 %collective-permute-start.26 = (f16[96,640]{1,0:T(8,128)(2,1)S(1)}, f16[96,640]{1,0:T(8,128)(2,1)S(1)}, u32[]{:S(2)}, u32[]{:S(2)}) collective-permute-start(f16[96,640]{1,0:T(8,128)(2,1)S(1)} %convert_element_type.78), channel_id=1, source_target_pairs={{0,192},{64,128},{128,64},{192,0},{1,193},{65,129},{129,65},{193,1... | collective-permute-start | bytes 368648 | tf_op jit(solution)/shard_map/ppermute | solution.py:46
  84.0 5.2 %collective-permute-start.25 = (f16[96,640]{1,0:T(8,128)(2,1)S(1)}, f16[96,640]{1,0:T(8,128)(2,1)S(1)}, u32[]{:S(2)}, u32[]{:S(2)}) collective-permute-start(f16[96,640]{1,0:T(8,128)(2,1)S(1)} %convert_element_type.76), channel_id=1, source_target_pairs={{0,128},{64,192},{128,0},{192,64},{1,129},{65,193},{129,1},{193,65... | collective-permute-start | bytes 368648 | tf_op jit(solution)/shard_map/ppermute | solution.py:46
  84.4 4.8 %collective-permute-start.24 = (f16[96,640]{1,0:T(8,128)(2,1)S(1)}, f16[96,640]{1,0:T(8,128)(2,1)S(1)}, u32[]{:S(2)}, u32[]{:S(2)}) collective-permute-start(f16[96,640]{1,0:T(8,128)(2,1)S(1)} %convert_element_type.74), channel_id=1, source_target_pairs={{0,64},{64,0},{128,192},{192,128},{1,65},{65,1},{129,193},{193,129... | collective-permute-start | bytes 368648 | tf_op jit(solution)/shard_map/ppermute | solution.py:46
  85.0 11.8 %collective-permute-start.23 = (f32[88,288]{1,0:T(8,128)S(1)}, f32[88,288]{1,0:T(8,128)S(1)}, u32[]{:S(2)}, u32[]{:S(2)}) collective-permute-start(f32[88,288]{1,0:T(8,128)S(1)} %get-tuple-element.87), channel_id=1, source_target_pairs={{0,2},{2,0},{1,3},{3,1},{4,6},{6,4},{5,7},{7,5},{8,10},{10,8},{9,1... | collective-permute-start | bytes 304136 | tf_op jit(solution)/shard_map/ppermute | solution.py:46
  89.5 8.3 %collective-permute-start.27 = (f32[88,288]{1,0:T(8,128)S(1)}, f32[88,288]{1,0:T(8,128)S(1)}, u32[]{:S(2)}, u32[]{:S(2)}) collective-permute-start(f32[88,288]{1,0:T(8,128)S(1)} %get-tuple-element.97), channel_id=1, source_target_pairs={{0,1},{1,0},{2,3},{3,2},{4,5},{5,4},{6,7},{7,6},{8,9},{9,8},{10,11... | collective-permute-start | bytes 304136 | tf_op jit(solution)/shard_map/ppermute | solution.py:46

commit v3 on v2

v3 whole, which is shorter than its diff:
```python
import jax
import jax.numpy as jnp
from jax import lax
from jax.experimental import pallas as pl
from jax.experimental.pallas import tpu as pltpu
from jax.sharding import Mesh
from jax.sharding import PartitionSpec as P

AXES = ("y", "z", "l", "h", "c")
SIZES = {"y": 4, "z": 8, "l": 2, "h": 2, "c": 2}
ROWS = 88
SLOT = 96
QUART = 288
HALF = 576
WIDE = 640
X = ("l", "h")
F32 = jnp.float32
BF16 = jnp.bfloat16
F16 = jnp.float16
VMEM = pl.BlockSpec(memory_space=pltpu.VMEM)
SMEM = pl.BlockSpec(memory_space=pltpu.SMEM)


def shape(dims, dtype):
    return jax.ShapeDtypeStruct(dims, dtype)


def call(kernel, outs, *args, smem=0, scratch=(), flops=0, mib=32):
    specs = [VMEM] * (len(args) - smem) + [SMEM] * smem
    moved = sum(a.size * a.dtype.itemsize for a in (*args, *outs))
    return pl.pallas_call(
        kernel,
        out_shape=outs,
        in_specs=specs,
        out_specs=[VMEM] * len(outs),
        scratch_shapes=list(scratch),
        compiler_params=pltpu.CompilerParams(vmem_limit_bytes=mib * 2**20),
        cost_estimate=pl.CostEstimate(flops=flops, bytes_accessed=moved, transcendentals=0),
    )(*args)


def flip(x, axis, mask):
    count = 4 if axis == X else SIZES[axis]
    return lax.ppermute(x, axis, [(i, i ^ mask) for i in range(count)])


def behind(x, axis, distance):
    count = SIZES[axis]
    return lax.ppermute(x, axis, [(i, (i + distance) % count) for i in range(count)])


def together(*xs):
    return lax.optimization_barrier(xs)


def split_kernel(image, text, image_keep, image_send, text_keep, text_send):
    for source, axis, keep, send in (
        (image, "h", image_keep, image_send),
        (text, "c", text_keep, text_send),
    ):
        low = lax.axis_index(axis) == 0
        x = source[...].astype(F32)
        first, second = x[:ROWS], x[ROWS:]
        keep[...] = jnp.where(low, first, second).astype(BF16)
        sent = jnp.where(low, second, first)
        if send is image_send:
            sent = jnp.concatenate([sent, jnp.zeros((ROWS, WIDE - QUART), F32)], axis=1)
            sent = jnp.concatenate([sent, jnp.zeros((SLOT - ROWS, WIDE), F32)], axis=0)
        send[...] = sent.astype(BF16)


def piece_kernel(keep, recv, out):
    a, b = keep[...].astype(F32), recv[...].astype(F32)[:ROWS, :QUART]
    out[...] = jnp.concatenate([a, b, jnp.zeros((ROWS, WIDE - HALF), F32)], axis=1).astype(BF16)


def stack_kernel(*refs):
    for n, ref in enumerate(refs[:-1]):
        refs[-1][n] = ref[...]


def scaled(x):
    most = jnp.max(jnp.max(jnp.abs(x), axis=0, keepdims=True), axis=1, keepdims=True)
    power = jnp.floor(jnp.log2(jnp.maximum(most, 1e-30)))
    lane = lax.broadcasted_iota(jnp.int32, x.shape, 1)
    return jnp.where(lane < HALF, x * jnp.exp2(13.0 - power), power)


def unscaled(p):
    return p * jnp.exp2(p[:1, HALF : HALF + 1] - 13.0)


def slope_kernel(*refs):
    halves, text, across = (refs[0:3], refs[3:6]), refs[6:9], refs[9:13]
    scale_ref, bias_ref = refs[13:15]
    keep, send, slope, images = refs[15:19]
    texts = refs[19]
    scale, bias = scale_ref[0], bias_ref[0]
    zeros = jnp.zeros((ROWS, WIDE - HALF), BF16)
    for s in range(8):
        rows = pl.ds(SLOT * s, ROWS)
        for half, parts in enumerate(halves):
            images[rows, WIDE * half : WIDE * (half + 1)] = parts[s // 3][s % 3]
        a, b = (text[0][s], across[s][...]) if s < 4 else (text[1][s - 4], text[2][s - 4])
        texts[rows, 0:WIDE] = jnp.concatenate([a[:, :QUART], b[:, :QUART], zeros], axis=1)
        texts[rows, WIDE:] = jnp.concatenate([a[:, QUART:HALF], b[:, QUART:HALF], zeros], axis=1)
        rows = pl.ds(SLOT * s + ROWS, SLOT - ROWS)
        images[rows, :] = jnp.zeros((SLOT - ROWS, 2 * WIDE), BF16)
        texts[rows, :] = jnp.zeros((SLOT - ROWS, 2 * WIDE), BF16)
    own = lax.axis_index("h") == lax.axis_index("c")
    for j in range(3):
        cols = pl.ds(256 * j, 256)
        dots = lax.dot_general(
            images[...], texts[cols, :], (((1,), (1,)), ((), ())), preferred_element_type=F32
        )
        logit = scale * dots + bias
        value = jax.nn.sigmoid(logit)
        if j == 0:
            top = logit[:SLOT]
            row = lax.broadcasted_iota(jnp.int32, top.shape, 0)
            col = lax.broadcasted_iota(jnp.int32, top.shape, 1)
            paired = (col == row) & (row < ROWS) & own
            top = jnp.where(paired, -jax.nn.sigmoid(-top), value[:SLOT])
            value = jnp.concatenate([top, value[SLOT:]], axis=0)
        slope[:, cols] = value.astype(BF16)
    add = jnp.dot(slope[...], texts[...], preferred_element_type=F32)
    for s in range(8):
        keep[s] = add[SLOT * s : SLOT * s + ROWS, :WIDE]
        send[s] = add[SLOT * s : SLOT * s + ROWS, WIDE:]


def text_kernel(slope, images, own, two, three, *across):
    total = lax.dot_general(
        slope[...], images[...], (((0,), (0,)), ((), ())), preferred_element_type=F32
    )
    pad = jnp.zeros((ROWS, WIDE - HALF), F32)
    for s in range(8):
        x = total[SLOT * s : SLOT * s + ROWS, :]
        for d in range(2):
            low, high = x[:, QUART * d : QUART * (d + 1)], x[:, WIDE + QUART * d : WIDE + QUART * (d + 1)]
            part = jnp.concatenate([low, high, pad], axis=1)
            if s >= 4:
                (two, three)[d][s - 4] = scaled(part)
            elif d == 0:
                own[s] = part
            else:
                across[s][...] = part if s == 0 else scaled(part)


def image_first_kernel(keep, recv, own, below, above):
    for s in range(8):
        x = keep[s] + recv[s]
        if s < 3:
            own[s] = x
        else:
            (below, above)[s // 3 - 1][s % 3] = scaled(x)


def image_sum_kernel(own, from_above, from_below, kept, below, above):
    kept[...] = own[0] + unscaled(from_above[0]) + unscaled(from_below[0])
    below[...] = scaled(own[1] + unscaled(from_above[1]) + unscaled(from_below[1]))
    above[...] = scaled(own[2] + unscaled(from_above[2]))


def text_across_kernel(own, r1, r2, r3, out):
    out[...] = scaled(own[...] + unscaled(r1[...]) + unscaled(r2[...]) + unscaled(r3[...]))


def text_sum_kernel(own, r2, r3, kept, *outs):
    for n in range(4):
        x = own[n] + unscaled(r2[n]) + unscaled(r3[n])
        if n == 0:
            kept[...] = x
        else:
            outs[n - 1][...] = scaled(x)


def last_kernel(*refs):
    own, *parts, scale, keep, send = refs
    x = own[...]
    for part in parts:
        x = x + unscaled(part[...])
    x = scale[0] * x
    keep[...] = x[:, :QUART]
    send[:, :QUART] = x[:, QUART:HALF]
    send[:, QUART:] = jnp.zeros((ROWS, send.shape[1] - QUART), F32)


def place_kernel(image_keep, image_recv, text_keep, text_recv, image_out, text_out):
    for axis, keep, recv, out in (
        ("h", image_keep, image_recv, image_out),
        ("c", text_keep, text_recv, text_out),
    ):
        low = lax.axis_index(axis) == 0
        a, b = keep[...], recv[...][:, :QUART]
        out[:ROWS] = jnp.where(low, a, b)
        out[ROWS:] = jnp.where(low, b, a)


def shards(image, text, scale, bias):
    scale, bias = scale.reshape(1), bias.reshape(1)
    half = shape((ROWS, QUART), BF16)
    image_keep, image_send, text_keep, text_send = call(
        split_kernel, [half, shape((SLOT, WIDE), BF16), half, half], image, text, mib=4
    )
    image_recv = flip(image_send, "h", 1)
    text_recv = flip(text_send, "c", 1)
    piece = [shape((ROWS, WIDE), BF16)]
    (text,) = call(piece_kernel, piece, text_keep, text_recv, mib=4)
    (image,) = call(piece_kernel, piece, image_keep, image_recv, mib=4)

    def stacked(*xs):
        return call(stack_kernel, [shape((len(xs), ROWS, WIDE), BF16)], *xs, mib=4)[0]

    four = stacked(text, *(flip(text, "y", n) for n in (1, 2, 3)))
    other = flip(text, "h", 1)
    other = [other] + [flip(other, "y", n) for n in (1, 2, 3)]
    texts = [four] + [flip(four, X, n) for n in (2, 3)]
    near = image, behind(image, "z", 3), behind(image, "z", -3)
    trio, duo, *other = together(stacked(*near), stacked(*near[:2]), *other)
    images = [trio, behind(trio, "z", 1), behind(duo, "z", -1)]
    *images, t0, t1, t2 = together(*images, *texts)
    texts = [t0, t1, t2, *other]
    swapped = [flip(x, "c", 1) for x in images]

    big, quad, three, one = (shape((*d, ROWS, WIDE), F32) for d in ((8,), (4,), (3,), ()))
    two = shape((2, ROWS, WIDE), F32)
    keep, send, slope, images = call(
        slope_kernel,
        [big, big, shape((8 * SLOT, 8 * SLOT), BF16), shape((8 * SLOT, 2 * WIDE), BF16)],
        *images,
        *swapped,
        *texts,
        scale,
        bias,
        smem=2,
        scratch=[pltpu.VMEM((8 * SLOT, 2 * WIDE), BF16)],
        flops=4 * 704 * 704 * 1152,
        mib=16,
    )
    recv = flip(send, "c", 1)
    text_own, *text_out = call(
        text_kernel, [quad] * 3 + [one] * 4, slope, images, flops=2 * 704 * 704 * 1152, mib=12
    )
    text_out, text_across, *across_out = text_out[:2], *text_out[2:]
    image_own, below, above = call(image_first_kernel, [three, three, two], keep, recv, mib=12)
    below, above, *text_out = together(below, above, *text_out)

    def moved(x, move, axis, n):
        return move(x.astype(F16), axis, n).astype(F32)

    across_in = [moved(x, flip, "y", n) for n, x in enumerate(across_out, 1)]
    text_in = [moved(x, flip, X, n) for n, x in zip((2, 3), text_out)]
    image_in = [moved(below, behind, "z", -1), moved(above, behind, "z", 1)]
    (across,) = call(text_across_kernel, [one], text_across, *across_in, mib=4)
    across = moved(across, flip, "h", 1)
    image_own, below, above = call(image_sum_kernel, [one] * 3, image_own, *image_in, mib=8)
    below, above = moved(below, behind, "z", -3), moved(above, behind, "z", 3)
    below, above, *text_in = together(below, above, *text_in)
    text_own, *text_out = call(text_sum_kernel, [one] * 4, text_own, *text_in, mib=12)
    text_in = [across] + [moved(x, flip, "y", n) for n, x in enumerate(text_out, 1)]
    image_in = [below, above]
    part = [shape((ROWS, n), F32) for n in (QUART, 384)]
    image_keep, image_send = call(last_kernel, part, image_own, *image_in, scale, smem=1, mib=4)
    image_recv = flip(image_send, "h", 1)
    text_keep, text_send = call(last_kernel, part, text_own, *text_in, scale, smem=1, mib=4)
    text_recv = flip(text_send, "c", 1)
    grads = [shape((2 * ROWS, QUART), F32)] * 2
    return tuple(call(place_kernel, grads, image_keep, image_recv, text_keep, text_recv, mib=4))


def solution(mesh):
    fine = Mesh(mesh.devices.reshape([SIZES[a] for a in AXES]), AXES)
    spec = P(("y", "z", "l"), ("h", "c"))
    return jax.shard_map(
        shards, mesh=fine, in_specs=(spec, spec, P(), P()), out_specs=(spec, spec), check_vma=False
    )
```

time: 98.8 us -> 90.7 us (0.918)
  the two profiles are of different devices: /device:TPU:97 before, /device:TPU:8 now
where the time goes in v3:
time: 90.7 us; the launch traced here: 89.5 us
  starting transfers between devices  50.9 us (56%)
  waiting for transfers between devices  23.6 us (26%)
  Pallas kernels  8.64 us (10%)
  local copies, waits for them, and re-layouts  3.34 us (4%)
  between operations  2.34 us (3%)
    ppermute x26, starting transfers between devices, flip(): return lax.ppermute(x, axis, [(i, i ^ mask) for i in range(count)])  35.9 us
    ppermute x8, starting transfers between devices, behind(): lax.ppermute(x, axis, [(i, (i + distance) % count) for i in range(count)])  15 us
    ppermute x8, waiting for transfers between devices, behind(): lax.ppermute(x, axis, [(i, (i + distance) % count) for i in range(count)])  15 us
    pallas_call x15, Pallas kernels, call(): pl.pallas_call(kernel, out_shape=outs, in_specs=specs, out_specs=[VMEM] *...  8.64 us
    ppermute x26, waiting for transfers between devices, flip(): return lax.ppermute(x, axis, [(i, i ^ mask) for i in range(count)])  8.54 us
    unnamed x8, local copies, waits for them, and re-layouts  3.34 us
  transfers between devices with their start and end apart: 34, of which 11 were waited for; matrix products, arithmetic and copies ran while one was open for 1% of the time, Pallas kernels for 4%

profile of v3, /device:TPU:8, one launch (start us, length us, event | category | flops | bytes accessed | tf_op | source)
XLA Modules:
  0.0 89.5 jit_solution(14664531232636677665)
XLA Ops:
  2.6 3.1 %collective-permute-start = (bf16[96,640]{1,0:T(8,128)(2,1)S(1)}, bf16[96,640]{1,0:T(8,128)(2,1)S(1)}, u32[]{:S(2)}, u32[]{:S(2)}) collective-permute-start(bf16[96,640]{1,0:T(8,128)(2,1)S(1)} %get-tuple-element.52), channel_id=1, source_target_pairs={{0,2},{2,0},{1,3},{3,1},{4,6},{6,4},{5,7},{7,5},{8,10},{10,8},{9,1... | collective-permute-start | bytes 368648 | tf_op jit(solution)/shard_map/ppermute | solution.py:44
  5.8 1.7 %collective-permute-start.12 = (bf16[88,640]{1,0:T(8,128)(2,1)S(1)}, bf16[88,640]{1,0:T(8,128)(2,1)S(1)}, u32[]{:S(2)}, u32[]{:S(2)}) collective-permute-start(bf16[88,640]{1,0:T(8,128)(2,1)S(1)} %shard_map.63.refs_0_), channel_id=1, source_target_pairs={{0,192},{64,128},{128,64},{192,0},{1,193},{65,129},{129,65},{193,1... | collective-permute-start | bytes 337928 | tf_op jit(solution)/shard_map/ppermute | solution.py:44
  7.5 1.2 %collective-permute-start.4 = (bf16[88,640]{1,0:T(8,128)(2,1)S(1)}, bf16[88,640]{1,0:T(8,128)(2,1)S(1)}, u32[]{:S(2)}, u32[]{:S(2)}) collective-permute-start(bf16[88,640]{1,0:T(8,128)(2,1)S(1)} %shard_map.63.refs_0_), channel_id=1, source_target_pairs={{0,2},{2,0},{1,3},{3,1},{4,6},{6,4},{5,7},{7,5},{8,10},{10,8},{9,1... | collective-permute-start | bytes 337928 | tf_op jit(solution)/shard_map/ppermute | solution.py:44
  8.6 2.0 %collective-permute-start.11 = (bf16[88,640]{1,0:T(8,128)(2,1)S(1)}, bf16[88,640]{1,0:T(8,128)(2,1)S(1)}, u32[]{:S(2)}, u32[]{:S(2)}) collective-permute-start(bf16[88,640]{1,0:T(8,128)(2,1)S(1)} %shard_map.63.refs_0_), channel_id=1, source_target_pairs={{0,128},{64,192},{128,0},{192,64},{1,129},{65,193},{129,1},{193,65... | collective-permute-start | bytes 337928 | tf_op jit(solution)/shard_map/ppermute | solution.py:44
  11.3 6.8 %collective-permute-start.2 = (bf16[88,640]{1,0:T(8,128)(2,1)S(1)}, bf16[88,640]{1,0:T(8,128)(2,1)S(1)}, u32[]{:S(2)}, u32[]{:S(2)}) collective-permute-start(bf16[88,640]{1,0:T(8,128)(2,1)S(1)} %shard_map.60.refs_0_), channel_id=1, source_target_pairs={{0,40},{8,48},{16,56},{24,0},{32,8},{40,16},{48,24},{56,32},{1,41}... | collective-permute-start | bytes 337928 | tf_op jit(solution)/shard_map/ppermute | solution.py:49
  18.1 1.7 %collective-permute-start.7 = (bf16[88,640]{1,0:T(8,128)(2,1)S(1)}, bf16[88,640]{1,0:T(8,128)(2,1)S(1)}, u32[]{:S(2)}, u32[]{:S(2)}) collective-permute-start(bf16[88,640]{1,0:T(8,128)(2,1)S(1)} %collective-permute-done.4.refs_9_), channel_id=1, source_target_pairs={{0,192},{64,128},{128,64},{192,0},{1,193},{65,129},{129,65},{193,1... | collective-permute-start | bytes 337928 | tf_op jit(solution)/shard_map/ppermute | solution.py:44
  19.8 1.8 %collective-permute-start.6 = (bf16[88,640]{1,0:T(8,128)(2,1)S(1)}, bf16[88,640]{1,0:T(8,128)(2,1)S(1)}, u32[]{:S(2)}, u32[]{:S(2)}) collective-permute-start(bf16[88,640]{1,0:T(8,128)(2,1)S(1)} %collective-permute-done.4.refs_9_), channel_id=1, source_target_pairs={{0,128},{64,192},{128,0},{192,64},{1,129},{65,193},{129,1},{193,65... | collective-permute-start | bytes 337928 | tf_op jit(solution)/shard_map/ppermute | solution.py:44
  21.6 1.2 %collective-permute-start.5 = (bf16[88,640]{1,0:T(8,128)(2,1)S(1)}, bf16[88,640]{1,0:T(8,128)(2,1)S(1)}, u32[]{:S(2)}, u32[]{:S(2)}) collective-permute-start(bf16[88,640]{1,0:T(8,128)(2,1)S(1)} %collective-permute-done.4.refs_9_), channel_id=1, source_target_pairs={{0,64},{64,0},{128,192},{192,128},{1,65},{65,1},{129,193},{193,129... | collective-permute-start | bytes 337928 | tf_op jit(solution)/shard_map/ppermute | solution.py:44
  22.8 1.7 %collective-permute-done.2.refs_2_ = bf16[88,640]{1,0:T(8,128)(2,1)S(1)} collective-permute-done((bf16[88,640]{1,0:T(8,128)(2,1)S(1)}, bf16[88,640]{1,0:T(8,128)(2,1)S(1)}, u32[]{:S(2)}, u32[]{:S(2)}) %collective-permute-start.2) | collective-permute-done | bytes 112672 | tf_op jit(solution)/shard_map/ppermute | solution.py:49
  24.5 2.1 %collective-permute-start.14 = (bf16[4,88,640]{2,1,0:T(8,128)(2,1)S(1)}, bf16[4,88,640]{2,1,0:T(8,128)(2,1)S(1)}, u32[]{:S(2)}, u32[]{:S(2)}) collective-permute-start(bf16[4,88,640]{2,1,0:T(8,128)(2,1)S(1)} %shard_map.64.refs_6_), channel_id=1, source_target_pairs={{0,6},{2,4},{4,2},{6,0},{1,7},{3,5},{5,3},{7,1},{8,14},{10,12},{12... | collective-permute-start | bytes 1351688 | tf_op jit(solution)/shard_map/ppermute | solution.py:44
  26.6 2.4 %collective-permute-done.1.refs_1_ = bf16[88,640]{1,0:T(8,128)(2,1)S(1)} collective-permute-done((bf16[88,640]{1,0:T(8,128)(2,1)S(1)}, bf16[88,640]{1,0:T(8,128)(2,1)S(1)}, u32[]{:S(2)}, u32[]{:S(2)}) %collective-permute-start.1) | collective-permute-done | bytes 112672 | tf_op jit(solution)/shard_map/ppermute | solution.py:49
  30.6 3.2 %collective-permute-start.9 = (bf16[2,88,640]{2,1,0:T(8,128)(2,1)S(1)}, bf16[2,88,640]{2,1,0:T(8,128)(2,1)S(1)}, u32[]{:S(2)}, u32[]{:S(2)}) collective-permute-start(bf16[2,88,640]{2,1,0:T(8,128)(2,1)S(1)} %shard_map.62), channel_id=1, source_target_pairs={{0,56},{8,0},{16,8},{24,16},{32,24},{40,32},{48,40},{56,48},{1,57}... | collective-permute-start | bytes 675848 | tf_op jit(solution)/shard_map/ppermute | solution.py:49
  33.8 3.9 %collective-permute-done.9.refs_2_ = bf16[2,88,640]{2,1,0:T(8,128)(2,1)S(1)} collective-permute-done((bf16[2,88,640]{2,1,0:T(8,128)(2,1)S(1)}, bf16[2,88,640]{2,1,0:T(8,128)(2,1)S(1)}, u32[]{:S(2)}, u32[]{:S(2)}) %collective-permute-start.9) | collective-permute-done | bytes 225312 | tf_op jit(solution)/shard_map/ppermute | solution.py:49
  37.7 3.1 %collective-permute-done.8.refs_1_ = bf16[3,88,640]{2,1,0:T(8,128)(2,1)S(1)} collective-permute-done((bf16[3,88,640]{2,1,0:T(8,128)(2,1)S(1)}, bf16[3,88,640]{2,1,0:T(8,128)(2,1)S(1)}, u32[]{:S(2)}, u32[]{:S(2)}) %collective-permute-start.8) | collective-permute-done | bytes 337952 | tf_op jit(solution)/shard_map/ppermute | solution.py:49
  44.2 3.5 %shard_map.65 = (f32[8,88,640]{2,1,0:T(8,128)S(1)}, f32[8,88,640]{2,1,0:T(8,128)S(1)}, bf16[768,768]{1,0:T(8,128)(2,1)S(1)}, bf16[768,1280]{1,0:T(8,128)(2,1)S(1)}) custom-call(bf16[3,88,640]{2,1,0:T(8,128)(2,1)S(1)} %shard_map.61.refs_0_, bf16[3,88,640]{2,1,0:T(8,128)(2,1)S(1)} %collective-permute-done.8.refs_1_, ...), custom_call_target="tpu_custom_call" | custom-call | flops 2283798528 | bytes 10354696 | tf_op jit(solution)/shard_map/pallas_call | solution.py:31
  47.9 2.1 %shard_map.67 = (f32[4,88,640]{2,1,0:T(8,128)S(1)}, f32[4,88,640]{2,1,0:T(8,128)S(1)}, f32[4,88,640]{2,1,0:T(8,128)S(1)}, f32[88,640]{1,0:T(8,128)S(1)}, f32[88,...) custom-call(bf16[768,768]{1,0:T(8,128)(2,1)S(1)} %get-tuple-element.72.slope, ...), custom_call_target="tpu_custom_call" | custom-call | flops 1141899264 | bytes 6750208 | tf_op jit(solution)/shard_map/pallas_call | solution.py:31
  50.0 1.5 %collective-permute-done.18.recv = f32[8,88,640]{2,1,0:T(8,128)S(1)} collective-permute-done((f32[8,88,640]{2,1,0:T(8,128)S(1)}, f32[8,88,640]{2,1,0:T(8,128)S(1)}, u32[]{:S(2)}, u32[]{:S(2)}) %collective-permute-start.18) | collective-permute-done | bytes 1802272 | tf_op jit(solution)/shard_map/ppermute | solution.py:44
  52.6 1.5 %collective-permute-start.20 = (f16[2,88,640]{2,1,0:T(8,128)(2,1)S(1)}, f16[2,88,640]{2,1,0:T(8,128)(2,1)S(1)}, u32[]{:S(2)}, u32[]{:S(2)}) collective-permute-start(f16[2,88,640]{2,1,0:T(8,128)(2,1)S(1)} %convert_element_type.80), channel_id=1, source_target_pairs={{0,8},{8,16},{16,24},{24,32},{32,40},{40,48},{48,56},{56,0},{1,9},... | collective-permute-start | bytes 675848 | tf_op jit(solution)/shard_map/ppermute | solution.py:49
  54.2 2.2 %collective-permute-start.24 = (f16[4,88,640]{2,1,0:T(8,128)(2,1)S(1)}, f16[4,88,640]{2,1,0:T(8,128)(2,1)S(1)}, u32[]{:S(2)}, u32[]{:S(2)}) collective-permute-start(f16[4,88,640]{2,1,0:T(8,128)(2,1)S(1)} %convert_element_type.88), channel_id=1, source_target_pairs={{0,6},{2,4},{4,2},{6,0},{1,7},{3,5},{5,3},{7,1},{8,14},{10,12},{12... | collective-permute-start | bytes 1351688 | tf_op jit(solution)/shard_map/ppermute | solution.py:44
  57.1 1.7 %collective-permute-start.28 = (f16[88,640]{1,0:T(8,128)(2,1)S(1)}, f16[88,640]{1,0:T(8,128)(2,1)S(1)}, u32[]{:S(2)}, u32[]{:S(2)}) collective-permute-start(f16[88,640]{1,0:T(8,128)(2,1)S(1)} %convert_element_type.94), channel_id=1, source_target_pairs={{0,192},{64,128},{128,64},{192,0},{1,193},{65,129},{129,65},{193,1... | collective-permute-start | bytes 337928 | tf_op jit(solution)/shard_map/ppermute | solution.py:44
  58.8 2.4 %collective-permute-done.20 = f16[2,88,640]{2,1,0:T(8,128)(2,1)S(1)} collective-permute-done((f16[2,88,640]{2,1,0:T(8,128)(2,1)S(1)}, f16[2,88,640]{2,1,0:T(8,128)(2,1)S(1)}, u32[]{:S(2)}, u32[]{:S(2)}) %collective-permute-start.20) | collective-permute-done | bytes 225312 | tf_op jit(solution)/shard_map/ppermute | solution.py:49
  61.2 1.3 %collective-permute-start.27 = (f16[88,640]{1,0:T(8,128)(2,1)S(1)}, f16[88,640]{1,0:T(8,128)(2,1)S(1)}, u32[]{:S(2)}, u32[]{:S(2)}) collective-permute-start(f16[88,640]{1,0:T(8,128)(2,1)S(1)} %convert_element_type.92), channel_id=1, source_target_pairs={{0,128},{64,192},{128,0},{192,64},{1,129},{65,193},{129,1},{193,65... | collective-permute-start | bytes 337928 | tf_op jit(solution)/shard_map/ppermute | solution.py:44
  62.6 2.4 %collective-permute-start.26 = (f16[88,640]{1,0:T(8,128)(2,1)S(1)}, f16[88,640]{1,0:T(8,128)(2,1)S(1)}, u32[]{:S(2)}, u32[]{:S(2)}) collective-permute-start(f16[88,640]{1,0:T(8,128)(2,1)S(1)} %convert_element_type.90), channel_id=1, source_target_pairs={{0,64},{64,0},{128,192},{192,128},{1,65},{65,1},{129,193},{193,129... | collective-permute-start | bytes 337928 | tf_op jit(solution)/shard_map/ppermute | solution.py:44
  65.6 2.3 %collective-permute-done.27 = f16[88,640]{1,0:T(8,128)(2,1)S(1)} collective-permute-done((f16[88,640]{1,0:T(8,128)(2,1)S(1)}, f16[88,640]{1,0:T(8,128)(2,1)S(1)}, u32[]{:S(2)}, u32[]{:S(2)}) %collective-permute-start.27) | collective-permute-done | bytes 112672 | tf_op jit(solution)/shard_map/ppermute | solution.py:44
  67.9 2.7 %collective-permute-start.21 = (f16[88,640]{1,0:T(8,128)(2,1)S(1)}, f16[88,640]{1,0:T(8,128)(2,1)S(1)}, u32[]{:S(2)}, u32[]{:S(2)}) collective-permute-start(f16[88,640]{1,0:T(8,128)(2,1)S(1)} %convert_element_type.82), channel_id=1, source_target_pairs={{0,40},{8,48},{16,56},{24,0},{32,8},{40,16},{48,24},{56,32},{1,41}... | collective-permute-start | bytes 337928 | tf_op jit(solution)/shard_map/ppermute | solution.py:49
  71.0 3.0 %collective-permute-start.29 = (f16[88,640]{1,0:T(8,128)(2,1)S(1)}, f16[88,640]{1,0:T(8,128)(2,1)S(1)}, u32[]{:S(2)}, u32[]{:S(2)}) collective-permute-start(f16[88,640]{1,0:T(8,128)(2,1)S(1)} %convert_element_type.96), channel_id=1, source_target_pairs={{0,2},{2,0},{1,3},{3,1},{4,6},{6,4},{5,7},{7,5},{8,10},{10,8},{9,1... | collective-permute-start | bytes 337928 | tf_op jit(solution)/shard_map/ppermute | solution.py:44
  74.1 1.5 %collective-permute-done.22 = f16[88,640]{1,0:T(8,128)(2,1)S(1)} collective-permute-done((f16[88,640]{1,0:T(8,128)(2,1)S(1)}, f16[88,640]{1,0:T(8,128)(2,1)S(1)}, u32[]{:S(2)}, u32[]{:S(2)}) %collective-permute-start.22) | collective-permute-done | bytes 112672 | tf_op jit(solution)/shard_map/ppermute | solution.py:49
  76.3 3.2 %collective-permute-start.32 = (f16[88,640]{1,0:T(8,128)(2,1)S(1)}, f16[88,640]{1,0:T(8,128)(2,1)S(1)}, u32[]{:S(2)}, u32[]{:S(2)}) collective-permute-start(f16[88,640]{1,0:T(8,128)(2,1)S(1)} %convert_element_type.102), channel_id=1, source_target_pairs={{0,192},{64,128},{128,64},{192,0},{1,193},{65,129},{129,65},{193,1... | collective-permute-start | bytes 337928 | tf_op jit(solution)/shard_map/ppermute | solution.py:44
  79.5 1.2 %collective-permute-start.31 = (f16[88,640]{1,0:T(8,128)(2,1)S(1)}, f16[88,640]{1,0:T(8,128)(2,1)S(1)}, u32[]{:S(2)}, u32[]{:S(2)}) collective-permute-start(f16[88,640]{1,0:T(8,128)(2,1)S(1)} %convert_element_type.100), channel_id=1, source_target_pairs={{0,128},{64,192},{128,0},{192,64},{1,129},{65,193},{129,1},{193,65... | collective-permute-start | bytes 337928 | tf_op jit(solution)/shard_map/ppermute | solution.py:44
  82.0 2.1 %collective-permute-start.25 = (f32[88,384]{1,0:T(8,128)S(1)}, f32[88,384]{1,0:T(8,128)S(1)}, u32[]{:S(2)}, u32[]{:S(2)}) collective-permute-start(f32[88,384]{1,0:T(8,128)S(1)} %get-tuple-element.86), channel_id=1, source_target_pairs={{0,2},{2,0},{1,3},{3,1},{4,6},{6,4},{5,7},{7,5},{8,10},{10,8},{9,1... | collective-permute-start | bytes 405512 | tf_op jit(solution)/shard_map/ppermute | solution.py:44
  84.1 1.6 %collective-permute-done.31 = f16[88,640]{1,0:T(8,128)(2,1)S(1)} collective-permute-done((f16[88,640]{1,0:T(8,128)(2,1)S(1)}, f16[88,640]{1,0:T(8,128)(2,1)S(1)}, u32[]{:S(2)}, u32[]{:S(2)}) %collective-permute-start.31) | collective-permute-done | bytes 112672 | tf_op jit(solution)/shard_map/ppermute | solution.py:44
  86.2 2.4 %collective-permute-done.25.image_recv = f32[88,384]{1,0:T(8,128)S(1)} collective-permute-done((f32[88,384]{1,0:T(8,128)S(1)}, f32[88,384]{1,0:T(8,128)S(1)}, u32[]{:S(2)}, u32[]{:S(2)}) %collective-permute-start.25) | collective-permute-done | bytes 135200 | tf_op jit(solution)/shard_map/ppermute | solution.py:44
  (85 shorter events, 12.6 us)
Async XLA Ops:
  2.5 3.2 %collective-permute-start.3 = (bf16[88,288]{1,0:T(8,128)(2,1)S(1)}, bf16[88,288]{1,0:T(8,128)(2,1)S(1)}, u32[]{:S(2)}, u32[]{:S(2)}) collective-permute-start(bf16[88,288]{1,0:T(8,128)(2,1)S(1)} %get-tuple-element.54), channel_id=1, source_target_pairs={{0,1},{1,0},{2,3},{3,2},{4,5},{5,4},{6,7},{7,6},{8,9},{9,8},{10,11... | collective-permute-start | bytes 152072 | tf_op jit(solution)/shard_map/ppermute | solution.py:44
  2.6 8.5 %collective-permute-start = (bf16[96,640]{1,0:T(8,128)(2,1)S(1)}, bf16[96,640]{1,0:T(8,128)(2,1)S(1)}, u32[]{:S(2)}, u32[]{:S(2)}) collective-permute-start(bf16[96,640]{1,0:T(8,128)(2,1)S(1)} %get-tuple-element.52), channel_id=1, source_target_pairs={{0,2},{2,0},{1,3},{3,1},{4,6},{6,4},{5,7},{7,5},{8,10},{10,8},{9,1... | collective-permute-start | bytes 368648 | tf_op jit(solution)/shard_map/ppermute | solution.py:44
  5.8 12.3 %collective-permute-start.12 = (bf16[88,640]{1,0:T(8,128)(2,1)S(1)}, bf16[88,640]{1,0:T(8,128)(2,1)S(1)}, u32[]{:S(2)}, u32[]{:S(2)}) collective-permute-start(bf16[88,640]{1,0:T(8,128)(2,1)S(1)} %shard_map.63.refs_0_), channel_id=1, source_target_pairs={{0,192},{64,128},{128,64},{192,0},{1,193},{65,129},{129,65},{193,1... | collective-permute-start | bytes 337928 | tf_op jit(solution)/shard_map/ppermute | solution.py:44
  7.5 10.6 %collective-permute-start.4 = (bf16[88,640]{1,0:T(8,128)(2,1)S(1)}, bf16[88,640]{1,0:T(8,128)(2,1)S(1)}, u32[]{:S(2)}, u32[]{:S(2)}) collective-permute-start(bf16[88,640]{1,0:T(8,128)(2,1)S(1)} %shard_map.63.refs_0_), channel_id=1, source_target_pairs={{0,2},{2,0},{1,3},{3,1},{4,6},{6,4},{5,7},{7,5},{8,10},{10,8},{9,1... | collective-permute-start | bytes 337928 | tf_op jit(solution)/shard_map/ppermute | solution.py:44
  8.6 11.1 %collective-permute-start.11 = (bf16[88,640]{1,0:T(8,128)(2,1)S(1)}, bf16[88,640]{1,0:T(8,128)(2,1)S(1)}, u32[]{:S(2)}, u32[]{:S(2)}) collective-permute-start(bf16[88,640]{1,0:T(8,128)(2,1)S(1)} %shard_map.63.refs_0_), channel_id=1, source_target_pairs={{0,128},{64,192},{128,0},{192,64},{1,129},{65,193},{129,1},{193,65... | collective-permute-start | bytes 337928 | tf_op jit(solution)/shard_map/ppermute | solution.py:44
  10.7 10.9 %collective-permute-start.10 = (bf16[88,640]{1,0:T(8,128)(2,1)S(1)}, bf16[88,640]{1,0:T(8,128)(2,1)S(1)}, u32[]{:S(2)}, u32[]{:S(2)}) collective-permute-start(bf16[88,640]{1,0:T(8,128)(2,1)S(1)} %shard_map.63.refs_0_), channel_id=1, source_target_pairs={{0,64},{64,0},{128,192},{192,128},{1,65},{65,1},{129,193},{193,129... | collective-permute-start | bytes 337928 | tf_op jit(solution)/shard_map/ppermute | solution.py:44
  11.3 13.2 %collective-permute-start.2 = (bf16[88,640]{1,0:T(8,128)(2,1)S(1)}, bf16[88,640]{1,0:T(8,128)(2,1)S(1)}, u32[]{:S(2)}, u32[]{:S(2)}) collective-permute-start(bf16[88,640]{1,0:T(8,128)(2,1)S(1)} %shard_map.60.refs_0_), channel_id=1, source_target_pairs={{0,40},{8,48},{16,56},{24,0},{32,8},{40,16},{48,24},{56,32},{1,41}... | collective-permute-start | bytes 337928 | tf_op jit(solution)/shard_map/ppermute | solution.py:49
  18.1 10.9 %collective-permute-start.1 = (bf16[88,640]{1,0:T(8,128)(2,1)S(1)}, bf16[88,640]{1,0:T(8,128)(2,1)S(1)}, u32[]{:S(2)}, u32[]{:S(2)}) collective-permute-start(bf16[88,640]{1,0:T(8,128)(2,1)S(1)} %shard_map.60.refs_0_), channel_id=1, source_target_pairs={{0,24},{8,32},{16,40},{24,48},{32,56},{40,0},{48,8},{56,16},{1,25}... | collective-permute-start | bytes 337928 | tf_op jit(solution)/shard_map/ppermute | solution.py:49
  18.1 11.8 %collective-permute-start.7 = (bf16[88,640]{1,0:T(8,128)(2,1)S(1)}, bf16[88,640]{1,0:T(8,128)(2,1)S(1)}, u32[]{:S(2)}, u32[]{:S(2)}) collective-permute-start(bf16[88,640]{1,0:T(8,128)(2,1)S(1)} %collective-permute-done.4.refs_9_), channel_id=1, source_target_pairs={{0,192},{64,128},{128,64},{192,0},{1,193},{65,129},{129,65},{193,1... | collective-permute-start | bytes 337928 | tf_op jit(solution)/shard_map/ppermute | solution.py:44
  19.8 10.2 %collective-permute-start.6 = (bf16[88,640]{1,0:T(8,128)(2,1)S(1)}, bf16[88,640]{1,0:T(8,128)(2,1)S(1)}, u32[]{:S(2)}, u32[]{:S(2)}) collective-permute-start(bf16[88,640]{1,0:T(8,128)(2,1)S(1)} %collective-permute-done.4.refs_9_), channel_id=1, source_target_pairs={{0,128},{64,192},{128,0},{192,64},{1,129},{65,193},{129,1},{193,65... | collective-permute-start | bytes 337928 | tf_op jit(solution)/shard_map/ppermute | solution.py:44
  21.6 8.3 %collective-permute-start.5 = (bf16[88,640]{1,0:T(8,128)(2,1)S(1)}, bf16[88,640]{1,0:T(8,128)(2,1)S(1)}, u32[]{:S(2)}, u32[]{:S(2)}) collective-permute-start(bf16[88,640]{1,0:T(8,128)(2,1)S(1)} %collective-permute-done.4.refs_9_), channel_id=1, source_target_pairs={{0,64},{64,0},{128,192},{192,128},{1,65},{65,1},{129,193},{193,129... | collective-permute-start | bytes 337928 | tf_op jit(solution)/shard_map/ppermute | solution.py:44
  24.5 16.4 %collective-permute-start.14 = (bf16[4,88,640]{2,1,0:T(8,128)(2,1)S(1)}, bf16[4,88,640]{2,1,0:T(8,128)(2,1)S(1)}, u32[]{:S(2)}, u32[]{:S(2)}) collective-permute-start(bf16[4,88,640]{2,1,0:T(8,128)(2,1)S(1)} %shard_map.64.refs_6_), channel_id=1, source_target_pairs={{0,6},{2,4},{4,2},{6,0},{1,7},{3,5},{5,3},{7,1},{8,14},{10,12},{12... | collective-permute-start | bytes 1351688 | tf_op jit(solution)/shard_map/ppermute | solution.py:44
  29.0 11.8 %collective-permute-start.13 = (bf16[4,88,640]{2,1,0:T(8,128)(2,1)S(1)}, bf16[4,88,640]{2,1,0:T(8,128)(2,1)S(1)}, u32[]{:S(2)}, u32[]{:S(2)}) collective-permute-start(bf16[4,88,640]{2,1,0:T(8,128)(2,1)S(1)} %shard_map.64.refs_6_), channel_id=1, source_target_pairs={{0,4},{2,6},{4,0},{6,2},{1,5},{3,7},{5,1},{7,3},{8,12},{10,14},{12... | collective-permute-start | bytes 1351688 | tf_op jit(solution)/shard_map/ppermute | solution.py:44
  30.6 10.2 %collective-permute-start.8 = (bf16[3,88,640]{2,1,0:T(8,128)(2,1)S(1)}, bf16[3,88,640]{2,1,0:T(8,128)(2,1)S(1)}, u32[]{:S(2)}, u32[]{:S(2)}) collective-permute-start(bf16[3,88,640]{2,1,0:T(8,128)(2,1)S(1)} %shard_map.61.refs_0_), channel_id=1, source_target_pairs={{0,8},{8,16},{16,24},{24,32},{32,40},{40,48},{48,56},{56,0},{1,9},... | collective-permute-start | bytes 1013768 | tf_op jit(solution)/shard_map/ppermute | solution.py:49
  30.6 7.1 %collective-permute-start.9 = (bf16[2,88,640]{2,1,0:T(8,128)(2,1)S(1)}, bf16[2,88,640]{2,1,0:T(8,128)(2,1)S(1)}, u32[]{:S(2)}, u32[]{:S(2)}) collective-permute-start(bf16[2,88,640]{2,1,0:T(8,128)(2,1)S(1)} %shard_map.62), channel_id=1, source_target_pairs={{0,56},{8,0},{16,8},{24,16},{32,24},{40,32},{48,40},{56,48},{1,57}... | collective-permute-start | bytes 675848 | tf_op jit(solution)/shard_map/ppermute | solution.py:49
  40.8 2.5 %collective-permute-start.15 = (bf16[3,88,640]{2,1,0:T(8,128)(2,1)S(1)}, bf16[3,88,640]{2,1,0:T(8,128)(2,1)S(1)}, u32[]{:S(2)}, u32[]{:S(2)}) collective-permute-start(bf16[3,88,640]{2,1,0:T(8,128)(2,1)S(1)} %shard_map.61.refs_0_), channel_id=1, source_target_pairs={{0,1},{1,0},{2,3},{3,2},{4,5},{5,4},{6,7},{7,6},{8,9},{9,8},{10,11... | collective-permute-start | bytes 1013768 | tf_op jit(solution)/shard_map/ppermute | solution.py:44
  47.7 3.8 %collective-permute-start.18 = (f32[8,88,640]{2,1,0:T(8,128)S(1)}, f32[8,88,640]{2,1,0:T(8,128)S(1)}, u32[]{:S(2)}, u32[]{:S(2)}) collective-permute-start(f32[8,88,640]{2,1,0:T(8,128)S(1)} %get-tuple-element.68), channel_id=1, source_target_pairs={{0,1},{1,0},{2,3},{3,2},{4,5},{5,4},{6,7},{7,6},{8,9},{9,8},{10,11... | collective-permute-start | bytes 5406728 | tf_op jit(solution)/shard_map/ppermute | solution.py:44
  51.9 10.7 %collective-permute-start.19 = (f16[3,88,640]{2,1,0:T(8,128)(2,1)S(1)}, f16[3,88,640]{2,1,0:T(8,128)(2,1)S(1)}, u32[]{:S(2)}, u32[]{:S(2)}) collective-permute-start(f16[3,88,640]{2,1,0:T(8,128)(2,1)S(1)} %convert_element_type.78), channel_id=1, source_target_pairs={{0,56},{8,0},{16,8},{24,16},{32,24},{40,32},{48,40},{56,48},{1,57}... | collective-permute-start | bytes 1013768 | tf_op jit(solution)/shard_map/ppermute | solution.py:49
  52.6 8.6 %collective-permute-start.20 = (f16[2,88,640]{2,1,0:T(8,128)(2,1)S(1)}, f16[2,88,640]{2,1,0:T(8,128)(2,1)S(1)}, u32[]{:S(2)}, u32[]{:S(2)}) collective-permute-start(f16[2,88,640]{2,1,0:T(8,128)(2,1)S(1)} %convert_element_type.80), channel_id=1, source_target_pairs={{0,8},{8,16},{16,24},{24,32},{32,40},{40,48},{48,56},{56,0},{1,9},... | collective-permute-start | bytes 675848 | tf_op jit(solution)/shard_map/ppermute | solution.py:49
  54.2 21.5 %collective-permute-start.24 = (f16[4,88,640]{2,1,0:T(8,128)(2,1)S(1)}, f16[4,88,640]{2,1,0:T(8,128)(2,1)S(1)}, u32[]{:S(2)}, u32[]{:S(2)}) collective-permute-start(f16[4,88,640]{2,1,0:T(8,128)(2,1)S(1)} %convert_element_type.88), channel_id=1, source_target_pairs={{0,6},{2,4},{4,2},{6,0},{1,7},{3,5},{5,3},{7,1},{8,14},{10,12},{12... | collective-permute-start | bytes 1351688 | tf_op jit(solution)/shard_map/ppermute | solution.py:44
  56.4 19.3 %collective-permute-start.23 = (f16[4,88,640]{2,1,0:T(8,128)(2,1)S(1)}, f16[4,88,640]{2,1,0:T(8,128)(2,1)S(1)}, u32[]{:S(2)}, u32[]{:S(2)}) collective-permute-start(f16[4,88,640]{2,1,0:T(8,128)(2,1)S(1)} %convert_element_type.86), channel_id=1, source_target_pairs={{0,4},{2,6},{4,0},{6,2},{1,5},{3,7},{5,1},{7,3},{8,12},{10,14},{12... | collective-permute-start | bytes 1351688 | tf_op jit(solution)/shard_map/ppermute | solution.py:44
  57.1 8.4 %collective-permute-start.28 = (f16[88,640]{1,0:T(8,128)(2,1)S(1)}, f16[88,640]{1,0:T(8,128)(2,1)S(1)}, u32[]{:S(2)}, u32[]{:S(2)}) collective-permute-start(f16[88,640]{1,0:T(8,128)(2,1)S(1)} %convert_element_type.94), channel_id=1, source_target_pairs={{0,192},{64,128},{128,64},{192,0},{1,193},{65,129},{129,65},{193,1... | collective-permute-start | bytes 337928 | tf_op jit(solution)/shard_map/ppermute | solution.py:44
  61.2 6.7 %collective-permute-start.27 = (f16[88,640]{1,0:T(8,128)(2,1)S(1)}, f16[88,640]{1,0:T(8,128)(2,1)S(1)}, u32[]{:S(2)}, u32[]{:S(2)}) collective-permute-start(f16[88,640]{1,0:T(8,128)(2,1)S(1)} %convert_element_type.92), channel_id=1, source_target_pairs={{0,128},{64,192},{128,0},{192,64},{1,129},{65,193},{129,1},{193,65... | collective-permute-start | bytes 337928 | tf_op jit(solution)/shard_map/ppermute | solution.py:44
  62.6 8.1 %collective-permute-start.26 = (f16[88,640]{1,0:T(8,128)(2,1)S(1)}, f16[88,640]{1,0:T(8,128)(2,1)S(1)}, u32[]{:S(2)}, u32[]{:S(2)}) collective-permute-start(f16[88,640]{1,0:T(8,128)(2,1)S(1)} %convert_element_type.90), channel_id=1, source_target_pairs={{0,64},{64,0},{128,192},{192,128},{1,65},{65,1},{129,193},{193,129... | collective-permute-start | bytes 337928 | tf_op jit(solution)/shard_map/ppermute | solution.py:44
  65.5 10.1 %collective-permute-start.22 = (f16[88,640]{1,0:T(8,128)(2,1)S(1)}, f16[88,640]{1,0:T(8,128)(2,1)S(1)}, u32[]{:S(2)}, u32[]{:S(2)}) collective-permute-start(f16[88,640]{1,0:T(8,128)(2,1)S(1)} %convert_element_type.84), channel_id=1, source_target_pairs={{0,24},{8,32},{16,40},{24,48},{32,56},{40,0},{48,8},{56,16},{1,25}... | collective-permute-start | bytes 337928 | tf_op jit(solution)/shard_map/ppermute | solution.py:49
  67.9 7.7 %collective-permute-start.21 = (f16[88,640]{1,0:T(8,128)(2,1)S(1)}, f16[88,640]{1,0:T(8,128)(2,1)S(1)}, u32[]{:S(2)}, u32[]{:S(2)}) collective-permute-start(f16[88,640]{1,0:T(8,128)(2,1)S(1)} %convert_element_type.82), channel_id=1, source_target_pairs={{0,40},{8,48},{16,56},{24,0},{32,8},{40,16},{48,24},{56,32},{1,41}... | collective-permute-start | bytes 337928 | tf_op jit(solution)/shard_map/ppermute | solution.py:49
  71.0 10.7 %collective-permute-start.29 = (f16[88,640]{1,0:T(8,128)(2,1)S(1)}, f16[88,640]{1,0:T(8,128)(2,1)S(1)}, u32[]{:S(2)}, u32[]{:S(2)}) collective-permute-start(f16[88,640]{1,0:T(8,128)(2,1)S(1)} %convert_element_type.96), channel_id=1, source_target_pairs={{0,2},{2,0},{1,3},{3,1},{4,6},{6,4},{5,7},{7,5},{8,10},{10,8},{9,1... | collective-permute-start | bytes 337928 | tf_op jit(solution)/shard_map/ppermute | solution.py:44
  76.3 7.8 %collective-permute-start.32 = (f16[88,640]{1,0:T(8,128)(2,1)S(1)}, f16[88,640]{1,0:T(8,128)(2,1)S(1)}, u32[]{:S(2)}, u32[]{:S(2)}) collective-permute-start(f16[88,640]{1,0:T(8,128)(2,1)S(1)} %convert_element_type.102), channel_id=1, source_target_pairs={{0,192},{64,128},{128,64},{192,0},{1,193},{65,129},{129,65},{193,1... | collective-permute-start | bytes 337928 | tf_op jit(solution)/shard_map/ppermute | solution.py:44
  79.5 6.3 %collective-permute-start.31 = (f16[88,640]{1,0:T(8,128)(2,1)S(1)}, f16[88,640]{1,0:T(8,128)(2,1)S(1)}, u32[]{:S(2)}, u32[]{:S(2)}) collective-permute-start(f16[88,640]{1,0:T(8,128)(2,1)S(1)} %convert_element_type.100), channel_id=1, source_target_pairs={{0,128},{64,192},{128,0},{192,64},{1,129},{65,193},{129,1},{193,65... | collective-permute-start | bytes 337928 | tf_op jit(solution)/shard_map/ppermute | solution.py:44
  80.7 5.1 %collective-permute-start.30 = (f16[88,640]{1,0:T(8,128)(2,1)S(1)}, f16[88,640]{1,0:T(8,128)(2,1)S(1)}, u32[]{:S(2)}, u32[]{:S(2)}) collective-permute-start(f16[88,640]{1,0:T(8,128)(2,1)S(1)} %convert_element_type.98), channel_id=1, source_target_pairs={{0,64},{64,0},{128,192},{192,128},{1,65},{65,1},{129,193},{193,129... | collective-permute-start | bytes 337928 | tf_op jit(solution)/shard_map/ppermute | solution.py:44
  82.0 6.6 %collective-permute-start.25 = (f32[88,384]{1,0:T(8,128)S(1)}, f32[88,384]{1,0:T(8,128)S(1)}, u32[]{:S(2)}, u32[]{:S(2)}) collective-permute-start(f32[88,384]{1,0:T(8,128)S(1)} %get-tuple-element.86), channel_id=1, source_target_pairs={{0,2},{2,0},{1,3},{3,1},{4,6},{6,4},{5,7},{7,5},{8,10},{10,8},{9,1... | collective-permute-start | bytes 405512 | tf_op jit(solution)/shard_map/ppermute | solution.py:44
  86.1 2.5 %collective-permute-start.33 = (f32[88,384]{1,0:T(8,128)S(1)}, f32[88,384]{1,0:T(8,128)S(1)}, u32[]{:S(2)}, u32[]{:S(2)}) collective-permute-start(f32[88,384]{1,0:T(8,128)S(1)} %get-tuple-element.99), channel_id=1, source_target_pairs={{0,1},{1,0},{2,3},{3,2},{4,5},{5,4},{6,7},{7,6},{8,9},{9,8},{10,11... | collective-permute-start | bytes 405512 | tf_op jit(solution)/shard_map/ppermute | solution.py:44
  (6 other events, 7.7 us)

commit v4 on v3

--- a/solution.py
+++ b/solution.py
@@ -13,6 +13,7 @@
 QUART = 288
 HALF = 576
 WIDE = 640
+CODED = 577
 X = ("l", "h")
 F32 = jnp.float32
 BF16 = jnp.bfloat16
@@ -91,17 +92,16 @@
 
 
 def slope_kernel(*refs):
-    halves, text, across = (refs[0:3], refs[3:6]), refs[6:9], refs[9:13]
-    scale_ref, bias_ref = refs[13:15]
-    keep, send, slope, images = refs[15:19]
-    texts = refs[19]
+    halves, text, across = (refs[0:3], refs[3:6]), refs[6:9], refs[9]
+    scale_ref, bias_ref = refs[10:12]
+    send, slope, images, texts = refs[12:16]
     scale, bias = scale_ref[0], bias_ref[0]
     zeros = jnp.zeros((ROWS, WIDE - HALF), BF16)
     for s in range(8):
         rows = pl.ds(SLOT * s, ROWS)
         for half, parts in enumerate(halves):
             images[rows, WIDE * half : WIDE * (half + 1)] = parts[s // 3][s % 3]
-        a, b = (text[0][s], across[s][...]) if s < 4 else (text[1][s - 4], text[2][s - 4])
+        a, b = (text[0][s], across[s]) if s < 4 else (text[1][s - 4], text[2][s - 4])
         texts[rows, 0:WIDE] = jnp.concatenate([a[:, :QUART], b[:, :QUART], zeros], axis=1)
         texts[rows, WIDE:] = jnp.concatenate([a[:, QUART:HALF], b[:, QUART:HALF], zeros], axis=1)
         rows = pl.ds(SLOT * s + ROWS, SLOT - ROWS)
@@ -123,17 +123,21 @@
             top = jnp.where(paired, -jax.nn.sigmoid(-top), value[:SLOT])
             value = jnp.concatenate([top, value[SLOT:]], axis=0)
         slope[:, cols] = value.astype(BF16)
-    add = jnp.dot(slope[...], texts[...], preferred_element_type=F32)
-    for s in range(8):
-        keep[s] = add[SLOT * s : SLOT * s + ROWS, :WIDE]
-        send[s] = add[SLOT * s : SLOT * s + ROWS, WIDE:]
-
-
-def text_kernel(slope, images, own, two, three, *across):
+    image_terms(slope, texts, 1, send)
+
+
+def image_terms(slope, texts, half, out):
+    add = jnp.dot(slope[...], texts[:, WIDE * half : WIDE * (half + 1)], preferred_element_type=F32)
+    for s in range(8):
+        out[s] = add[SLOT * s : SLOT * s + ROWS, :]
+
+
+def text_kernel(slope, images, texts, keep, own, two, three, *across):
+    image_terms(slope, texts, 0, keep)
     total = lax.dot_general(
         slope[...], images[...], (((0,), (0,)), ((), ())), preferred_element_type=F32
     )
-    pad = jnp.zeros((ROWS, WIDE - HALF), F32)
+    pad = jnp.zeros((ROWS, CODED - HALF), F32)
     for s in range(8):
         x = total[SLOT * s : SLOT * s + ROWS, :]
         for d in range(2):
@@ -183,7 +187,8 @@
     x = scale[0] * x
     keep[...] = x[:, :QUART]
     send[:, :QUART] = x[:, QUART:HALF]
-    send[:, QUART:] = jnp.zeros((ROWS, send.shape[1] - QUART), F32)
+    if send.shape[1] > QUART:
+        send[:, QUART:] = jnp.zeros((ROWS, send.shape[1] - QUART), F32)
 
 
 def place_kernel(image_keep, image_recv, text_keep, text_recv, image_out, text_out):
@@ -217,30 +222,31 @@
     other = [other] + [flip(other, "y", n) for n in (1, 2, 3)]
     texts = [four] + [flip(four, X, n) for n in (2, 3)]
     near = image, behind(image, "z", 3), behind(image, "z", -3)
-    trio, duo, *other = together(stacked(*near), stacked(*near[:2]), *other)
+    trio, duo, other = together(stacked(*near), stacked(*near[:2]), stacked(*other))
     images = [trio, behind(trio, "z", 1), behind(duo, "z", -1)]
     *images, t0, t1, t2 = together(*images, *texts)
-    texts = [t0, t1, t2, *other]
+    texts = [t0, t1, t2, other]
     swapped = [flip(x, "c", 1) for x in images]
 
-    big, quad, three, one = (shape((*d, ROWS, WIDE), F32) for d in ((8,), (4,), (3,), ()))
+    big, three, one = (shape((*d, ROWS, WIDE), F32) for d in ((8,), (3,), ()))
+    quad, coded = shape((4, ROWS, CODED), F32), shape((ROWS, CODED), F32)
     two = shape((2, ROWS, WIDE), F32)
-    keep, send, slope, images = call(
+    joined = shape((8 * SLOT, 2 * WIDE), BF16)
+    send, slope, images, texts = call(
         slope_kernel,
-        [big, big, shape((8 * SLOT, 8 * SLOT), BF16), shape((8 * SLOT, 2 * WIDE), BF16)],
+        [big, shape((8 * SLOT, 8 * SLOT), BF16), joined, joined],
         *images,
         *swapped,
         *texts,
         scale,
         bias,
         smem=2,
-        scratch=[pltpu.VMEM((8 * SLOT, 2 * WIDE), BF16)],
-        flops=4 * 704 * 704 * 1152,
-        mib=16,
+        flops=3 * 704 * 704 * 1152,
+        mib=12,
     )
     recv = flip(send, "c", 1)
-    text_own, *text_out = call(
-        text_kernel, [quad] * 3 + [one] * 4, slope, images, flops=2 * 704 * 704 * 1152, mib=12
+    keep, text_own, *text_out = call(
+        text_kernel, [big] + [quad] * 3 + [coded] * 4, slope, images, texts, flops=3 * 704 * 704 * 1152, mib=12
     )
     text_out, text_across, *across_out = text_out[:2], *text_out[2:]
     image_own, below, above = call(image_first_kernel, [three, three, two], keep, recv, mib=12)
@@ -252,18 +258,17 @@
     across_in = [moved(x, flip, "y", n) for n, x in enumerate(across_out, 1)]
     text_in = [moved(x, flip, X, n) for n, x in zip((2, 3), text_out)]
     image_in = [moved(below, behind, "z", -1), moved(above, behind, "z", 1)]
-    (across,) = call(text_across_kernel, [one], text_across, *across_in, mib=4)
+    (across,) = call(text_across_kernel, [coded], text_across, *across_in, mib=4)
     across = moved(across, flip, "h", 1)
     image_own, below, above = call(image_sum_kernel, [one] * 3, image_own, *image_in, mib=8)
     below, above = moved(below, behind, "z", -3), moved(above, behind, "z", 3)
-    below, above, *text_in = together(below, above, *text_in)
-    text_own, *text_out = call(text_sum_kernel, [one] * 4, text_own, *text_in, mib=12)
+    text_own, *text_out = call(text_sum_kernel, [coded] * 4, text_own, *text_in, mib=12)
     text_in = [across] + [moved(x, flip, "y", n) for n, x in enumerate(text_out, 1)]
     image_in = [below, above]
-    part = [shape((ROWS, n), F32) for n in (QUART, 384)]
-    image_keep, image_send = call(last_kernel, part, image_own, *image_in, scale, smem=1, mib=4)
+    part, wider = shape((ROWS, QUART), F32), shape((ROWS, 512), F32)
+    image_keep, image_send = call(last_kernel, [part, wider], image_own, *image_in, scale, smem=1, mib=4)
     image_recv = flip(image_send, "h", 1)
-    text_keep, text_send = call(last_kernel, part, text_own, *text_in, scale, smem=1, mib=4)
+    text_keep, text_send = call(last_kernel, [part, part], text_own, *text_in, scale, smem=1, mib=4)
     text_recv = flip(text_send, "c", 1)
     grads = [shape((2 * ROWS, QUART), F32)] * 2
     return tuple(call(place_kernel, grads, image_keep, image_recv, text_keep, text_recv, mib=4))

time: 90.7 us -> 86.5 us (0.954); the launches traced: 89.5 us -> 86.3 us
  starting transfers between devices: 50.9 us -> 48 us
  local copies, waits for them, and re-layouts: 3.34 us -> 1.8 us
  Pallas kernels: 8.64 us -> 9.86 us
    ppermute x26, starting transfers between devices: 35.9 us -> 31.2 us  [flip(): return lax.ppermute(x, axis, [(i, i ^ mask) for i in range(count)])]
    ppermute x8, starting transfers between devices: 15 us -> 16.8 us  [behind(): lax.ppermute(x, axis, [(i, (i + distance) % count) for i in range(count)])]
    ppermute x26, waiting for transfers between devices: 8.54 us -> 10.1 us  [flip(): return lax.ppermute(x, axis, [(i, i ^ mask) for i in range(count)])]
    unnamed x8 -> x4, local copies, waits for them, and re-layouts: 3.34 us -> 1.8 us
    ppermute x8, waiting for transfers between devices: 15 us -> 13.6 us  [behind(): lax.ppermute(x, axis, [(i, (i + distance) % count) for i in range(count)])]
    pallas_call x15 -> x16, Pallas kernels: 8.64 us -> 9.86 us  [call(): pl.pallas_call(kernel, out_shape=outs, in_specs=specs, out_specs=[VMEM] *...]
  transfers between devices with their start and end apart: 34 -> 34, of which waited for: 11 -> 13; matrix products, arithmetic and copies ran while one was open for 1% -> 1% of each run, Pallas kernels for 4% -> 6%
where the time goes in v4:
time: 86.5 us; the launch traced here: 86.3 us
  starting transfers between devices  48 us (55%)
  waiting for transfers between devices  23.7 us (27%)
  Pallas kernels  9.86 us (11%)
  between operations  2.32 us (3%)
  local copies, waits for them, and re-layouts  1.8 us (2%)
    ppermute x26, starting transfers between devices, flip(): return lax.ppermute(x, axis, [(i, i ^ mask) for i in range(count)])  31.2 us
    ppermute x8, starting transfers between devices, behind(): lax.ppermute(x, axis, [(i, (i + distance) % count) for i in range(count)])  16.8 us
    ppermute x8, waiting for transfers between devices, behind(): lax.ppermute(x, axis, [(i, (i + distance) % count) for i in range(count)])  13.6 us
    ppermute x26, waiting for transfers between devices, flip(): return lax.ppermute(x, axis, [(i, i ^ mask) for i in range(count)])  10.1 us
    pallas_call x16, Pallas kernels, call(): pl.pallas_call(kernel, out_shape=outs, in_specs=specs, out_specs=[VMEM] *...  9.86 us
    unnamed x4, local copies, waits for them, and re-layouts  1.8 us
  transfers between devices with their start and end apart: 34, of which 13 were waited for; matrix products, arithmetic and copies ran while one was open for 1% of the time, Pallas kernels for 6%

profile of v4, /device:TPU:8, one launch (start us, length us, event | category | flops | bytes accessed | tf_op | source)
XLA Modules:
  0.0 86.3 jit_solution(5997953704414733965)
XLA Ops:
  2.6 3.1 %collective-permute-start = (bf16[96,640]{1,0:T(8,128)(2,1)S(1)}, bf16[96,640]{1,0:T(8,128)(2,1)S(1)}, u32[]{:S(2)}, u32[]{:S(2)}) collective-permute-start(bf16[96,640]{1,0:T(8,128)(2,1)S(1)} %get-tuple-element.46), channel_id=1, source_target_pairs={{0,2},{2,0},{1,3},{3,1},{4,6},{6,4},{5,7},{7,5},{8,10},{10,8},{9,1... | collective-permute-start | bytes 368648 | tf_op jit(solution)/shard_map/ppermute | solution.py:45
  5.8 1.7 %collective-permute-start.12 = (bf16[88,640]{1,0:T(8,128)(2,1)S(1)}, bf16[88,640]{1,0:T(8,128)(2,1)S(1)}, u32[]{:S(2)}, u32[]{:S(2)}) collective-permute-start(bf16[88,640]{1,0:T(8,128)(2,1)S(1)} %shard_map.63.refs_0_), channel_id=1, source_target_pairs={{0,192},{64,128},{128,64},{192,0},{1,193},{65,129},{129,65},{193,1... | collective-permute-start | bytes 337928 | tf_op jit(solution)/shard_map/ppermute | solution.py:45
  7.5 1.2 %collective-permute-start.4 = (bf16[88,640]{1,0:T(8,128)(2,1)S(1)}, bf16[88,640]{1,0:T(8,128)(2,1)S(1)}, u32[]{:S(2)}, u32[]{:S(2)}) collective-permute-start(bf16[88,640]{1,0:T(8,128)(2,1)S(1)} %shard_map.63.refs_0_), channel_id=1, source_target_pairs={{0,2},{2,0},{1,3},{3,1},{4,6},{6,4},{5,7},{7,5},{8,10},{10,8},{9,1... | collective-permute-start | bytes 337928 | tf_op jit(solution)/shard_map/ppermute | solution.py:45
  8.6 2.0 %collective-permute-start.11 = (bf16[88,640]{1,0:T(8,128)(2,1)S(1)}, bf16[88,640]{1,0:T(8,128)(2,1)S(1)}, u32[]{:S(2)}, u32[]{:S(2)}) collective-permute-start(bf16[88,640]{1,0:T(8,128)(2,1)S(1)} %shard_map.63.refs_0_), channel_id=1, source_target_pairs={{0,128},{64,192},{128,0},{192,64},{1,129},{65,193},{129,1},{193,65... | collective-permute-start | bytes 337928 | tf_op jit(solution)/shard_map/ppermute | solution.py:45
  11.3 6.8 %collective-permute-start.2 = (bf16[88,640]{1,0:T(8,128)(2,1)S(1)}, bf16[88,640]{1,0:T(8,128)(2,1)S(1)}, u32[]{:S(2)}, u32[]{:S(2)}) collective-permute-start(bf16[88,640]{1,0:T(8,128)(2,1)S(1)} %shard_map.60.refs_0_), channel_id=1, source_target_pairs={{0,40},{8,48},{16,56},{24,0},{32,8},{40,16},{48,24},{56,32},{1,41}... | collective-permute-start | bytes 337928 | tf_op jit(solution)/shard_map/ppermute | solution.py:50
  18.1 1.7 %collective-permute-start.7 = (bf16[88,640]{1,0:T(8,128)(2,1)S(1)}, bf16[88,640]{1,0:T(8,128)(2,1)S(1)}, u32[]{:S(2)}, u32[]{:S(2)}) collective-permute-start(bf16[88,640]{1,0:T(8,128)(2,1)S(1)} %collective-permute-done.4.refs_0_), channel_id=1, source_target_pairs={{0,192},{64,128},{128,64},{192,0},{1,193},{65,129},{129,65},{193,1... | collective-permute-start | bytes 337928 | tf_op jit(solution)/shard_map/ppermute | solution.py:45
  19.8 1.8 %collective-permute-start.6 = (bf16[88,640]{1,0:T(8,128)(2,1)S(1)}, bf16[88,640]{1,0:T(8,128)(2,1)S(1)}, u32[]{:S(2)}, u32[]{:S(2)}) collective-permute-start(bf16[88,640]{1,0:T(8,128)(2,1)S(1)} %collective-permute-done.4.refs_0_), channel_id=1, source_target_pairs={{0,128},{64,192},{128,0},{192,64},{1,129},{65,193},{129,1},{193,65... | collective-permute-start | bytes 337928 | tf_op jit(solution)/shard_map/ppermute | solution.py:45
  21.6 1.2 %collective-permute-start.5 = (bf16[88,640]{1,0:T(8,128)(2,1)S(1)}, bf16[88,640]{1,0:T(8,128)(2,1)S(1)}, u32[]{:S(2)}, u32[]{:S(2)}) collective-permute-start(bf16[88,640]{1,0:T(8,128)(2,1)S(1)} %collective-permute-done.4.refs_0_), channel_id=1, source_target_pairs={{0,64},{64,0},{128,192},{192,128},{1,65},{65,1},{129,193},{193,129... | collective-permute-start | bytes 337928 | tf_op jit(solution)/shard_map/ppermute | solution.py:45
  22.8 1.7 %collective-permute-done.2.refs_2_ = bf16[88,640]{1,0:T(8,128)(2,1)S(1)} collective-permute-done((bf16[88,640]{1,0:T(8,128)(2,1)S(1)}, bf16[88,640]{1,0:T(8,128)(2,1)S(1)}, u32[]{:S(2)}, u32[]{:S(2)}) %collective-permute-start.2) | collective-permute-done | bytes 112672 | tf_op jit(solution)/shard_map/ppermute | solution.py:50
  24.5 2.1 %collective-permute-start.14 = (bf16[4,88,640]{2,1,0:T(8,128)(2,1)S(1)}, bf16[4,88,640]{2,1,0:T(8,128)(2,1)S(1)}, u32[]{:S(2)}, u32[]{:S(2)}) collective-permute-start(bf16[4,88,640]{2,1,0:T(8,128)(2,1)S(1)} %shard_map.65.refs_6_), channel_id=1, source_target_pairs={{0,6},{2,4},{4,2},{6,0},{1,7},{3,5},{5,3},{7,1},{8,14},{10,12},{12... | collective-permute-start | bytes 1351688 | tf_op jit(solution)/shard_map/ppermute | solution.py:45
  26.6 2.4 %collective-permute-done.1.refs_1_ = bf16[88,640]{1,0:T(8,128)(2,1)S(1)} collective-permute-done((bf16[88,640]{1,0:T(8,128)(2,1)S(1)}, bf16[88,640]{1,0:T(8,128)(2,1)S(1)}, u32[]{:S(2)}, u32[]{:S(2)}) %collective-permute-start.1) | collective-permute-done | bytes 112672 | tf_op jit(solution)/shard_map/ppermute | solution.py:50
  30.1 3.2 %collective-permute-start.9 = (bf16[2,88,640]{2,1,0:T(8,128)(2,1)S(1)}, bf16[2,88,640]{2,1,0:T(8,128)(2,1)S(1)}, u32[]{:S(2)}, u32[]{:S(2)}) collective-permute-start(bf16[2,88,640]{2,1,0:T(8,128)(2,1)S(1)} %shard_map.62), channel_id=1, source_target_pairs={{0,56},{8,0},{16,8},{24,16},{32,24},{40,32},{48,40},{56,48},{1,57}... | collective-permute-start | bytes 675848 | tf_op jit(solution)/shard_map/ppermute | solution.py:50
  33.3 3.9 %collective-permute-done.9.refs_2_ = bf16[2,88,640]{2,1,0:T(8,128)(2,1)S(1)} collective-permute-done((bf16[2,88,640]{2,1,0:T(8,128)(2,1)S(1)}, bf16[2,88,640]{2,1,0:T(8,128)(2,1)S(1)}, u32[]{:S(2)}, u32[]{:S(2)}) %collective-permute-start.9) | collective-permute-done | bytes 225312 | tf_op jit(solution)/shard_map/ppermute | solution.py:50
  37.2 3.1 %collective-permute-done.8.refs_1_ = bf16[3,88,640]{2,1,0:T(8,128)(2,1)S(1)} collective-permute-done((bf16[3,88,640]{2,1,0:T(8,128)(2,1)S(1)}, bf16[3,88,640]{2,1,0:T(8,128)(2,1)S(1)}, u32[]{:S(2)}, u32[]{:S(2)}) %collective-permute-start.8) | collective-permute-done | bytes 337952 | tf_op jit(solution)/shard_map/ppermute | solution.py:50
  43.3 3.9 %shard_map.66 = (f32[8,88,640]{2,1,0:T(8,128)S(1)}, bf16[768,768]{1,0:T(8,128)(2,1)S(1)}, bf16[768,1280]{1,0:T(8,128)(2,1)S(1)}, bf16[768,1280]{1,0:T(8,128)(2,1)S(1)}) custom-call(bf16[3,88,640]{2,1,0:T(8,128)(2,1)S(1)} %shard_map.61.refs_0_, bf16[3,88,640]{2,1,0:T(8,128)(2,1)S(1)} %collective-permute-done.8.refs_1_, ...), custom_call_target="tpu_custom_call" | custom-call | flops 1712848896 | bytes 10518536 | tf_op jit(solution)/shard_map/pallas_call | solution.py:32
  47.4 2.9 %shard_map.67 = (f32[8,88,640]{2,1,0:T(8,128)S(1)}, f32[4,88,577]{2,1,0:T(8,128)S(1)}, f32[4,88,577]{2,1,0:T(8,128)S(1)}, f32[4,88,577]{2,1,0:T(8,128)S(1)}, f32...) custom-call(bf16[768,768]{1,0:T(8,128)(2,1)S(1)} %get-tuple-element.58.slope, ...), custom_call_target="tpu_custom_call" | custom-call | flops 1712848896 | bytes 10163712 | tf_op jit(solution)/shard_map/pallas_call | solution.py:32
  51.7 1.9 %collective-permute-start.20 = (f16[2,88,640]{2,1,0:T(8,128)(2,1)S(1)}, f16[2,88,640]{2,1,0:T(8,128)(2,1)S(1)}, u32[]{:S(2)}, u32[]{:S(2)}) collective-permute-start(f16[2,88,640]{2,1,0:T(8,128)(2,1)S(1)} %convert_element_type.80), channel_id=1, source_target_pairs={{0,8},{8,16},{16,24},{24,32},{32,40},{40,48},{48,56},{56,0},{1,9},... | collective-permute-start | bytes 675848 | tf_op jit(solution)/shard_map/ppermute | solution.py:50
  53.7 2.2 %collective-permute-start.25 = (f16[4,88,577]{2,1,0:T(8,128)(2,1)S(1)}, f16[4,88,577]{2,1,0:T(8,128)(2,1)S(1)}, u32[]{:S(2)}, u32[]{:S(2)}) collective-permute-start(f16[4,88,577]{2,1,0:T(8,128)(2,1)S(1)} %convert_element_type.88), channel_id=1, source_target_pairs={{0,6},{2,4},{4,2},{6,0},{1,7},{3,5},{5,3},{7,1},{8,14},{10,12},{12... | collective-permute-start | bytes 1218632 | tf_op jit(solution)/shard_map/ppermute | solution.py:45
  56.2 1.7 %collective-permute-start.28 = (f16[88,577]{1,0:T(8,128)(2,1)S(1)}, f16[88,577]{1,0:T(8,128)(2,1)S(1)}, u32[]{:S(2)}, u32[]{:S(2)}) collective-permute-start(f16[88,577]{1,0:T(8,128)(2,1)S(1)} %convert_element_type.94), channel_id=1, source_target_pairs={{0,192},{64,128},{128,64},{192,0},{1,193},{65,129},{129,65},{193,1... | collective-permute-start | bytes 304664 | tf_op jit(solution)/shard_map/ppermute | solution.py:45
  57.9 2.4 %collective-permute-done.20 = f16[2,88,640]{2,1,0:T(8,128)(2,1)S(1)} collective-permute-done((f16[2,88,640]{2,1,0:T(8,128)(2,1)S(1)}, f16[2,88,640]{2,1,0:T(8,128)(2,1)S(1)}, u32[]{:S(2)}, u32[]{:S(2)}) %collective-permute-start.20) | collective-permute-done | bytes 225312 | tf_op jit(solution)/shard_map/ppermute | solution.py:50
  60.4 1.8 %collective-permute-start.27 = (f16[88,577]{1,0:T(8,128)(2,1)S(1)}, f16[88,577]{1,0:T(8,128)(2,1)S(1)}, u32[]{:S(2)}, u32[]{:S(2)}) collective-permute-start(f16[88,577]{1,0:T(8,128)(2,1)S(1)} %convert_element_type.92), channel_id=1, source_target_pairs={{0,128},{64,192},{128,0},{192,64},{1,129},{65,193},{129,1},{193,65... | collective-permute-start | bytes 304664 | tf_op jit(solution)/shard_map/ppermute | solution.py:45
  62.6 2.1 %collective-permute-start.22 = (f16[88,640]{1,0:T(8,128)(2,1)S(1)}, f16[88,640]{1,0:T(8,128)(2,1)S(1)}, u32[]{:S(2)}, u32[]{:S(2)}) collective-permute-start(f16[88,640]{1,0:T(8,128)(2,1)S(1)} %convert_element_type.84), channel_id=1, source_target_pairs={{0,24},{8,32},{16,40},{24,48},{32,56},{40,0},{48,8},{56,16},{1,25}... | collective-permute-start | bytes 337928 | tf_op jit(solution)/shard_map/ppermute | solution.py:50
  64.9 2.6 %collective-permute-done.27 = f16[88,577]{1,0:T(8,128)(2,1)S(1)} collective-permute-done((f16[88,577]{1,0:T(8,128)(2,1)S(1)}, f16[88,577]{1,0:T(8,128)(2,1)S(1)}, u32[]{:S(2)}, u32[]{:S(2)}) %collective-permute-start.27) | collective-permute-done | bytes 101584 | tf_op jit(solution)/shard_map/ppermute | solution.py:45
  67.4 2.4 %collective-permute-start.21 = (f16[88,640]{1,0:T(8,128)(2,1)S(1)}, f16[88,640]{1,0:T(8,128)(2,1)S(1)}, u32[]{:S(2)}, u32[]{:S(2)}) collective-permute-start(f16[88,640]{1,0:T(8,128)(2,1)S(1)} %convert_element_type.82), channel_id=1, source_target_pairs={{0,40},{8,48},{16,56},{24,0},{32,8},{40,16},{48,24},{56,32},{1,41}... | collective-permute-start | bytes 337928 | tf_op jit(solution)/shard_map/ppermute | solution.py:50
  70.2 2.9 %collective-permute-start.29 = (f16[88,577]{1,0:T(8,128)(2,1)S(1)}, f16[88,577]{1,0:T(8,128)(2,1)S(1)}, u32[]{:S(2)}, u32[]{:S(2)}) collective-permute-start(f16[88,577]{1,0:T(8,128)(2,1)S(1)} %convert_element_type.96), channel_id=1, source_target_pairs={{0,2},{2,0},{1,3},{3,1},{4,6},{6,4},{5,7},{7,5},{8,10},{10,8},{9,1... | collective-permute-start | bytes 304664 | tf_op jit(solution)/shard_map/ppermute | solution.py:45
  74.4 2.3 %collective-permute-start.31 = (f16[88,577]{1,0:T(8,128)(2,1)S(1)}, f16[88,577]{1,0:T(8,128)(2,1)S(1)}, u32[]{:S(2)}, u32[]{:S(2)}) collective-permute-start(f16[88,577]{1,0:T(8,128)(2,1)S(1)} %convert_element_type.100), channel_id=1, source_target_pairs={{0,128},{64,192},{128,0},{192,64},{1,129},{65,193},{129,1},{193,65... | collective-permute-start | bytes 304664 | tf_op jit(solution)/shard_map/ppermute | solution.py:45
  76.7 1.4 %collective-permute-start.30 = (f16[88,577]{1,0:T(8,128)(2,1)S(1)}, f16[88,577]{1,0:T(8,128)(2,1)S(1)}, u32[]{:S(2)}, u32[]{:S(2)}) collective-permute-start(f16[88,577]{1,0:T(8,128)(2,1)S(1)} %convert_element_type.98), channel_id=1, source_target_pairs={{0,64},{64,0},{128,192},{192,128},{1,65},{65,1},{129,193},{193,129... | collective-permute-start | bytes 304664 | tf_op jit(solution)/shard_map/ppermute | solution.py:45
  78.4 1.0 %collective-permute-start.23 = (f32[88,512]{1,0:T(8,128)S(1)}, f32[88,512]{1,0:T(8,128)S(1)}, u32[]{:S(2)}, u32[]{:S(2)}) collective-permute-start(f32[88,512]{1,0:T(8,128)S(1)} %get-tuple-element.74), channel_id=1, source_target_pairs={{0,2},{2,0},{1,3},{3,1},{4,6},{6,4},{5,7},{7,5},{8,10},{10,8},{9,1... | collective-permute-start | bytes 540680 | tf_op jit(solution)/shard_map/ppermute | solution.py:45
  79.4 1.3 %collective-permute-done.31 = f16[88,577]{1,0:T(8,128)(2,1)S(1)} collective-permute-done((f16[88,577]{1,0:T(8,128)(2,1)S(1)}, f16[88,577]{1,0:T(8,128)(2,1)S(1)}, u32[]{:S(2)}, u32[]{:S(2)}) %collective-permute-start.31) | collective-permute-done | bytes 101584 | tf_op jit(solution)/shard_map/ppermute | solution.py:45
  80.7 1.3 %collective-permute-done.30 = f16[88,577]{1,0:T(8,128)(2,1)S(1)} collective-permute-done((f16[88,577]{1,0:T(8,128)(2,1)S(1)}, f16[88,577]{1,0:T(8,128)(2,1)S(1)}, u32[]{:S(2)}, u32[]{:S(2)}) %collective-permute-start.30) | collective-permute-done | bytes 101584 | tf_op jit(solution)/shard_map/ppermute | solution.py:45
  82.4 1.3 %collective-permute-done.33.text_recv = f32[88,288]{1,0:T(8,128)S(1)} collective-permute-done((f32[88,288]{1,0:T(8,128)S(1)}, f32[88,288]{1,0:T(8,128)S(1)}, u32[]{:S(2)}, u32[]{:S(2)}) %collective-permute-start.33) | collective-permute-done | bytes 101408 | tf_op jit(solution)/shard_map/ppermute | solution.py:45
  83.8 1.7 %collective-permute-done.23.image_recv = f32[88,512]{1,0:T(8,128)S(1)} collective-permute-done((f32[88,512]{1,0:T(8,128)S(1)}, f32[88,512]{1,0:T(8,128)S(1)}, u32[]{:S(2)}, u32[]{:S(2)}) %collective-permute-start.23) | collective-permute-done | bytes 180256 | tf_op jit(solution)/shard_map/ppermute | solution.py:45
  (82 shorter events, 11.1 us)
Async XLA Ops:
  2.5 3.2 %collective-permute-start.3 = (bf16[88,288]{1,0:T(8,128)(2,1)S(1)}, bf16[88,288]{1,0:T(8,128)(2,1)S(1)}, u32[]{:S(2)}, u32[]{:S(2)}) collective-permute-start(bf16[88,288]{1,0:T(8,128)(2,1)S(1)} %get-tuple-element.48), channel_id=1, source_target_pairs={{0,1},{1,0},{2,3},{3,2},{4,5},{5,4},{6,7},{7,6},{8,9},{9,8},{10,11... | collective-permute-start | bytes 152072 | tf_op jit(solution)/shard_map/ppermute | solution.py:45
  2.6 8.5 %collective-permute-start = (bf16[96,640]{1,0:T(8,128)(2,1)S(1)}, bf16[96,640]{1,0:T(8,128)(2,1)S(1)}, u32[]{:S(2)}, u32[]{:S(2)}) collective-permute-start(bf16[96,640]{1,0:T(8,128)(2,1)S(1)} %get-tuple-element.46), channel_id=1, source_target_pairs={{0,2},{2,0},{1,3},{3,1},{4,6},{6,4},{5,7},{7,5},{8,10},{10,8},{9,1... | collective-permute-start | bytes 368648 | tf_op jit(solution)/shard_map/ppermute | solution.py:45
  5.8 12.3 %collective-permute-start.12 = (bf16[88,640]{1,0:T(8,128)(2,1)S(1)}, bf16[88,640]{1,0:T(8,128)(2,1)S(1)}, u32[]{:S(2)}, u32[]{:S(2)}) collective-permute-start(bf16[88,640]{1,0:T(8,128)(2,1)S(1)} %shard_map.63.refs_0_), channel_id=1, source_target_pairs={{0,192},{64,128},{128,64},{192,0},{1,193},{65,129},{129,65},{193,1... | collective-permute-start | bytes 337928 | tf_op jit(solution)/shard_map/ppermute | solution.py:45
  7.5 10.6 %collective-permute-start.4 = (bf16[88,640]{1,0:T(8,128)(2,1)S(1)}, bf16[88,640]{1,0:T(8,128)(2,1)S(1)}, u32[]{:S(2)}, u32[]{:S(2)}) collective-permute-start(bf16[88,640]{1,0:T(8,128)(2,1)S(1)} %shard_map.63.refs_0_), channel_id=1, source_target_pairs={{0,2},{2,0},{1,3},{3,1},{4,6},{6,4},{5,7},{7,5},{8,10},{10,8},{9,1... | collective-permute-start | bytes 337928 | tf_op jit(solution)/shard_map/ppermute | solution.py:45
  8.6 11.1 %collective-permute-start.11 = (bf16[88,640]{1,0:T(8,128)(2,1)S(1)}, bf16[88,640]{1,0:T(8,128)(2,1)S(1)}, u32[]{:S(2)}, u32[]{:S(2)}) collective-permute-start(bf16[88,640]{1,0:T(8,128)(2,1)S(1)} %shard_map.63.refs_0_), channel_id=1, source_target_pairs={{0,128},{64,192},{128,0},{192,64},{1,129},{65,193},{129,1},{193,65... | collective-permute-start | bytes 337928 | tf_op jit(solution)/shard_map/ppermute | solution.py:45
  10.7 10.9 %collective-permute-start.10 = (bf16[88,640]{1,0:T(8,128)(2,1)S(1)}, bf16[88,640]{1,0:T(8,128)(2,1)S(1)}, u32[]{:S(2)}, u32[]{:S(2)}) collective-permute-start(bf16[88,640]{1,0:T(8,128)(2,1)S(1)} %shard_map.63.refs_0_), channel_id=1, source_target_pairs={{0,64},{64,0},{128,192},{192,128},{1,65},{65,1},{129,193},{193,129... | collective-permute-start | bytes 337928 | tf_op jit(solution)/shard_map/ppermute | solution.py:45
  11.3 13.2 %collective-permute-start.2 = (bf16[88,640]{1,0:T(8,128)(2,1)S(1)}, bf16[88,640]{1,0:T(8,128)(2,1)S(1)}, u32[]{:S(2)}, u32[]{:S(2)}) collective-permute-start(bf16[88,640]{1,0:T(8,128)(2,1)S(1)} %shard_map.60.refs_0_), channel_id=1, source_target_pairs={{0,40},{8,48},{16,56},{24,0},{32,8},{40,16},{48,24},{56,32},{1,41}... | collective-permute-start | bytes 337928 | tf_op jit(solution)/shard_map/ppermute | solution.py:50
  18.1 10.9 %collective-permute-start.1 = (bf16[88,640]{1,0:T(8,128)(2,1)S(1)}, bf16[88,640]{1,0:T(8,128)(2,1)S(1)}, u32[]{:S(2)}, u32[]{:S(2)}) collective-permute-start(bf16[88,640]{1,0:T(8,128)(2,1)S(1)} %shard_map.60.refs_0_), channel_id=1, source_target_pairs={{0,24},{8,32},{16,40},{24,48},{32,56},{40,0},{48,8},{56,16},{1,25}... | collective-permute-start | bytes 337928 | tf_op jit(solution)/shard_map/ppermute | solution.py:50
  18.1 11.8 %collective-permute-start.7 = (bf16[88,640]{1,0:T(8,128)(2,1)S(1)}, bf16[88,640]{1,0:T(8,128)(2,1)S(1)}, u32[]{:S(2)}, u32[]{:S(2)}) collective-permute-start(bf16[88,640]{1,0:T(8,128)(2,1)S(1)} %collective-permute-done.4.refs_0_), channel_id=1, source_target_pairs={{0,192},{64,128},{128,64},{192,0},{1,193},{65,129},{129,65},{193,1... | collective-permute-start | bytes 337928 | tf_op jit(solution)/shard_map/ppermute | solution.py:45
  19.8 10.2 %collective-permute-start.6 = (bf16[88,640]{1,0:T(8,128)(2,1)S(1)}, bf16[88,640]{1,0:T(8,128)(2,1)S(1)}, u32[]{:S(2)}, u32[]{:S(2)}) collective-permute-start(bf16[88,640]{1,0:T(8,128)(2,1)S(1)} %collective-permute-done.4.refs_0_), channel_id=1, source_target_pairs={{0,128},{64,192},{128,0},{192,64},{1,129},{65,193},{129,1},{193,65... | collective-permute-start | bytes 337928 | tf_op jit(solution)/shard_map/ppermute | solution.py:45
  21.6 8.3 %collective-permute-start.5 = (bf16[88,640]{1,0:T(8,128)(2,1)S(1)}, bf16[88,640]{1,0:T(8,128)(2,1)S(1)}, u32[]{:S(2)}, u32[]{:S(2)}) collective-permute-start(bf16[88,640]{1,0:T(8,128)(2,1)S(1)} %collective-permute-done.4.refs_0_), channel_id=1, source_target_pairs={{0,64},{64,0},{128,192},{192,128},{1,65},{65,1},{129,193},{193,129... | collective-permute-start | bytes 337928 | tf_op jit(solution)/shard_map/ppermute | solution.py:45
  24.5 15.8 %collective-permute-start.14 = (bf16[4,88,640]{2,1,0:T(8,128)(2,1)S(1)}, bf16[4,88,640]{2,1,0:T(8,128)(2,1)S(1)}, u32[]{:S(2)}, u32[]{:S(2)}) collective-permute-start(bf16[4,88,640]{2,1,0:T(8,128)(2,1)S(1)} %shard_map.65.refs_6_), channel_id=1, source_target_pairs={{0,6},{2,4},{4,2},{6,0},{1,7},{3,5},{5,3},{7,1},{8,14},{10,12},{12... | collective-permute-start | bytes 1351688 | tf_op jit(solution)/shard_map/ppermute | solution.py:45
  29.0 11.7 %collective-permute-start.13 = (bf16[4,88,640]{2,1,0:T(8,128)(2,1)S(1)}, bf16[4,88,640]{2,1,0:T(8,128)(2,1)S(1)}, u32[]{:S(2)}, u32[]{:S(2)}) collective-permute-start(bf16[4,88,640]{2,1,0:T(8,128)(2,1)S(1)} %shard_map.65.refs_6_), channel_id=1, source_target_pairs={{0,4},{2,6},{4,0},{6,2},{1,5},{3,7},{5,1},{7,3},{8,12},{10,14},{12... | collective-permute-start | bytes 1351688 | tf_op jit(solution)/shard_map/ppermute | solution.py:45
  30.0 10.3 %collective-permute-start.8 = (bf16[3,88,640]{2,1,0:T(8,128)(2,1)S(1)}, bf16[3,88,640]{2,1,0:T(8,128)(2,1)S(1)}, u32[]{:S(2)}, u32[]{:S(2)}) collective-permute-start(bf16[3,88,640]{2,1,0:T(8,128)(2,1)S(1)} %shard_map.61.refs_0_), channel_id=1, source_target_pairs={{0,8},{8,16},{16,24},{24,32},{32,40},{40,48},{48,56},{56,0},{1,9},... | collective-permute-start | bytes 1013768 | tf_op jit(solution)/shard_map/ppermute | solution.py:50
  30.1 7.1 %collective-permute-start.9 = (bf16[2,88,640]{2,1,0:T(8,128)(2,1)S(1)}, bf16[2,88,640]{2,1,0:T(8,128)(2,1)S(1)}, u32[]{:S(2)}, u32[]{:S(2)}) collective-permute-start(bf16[2,88,640]{2,1,0:T(8,128)(2,1)S(1)} %shard_map.62), channel_id=1, source_target_pairs={{0,56},{8,0},{16,8},{24,16},{32,24},{40,32},{48,40},{56,48},{1,57}... | collective-permute-start | bytes 675848 | tf_op jit(solution)/shard_map/ppermute | solution.py:50
  40.7 2.6 %collective-permute-start.15 = (bf16[3,88,640]{2,1,0:T(8,128)(2,1)S(1)}, bf16[3,88,640]{2,1,0:T(8,128)(2,1)S(1)}, u32[]{:S(2)}, u32[]{:S(2)}) collective-permute-start(bf16[3,88,640]{2,1,0:T(8,128)(2,1)S(1)} %shard_map.61.refs_0_), channel_id=1, source_target_pairs={{0,1},{1,0},{2,3},{3,2},{4,5},{5,4},{6,7},{7,6},{8,9},{9,8},{10,11... | collective-permute-start | bytes 1013768 | tf_op jit(solution)/shard_map/ppermute | solution.py:45
  40.7 2.6 %collective-permute-start.16 = (bf16[3,88,640]{2,1,0:T(8,128)(2,1)S(1)}, bf16[3,88,640]{2,1,0:T(8,128)(2,1)S(1)}, u32[]{:S(2)}, u32[]{:S(2)}) collective-permute-start(bf16[3,88,640]{2,1,0:T(8,128)(2,1)S(1)} %collective-permute-done.8.refs_1_), channel_id=1, source_target_pairs={{0,1},{1,0},{2,3},{3,2},{4,5},{5,4},{6,7},{7,6},{8,9},{9,8},{10,11... | collective-permute-start | bytes 1013768 | tf_op jit(solution)/shard_map/ppermute | solution.py:45
  47.2 3.8 %collective-permute-start.18 = (f32[8,88,640]{2,1,0:T(8,128)S(1)}, f32[8,88,640]{2,1,0:T(8,128)S(1)}, u32[]{:S(2)}, u32[]{:S(2)}) collective-permute-start(f32[8,88,640]{2,1,0:T(8,128)S(1)} %get-tuple-element.62), channel_id=1, source_target_pairs={{0,1},{1,0},{2,3},{3,2},{4,5},{5,4},{6,7},{7,6},{8,9},{9,8},{10,11... | collective-permute-start | bytes 5406728 | tf_op jit(solution)/shard_map/ppermute | solution.py:45
  51.4 10.8 %collective-permute-start.19 = (f16[3,88,640]{2,1,0:T(8,128)(2,1)S(1)}, f16[3,88,640]{2,1,0:T(8,128)(2,1)S(1)}, u32[]{:S(2)}, u32[]{:S(2)}) collective-permute-start(f16[3,88,640]{2,1,0:T(8,128)(2,1)S(1)} %convert_element_type.78), channel_id=1, source_target_pairs={{0,56},{8,0},{16,8},{24,16},{32,24},{40,32},{48,40},{56,48},{1,57}... | collective-permute-start | bytes 1013768 | tf_op jit(solution)/shard_map/ppermute | solution.py:50
  51.7 8.7 %collective-permute-start.20 = (f16[2,88,640]{2,1,0:T(8,128)(2,1)S(1)}, f16[2,88,640]{2,1,0:T(8,128)(2,1)S(1)}, u32[]{:S(2)}, u32[]{:S(2)}) collective-permute-start(f16[2,88,640]{2,1,0:T(8,128)(2,1)S(1)} %convert_element_type.80), channel_id=1, source_target_pairs={{0,8},{8,16},{16,24},{24,32},{32,40},{40,48},{48,56},{56,0},{1,9},... | collective-permute-start | bytes 675848 | tf_op jit(solution)/shard_map/ppermute | solution.py:50
  53.7 19.5 %collective-permute-start.25 = (f16[4,88,577]{2,1,0:T(8,128)(2,1)S(1)}, f16[4,88,577]{2,1,0:T(8,128)(2,1)S(1)}, u32[]{:S(2)}, u32[]{:S(2)}) collective-permute-start(f16[4,88,577]{2,1,0:T(8,128)(2,1)S(1)} %convert_element_type.88), channel_id=1, source_target_pairs={{0,6},{2,4},{4,2},{6,0},{1,7},{3,5},{5,3},{7,1},{8,14},{10,12},{12... | collective-permute-start | bytes 1218632 | tf_op jit(solution)/shard_map/ppermute | solution.py:45
  55.9 17.4 %collective-permute-start.24 = (f16[4,88,577]{2,1,0:T(8,128)(2,1)S(1)}, f16[4,88,577]{2,1,0:T(8,128)(2,1)S(1)}, u32[]{:S(2)}, u32[]{:S(2)}) collective-permute-start(f16[4,88,577]{2,1,0:T(8,128)(2,1)S(1)} %convert_element_type.86), channel_id=1, source_target_pairs={{0,4},{2,6},{4,0},{6,2},{1,5},{3,7},{5,1},{7,3},{8,12},{10,14},{12... | collective-permute-start | bytes 1218632 | tf_op jit(solution)/shard_map/ppermute | solution.py:45
  56.2 8.5 %collective-permute-start.28 = (f16[88,577]{1,0:T(8,128)(2,1)S(1)}, f16[88,577]{1,0:T(8,128)(2,1)S(1)}, u32[]{:S(2)}, u32[]{:S(2)}) collective-permute-start(f16[88,577]{1,0:T(8,128)(2,1)S(1)} %convert_element_type.94), channel_id=1, source_target_pairs={{0,192},{64,128},{128,64},{192,0},{1,193},{65,129},{129,65},{193,1... | collective-permute-start | bytes 304664 | tf_op jit(solution)/shard_map/ppermute | solution.py:45
  60.4 7.1 %collective-permute-start.27 = (f16[88,577]{1,0:T(8,128)(2,1)S(1)}, f16[88,577]{1,0:T(8,128)(2,1)S(1)}, u32[]{:S(2)}, u32[]{:S(2)}) collective-permute-start(f16[88,577]{1,0:T(8,128)(2,1)S(1)} %convert_element_type.92), channel_id=1, source_target_pairs={{0,128},{64,192},{128,0},{192,64},{1,129},{65,193},{129,1},{193,65... | collective-permute-start | bytes 304664 | tf_op jit(solution)/shard_map/ppermute | solution.py:45
  62.6 14.1 %collective-permute-start.22 = (f16[88,640]{1,0:T(8,128)(2,1)S(1)}, f16[88,640]{1,0:T(8,128)(2,1)S(1)}, u32[]{:S(2)}, u32[]{:S(2)}) collective-permute-start(f16[88,640]{1,0:T(8,128)(2,1)S(1)} %convert_element_type.84), channel_id=1, source_target_pairs={{0,24},{8,32},{16,40},{24,48},{32,56},{40,0},{48,8},{56,16},{1,25}... | collective-permute-start | bytes 337928 | tf_op jit(solution)/shard_map/ppermute | solution.py:50
  64.7 5.2 %collective-permute-start.26 = (f16[88,577]{1,0:T(8,128)(2,1)S(1)}, f16[88,577]{1,0:T(8,128)(2,1)S(1)}, u32[]{:S(2)}, u32[]{:S(2)}) collective-permute-start(f16[88,577]{1,0:T(8,128)(2,1)S(1)} %convert_element_type.90), channel_id=1, source_target_pairs={{0,64},{64,0},{128,192},{192,128},{1,65},{65,1},{129,193},{193,129... | collective-permute-start | bytes 304664 | tf_op jit(solution)/shard_map/ppermute | solution.py:45
  67.4 10.7 %collective-permute-start.21 = (f16[88,640]{1,0:T(8,128)(2,1)S(1)}, f16[88,640]{1,0:T(8,128)(2,1)S(1)}, u32[]{:S(2)}, u32[]{:S(2)}) collective-permute-start(f16[88,640]{1,0:T(8,128)(2,1)S(1)} %convert_element_type.82), channel_id=1, source_target_pairs={{0,40},{8,48},{16,56},{24,0},{32,8},{40,16},{48,24},{56,32},{1,41}... | collective-permute-start | bytes 337928 | tf_op jit(solution)/shard_map/ppermute | solution.py:50
  70.2 9.1 %collective-permute-start.29 = (f16[88,577]{1,0:T(8,128)(2,1)S(1)}, f16[88,577]{1,0:T(8,128)(2,1)S(1)}, u32[]{:S(2)}, u32[]{:S(2)}) collective-permute-start(f16[88,577]{1,0:T(8,128)(2,1)S(1)} %convert_element_type.96), channel_id=1, source_target_pairs={{0,2},{2,0},{1,3},{3,1},{4,6},{6,4},{5,7},{7,5},{8,10},{10,8},{9,1... | collective-permute-start | bytes 304664 | tf_op jit(solution)/shard_map/ppermute | solution.py:45
  73.8 5.6 %collective-permute-start.32 = (f16[88,577]{1,0:T(8,128)(2,1)S(1)}, f16[88,577]{1,0:T(8,128)(2,1)S(1)}, u32[]{:S(2)}, u32[]{:S(2)}) collective-permute-start(f16[88,577]{1,0:T(8,128)(2,1)S(1)} %convert_element_type.102), channel_id=1, source_target_pairs={{0,192},{64,128},{128,64},{192,0},{1,193},{65,129},{129,65},{193,1... | collective-permute-start | bytes 304664 | tf_op jit(solution)/shard_map/ppermute | solution.py:45
  74.4 6.4 %collective-permute-start.31 = (f16[88,577]{1,0:T(8,128)(2,1)S(1)}, f16[88,577]{1,0:T(8,128)(2,1)S(1)}, u32[]{:S(2)}, u32[]{:S(2)}) collective-permute-start(f16[88,577]{1,0:T(8,128)(2,1)S(1)} %convert_element_type.100), channel_id=1, source_target_pairs={{0,128},{64,192},{128,0},{192,64},{1,129},{65,193},{129,1},{193,65... | collective-permute-start | bytes 304664 | tf_op jit(solution)/shard_map/ppermute | solution.py:45
  76.7 5.3 %collective-permute-start.30 = (f16[88,577]{1,0:T(8,128)(2,1)S(1)}, f16[88,577]{1,0:T(8,128)(2,1)S(1)}, u32[]{:S(2)}, u32[]{:S(2)}) collective-permute-start(f16[88,577]{1,0:T(8,128)(2,1)S(1)} %convert_element_type.98), channel_id=1, source_target_pairs={{0,64},{64,0},{128,192},{192,128},{1,65},{65,1},{129,193},{193,129... | collective-permute-start | bytes 304664 | tf_op jit(solution)/shard_map/ppermute | solution.py:45
  78.4 7.1 %collective-permute-start.23 = (f32[88,512]{1,0:T(8,128)S(1)}, f32[88,512]{1,0:T(8,128)S(1)}, u32[]{:S(2)}, u32[]{:S(2)}) collective-permute-start(f32[88,512]{1,0:T(8,128)S(1)} %get-tuple-element.74), channel_id=1, source_target_pairs={{0,2},{2,0},{1,3},{3,1},{4,6},{6,4},{5,7},{7,5},{8,10},{10,8},{9,1... | collective-permute-start | bytes 540680 | tf_op jit(solution)/shard_map/ppermute | solution.py:45
  (4 other events, 5.3 us)

commit v5 on v4

--- a/solution.py
+++ b/solution.py
@@ -26,15 +26,13 @@
     return jax.ShapeDtypeStruct(dims, dtype)
 
 
-def call(kernel, outs, *args, smem=0, scratch=(), flops=0, mib=32):
-    specs = [VMEM] * (len(args) - smem) + [SMEM] * smem
+def call(kernel, outs, *args, smem=0, flops=0, mib=32):
     moved = sum(a.size * a.dtype.itemsize for a in (*args, *outs))
     return pl.pallas_call(
         kernel,
         out_shape=outs,
-        in_specs=specs,
+        in_specs=[VMEM] * (len(args) - smem) + [SMEM] * smem,
         out_specs=[VMEM] * len(outs),
-        scratch_shapes=list(scratch),
         compiler_params=pltpu.CompilerParams(vmem_limit_bytes=mib * 2**20),
         cost_estimate=pl.CostEstimate(flops=flops, bytes_accessed=moved, transcendentals=0),
     )(*args)
@@ -75,6 +73,12 @@
     out[...] = jnp.concatenate([a, b, jnp.zeros((ROWS, WIDE - HALF), F32)], axis=1).astype(BF16)
 
 
+def first_stack_kernel(text, r1, r2, r3, scale, bias, out, scalars):
+    stack_kernel(text, r1, r2, r3, out)
+    scalars[:8] = jnp.full((8, 128), scale[0])
+    scalars[8:] = jnp.full((8, 128), bias[0])
+
+
 def stack_kernel(*refs):
     for n, ref in enumerate(refs[:-1]):
         refs[-1][n] = ref[...]
@@ -91,23 +95,38 @@
     return p * jnp.exp2(p[:1, HALF : HALF + 1] - 13.0)
 
 
-def slope_kernel(*refs):
-    halves, text, across = (refs[0:3], refs[3:6]), refs[6:9], refs[9]
-    scale_ref, bias_ref = refs[10:12]
-    send, slope, images, texts = refs[12:16]
-    scale, bias = scale_ref[0], bias_ref[0]
+def near_kernel(image, swapped, four, two, three, across, scalars, send, slope, images, texts):
     zeros = jnp.zeros((ROWS, WIDE - HALF), BF16)
     for s in range(8):
         rows = pl.ds(SLOT * s, ROWS)
-        for half, parts in enumerate(halves):
-            images[rows, WIDE * half : WIDE * (half + 1)] = parts[s // 3][s % 3]
-        a, b = (text[0][s], across[s]) if s < 4 else (text[1][s - 4], text[2][s - 4])
+        a, b = (four[s], across[s]) if s < 4 else (two[s - 4], three[s - 4])
         texts[rows, 0:WIDE] = jnp.concatenate([a[:, :QUART], b[:, :QUART], zeros], axis=1)
         texts[rows, WIDE:] = jnp.concatenate([a[:, QUART:HALF], b[:, QUART:HALF], zeros], axis=1)
-        rows = pl.ds(SLOT * s + ROWS, SLOT - ROWS)
-        images[rows, :] = jnp.zeros((SLOT - ROWS, 2 * WIDE), BF16)
-        texts[rows, :] = jnp.zeros((SLOT - ROWS, 2 * WIDE), BF16)
+        texts[pl.ds(SLOT * s + ROWS, SLOT - ROWS), :] = jnp.zeros((SLOT - ROWS, 2 * WIDE), BF16)
+    join_images(images, ((image, swapped),))
     own = lax.axis_index("h") == lax.axis_index("c")
+    slopes(scalars, slope, images, texts, own)
+    image_terms(slope, texts, 1, send)
+
+
+def far_kernel(below, below_swapped, above, above_swapped, texts, scalars, send, slope, images):
+    join_images(images, ((below, below_swapped), (above, above_swapped)))
+    slopes(scalars, slope, images, texts, None)
+    image_terms(slope, texts, 1, send)
+
+
+def join_images(images, parts):
+    s = 0
+    for part, swapped in parts:
+        for n in range(part.shape[0]):
+            images[pl.ds(SLOT * s, ROWS), 0:WIDE] = part[n]
+            images[pl.ds(SLOT * s, ROWS), WIDE:] = swapped[n]
+            images[pl.ds(SLOT * s + ROWS, SLOT - ROWS), :] = jnp.zeros((SLOT - ROWS, 2 * WIDE), BF16)
+            s += 1
+
+
+def slopes(scalars, slope, images, texts, own):
+    scale, bias = scalars[0:1, 0:1], scalars[8:9, 0:1]
     for j in range(3):
         cols = pl.ds(256 * j, 256)
         dots = lax.dot_general(
@@ -115,7 +134,7 @@
         )
         logit = scale * dots + bias
         value = jax.nn.sigmoid(logit)
-        if j == 0:
+        if j == 0 and own is not None:
             top = logit[:SLOT]
             row = lax.broadcasted_iota(jnp.int32, top.shape, 0)
             col = lax.broadcasted_iota(jnp.int32, top.shape, 1)
@@ -123,19 +142,21 @@
             top = jnp.where(paired, -jax.nn.sigmoid(-top), value[:SLOT])
             value = jnp.concatenate([top, value[SLOT:]], axis=0)
         slope[:, cols] = value.astype(BF16)
-    image_terms(slope, texts, 1, send)
 
 
 def image_terms(slope, texts, half, out):
     add = jnp.dot(slope[...], texts[:, WIDE * half : WIDE * (half + 1)], preferred_element_type=F32)
-    for s in range(8):
+    for s in range(out.shape[0]):
         out[s] = add[SLOT * s : SLOT * s + ROWS, :]
 
 
-def text_kernel(slope, images, texts, keep, own, two, three, *across):
+def text_kernel(slope, images, far_slope, far_images, texts, keep, far_keep, own, two, three, *across):
+    image_terms(far_slope, texts, 0, far_keep)
     image_terms(slope, texts, 0, keep)
     total = lax.dot_general(
         slope[...], images[...], (((0,), (0,)), ((), ())), preferred_element_type=F32
+    ) + lax.dot_general(
+        far_slope[...], far_images[...], (((0,), (0,)), ((), ())), preferred_element_type=F32
     )
     pad = jnp.zeros((ROWS, CODED - HALF), F32)
     for s in range(8):
@@ -151,13 +172,11 @@
                 across[s][...] = part if s == 0 else scaled(part)
 
 
-def image_first_kernel(keep, recv, own, below, above):
-    for s in range(8):
-        x = keep[s] + recv[s]
-        if s < 3:
-            own[s] = x
-        else:
-            (below, above)[s // 3 - 1][s % 3] = scaled(x)
+def image_first_kernel(keep, recv, far_keep, far_recv, own, below, above):
+    for s in range(5):
+        (below, above)[s // 3][s % 3] = scaled(far_keep[s] + far_recv[s])
+    for s in range(3):
+        own[s] = keep[s] + recv[s]
 
 
 def image_sum_kernel(own, from_above, from_below, kept, below, above):
@@ -180,11 +199,11 @@
 
 
 def last_kernel(*refs):
-    own, *parts, scale, keep, send = refs
+    own, *parts, scalars, keep, send = refs
     x = own[...]
     for part in parts:
         x = x + unscaled(part[...])
-    x = scale[0] * x
+    x = scalars[0:1, 0:1] * x
     keep[...] = x[:, :QUART]
     send[:, :QUART] = x[:, QUART:HALF]
     if send.shape[1] > QUART:
@@ -203,7 +222,6 @@
 
 
 def shards(image, text, scale, bias):
-    scale, bias = scale.reshape(1), bias.reshape(1)
     half = shape((ROWS, QUART), BF16)
     image_keep, image_send, text_keep, text_send = call(
         split_kernel, [half, shape((SLOT, WIDE), BF16), half, half], image, text, mib=4
@@ -217,39 +235,75 @@
     def stacked(*xs):
         return call(stack_kernel, [shape((len(xs), ROWS, WIDE), BF16)], *xs, mib=4)[0]
 
-    four = stacked(text, *(flip(text, "y", n) for n in (1, 2, 3)))
+    four, scalars = call(
+        first_stack_kernel,
+        [shape((4, ROWS, WIDE), BF16), shape((16, 128), F32)],
+        text,
+        *(flip(text, "y", n) for n in (1, 2, 3)),
+        scale.reshape(1),
+        bias.reshape(1),
+        smem=2,
+        mib=4,
+    )
     other = flip(text, "h", 1)
     other = [other] + [flip(other, "y", n) for n in (1, 2, 3)]
     texts = [four] + [flip(four, X, n) for n in (2, 3)]
     near = image, behind(image, "z", 3), behind(image, "z", -3)
     trio, duo, other = together(stacked(*near), stacked(*near[:2]), stacked(*other))
     images = [trio, behind(trio, "z", 1), behind(duo, "z", -1)]
-    *images, t0, t1, t2 = together(*images, *texts)
-    texts = [t0, t1, t2, other]
-    swapped = [flip(x, "c", 1) for x in images]
-
-    big, three, one = (shape((*d, ROWS, WIDE), F32) for d in ((8,), (3,), ()))
+    *images, four, two_x, three_x = together(*images, *texts)
+    swapped = [flip(x, "c", 1) for x in (trio, *images[1:])]
+
+    three, five, one = (shape((*d, ROWS, WIDE), F32) for d in ((3,), (5,), ()))
+    two = shape((2, ROWS, WIDE), F32)
     quad, coded = shape((4, ROWS, CODED), F32), shape((ROWS, CODED), F32)
-    two = shape((2, ROWS, WIDE), F32)
-    joined = shape((8 * SLOT, 2 * WIDE), BF16)
-    send, slope, images, texts = call(
-        slope_kernel,
-        [big, shape((8 * SLOT, 8 * SLOT), BF16), joined, joined],
-        *images,
-        *swapped,
-        *texts,
-        scale,
-        bias,
-        smem=2,
-        flops=3 * 704 * 704 * 1152,
+
+    def joined(n, lanes):
+        return shape((n * SLOT, lanes), BF16)
+
+    flops = 2 * 704 * 704 * 1152
+    send, slope, images_near, texts = call(
+        near_kernel,
+        [three, joined(3, 8 * SLOT), joined(3, 2 * WIDE), joined(8, 2 * WIDE)],
+        trio,
+        swapped[0],
+        four,
+        two_x,
+        three_x,
+        other,
+        scalars,
+        flops=flops // 2,
         mib=12,
     )
     recv = flip(send, "c", 1)
-    keep, text_own, *text_out = call(
-        text_kernel, [big] + [quad] * 3 + [coded] * 4, slope, images, texts, flops=3 * 704 * 704 * 1152, mib=12
+    send, far_slope, far_images = call(
+        far_kernel,
+        [five, joined(5, 8 * SLOT), joined(5, 2 * WIDE)],
+        images[1],
+        swapped[1],
+        images[2],
+        swapped[2],
+        texts,
+        scalars,
+        flops=flops,
+        mib=12,
+    )
+    far_recv = flip(send, "c", 1)
+    keep, far_keep, text_own, *text_out = call(
+        text_kernel,
+        [three, five] + [quad] * 3 + [coded] * 4,
+        slope,
+        images_near,
+        far_slope,
+        far_images,
+        texts,
+        flops=3 * flops // 2,
+        mib=12,
     )
     text_out, text_across, *across_out = text_out[:2], *text_out[2:]
-    image_own, below, above = call(image_first_kernel, [three, three, two], keep, recv, mib=12)
+    image_own, below, above = call(
+        image_first_kernel, [three, three, two], keep, recv, far_keep, far_recv, mib=12
+    )
     below, above, *text_out = together(below, above, *text_out)
 
     def moved(x, move, axis, n):
@@ -266,9 +320,9 @@
     text_in = [across] + [moved(x, flip, "y", n) for n, x in enumerate(text_out, 1)]
     image_in = [below, above]
     part, wider = shape((ROWS, QUART), F32), shape((ROWS, 512), F32)
-    image_keep, image_send = call(last_kernel, [part, wider], image_own, *image_in, scale, smem=1, mib=4)
+    image_keep, image_send = call(last_kernel, [part, wider], image_own, *image_in, scalars, mib=4)
     image_recv = flip(image_send, "h", 1)
-    text_keep, text_send = call(last_kernel, [part, part], text_own, *text_in, scale, smem=1, mib=4)
+    text_keep, text_send = call(last_kernel, [part, part], text_own, *text_in, scalars, mib=4)
     text_recv = flip(text_send, "c", 1)
     grads = [shape((2 * ROWS, QUART), F32)] * 2
     return tuple(call(place_kernel, grads, image_keep, image_recv, text_keep, text_recv, mib=4))

time: 86.5 us -> 84.3 us (0.975)
  waiting for transfers between devices: 23.7 us -> 19.4 us
  starting transfers between devices: 48 us -> 50.1 us
    ppermute x26 -> x27, waiting for transfers between devices: 10.1 us -> 7.22 us  [flip(): return lax.ppermute(x, axis, [(i, i ^ mask) for i in range(count)])]
    ppermute x8, waiting for transfers between devices: 13.6 us -> 12.2 us  [behind(): lax.ppermute(x, axis, [(i, (i + distance) % count) for i in range(count)])]
    ppermute x26 -> x27, starting transfers between devices: 31.2 us -> 32.3 us  [flip(): return lax.ppermute(x, axis, [(i, i ^ mask) for i in range(count)])]
    ppermute x8, starting transfers between devices: 16.8 us -> 17.8 us  [behind(): lax.ppermute(x, axis, [(i, (i + distance) % count) for i in range(count)])]
    pallas_call x16 -> x17, Pallas kernels: 9.86 us -> 9.84 us  [call(): pl.pallas_call(kernel, out_shape=outs, in_specs=[VMEM] * (len(args) - sme...]
  transfers between devices with their start and end apart: 34 -> 35, of which waited for: 13 -> 12; matrix products, arithmetic and copies ran while one was open for 1% -> 1% of each run, Pallas kernels for 6% -> 8%
where the time goes in v5:
time: 84.3 us; the launch traced here: 84.1 us
  starting transfers between devices  50.1 us (59%)
  waiting for transfers between devices  19.4 us (23%)
  Pallas kernels  9.84 us (12%)
  between operations  2.32 us (3%)
  local copies, waits for them, and re-layouts  1.8 us (2%)
    ppermute x27, starting transfers between devices, flip(): return lax.ppermute(x, axis, [(i, i ^ mask) for i in range(count)])  32.3 us
    ppermute x8, starting transfers between devices, behind(): lax.ppermute(x, axis, [(i, (i + distance) % count) for i in range(count)])  17.8 us
    ppermute x8, waiting for transfers between devices, behind(): lax.ppermute(x, axis, [(i, (i + distance) % count) for i in range(count)])  12.2 us
    pallas_call x17, Pallas kernels, call(): pl.pallas_call(kernel, out_shape=outs, in_specs=[VMEM] * (len(args) - sme...  9.84 us
    ppermute x27, waiting for transfers between devices, flip(): return lax.ppermute(x, axis, [(i, i ^ mask) for i in range(count)])  7.22 us
    unnamed x4, local copies, waits for them, and re-layouts  1.8 us
  transfers between devices with their start and end apart: 35, of which 12 were waited for; matrix products, arithmetic and copies ran while one was open for 1% of the time, Pallas kernels for 8%

profile of v5, /device:TPU:8, one launch (start us, length us, event | category | flops | bytes accessed | tf_op | source)
XLA Modules:
  0.0 84.1 jit_solution(14527013678315320648)
XLA Ops:
  2.6 3.1 %collective-permute-start = (bf16[96,640]{1,0:T(8,128)(2,1)S(1)}, bf16[96,640]{1,0:T(8,128)(2,1)S(1)}, u32[]{:S(2)}, u32[]{:S(2)}) collective-permute-start(bf16[96,640]{1,0:T(8,128)(2,1)S(1)} %get-tuple-element.51), channel_id=1, source_target_pairs={{0,2},{2,0},{1,3},{3,1},{4,6},{6,4},{5,7},{7,5},{8,10},{10,8},{9,1... | collective-permute-start | bytes 368648 | tf_op jit(solution)/shard_map/ppermute | solution.py:43
  5.8 1.7 %collective-permute-start.13 = (bf16[88,640]{1,0:T(8,128)(2,1)S(1)}, bf16[88,640]{1,0:T(8,128)(2,1)S(1)}, u32[]{:S(2)}, u32[]{:S(2)}) collective-permute-start(bf16[88,640]{1,0:T(8,128)(2,1)S(1)} %shard_map.63.text), channel_id=1, source_target_pairs={{0,192},{64,128},{128,64},{192,0},{1,193},{65,129},{129,65},{193,1... | collective-permute-start | bytes 337928 | tf_op jit(solution)/shard_map/ppermute | solution.py:43
  7.5 1.2 %collective-permute-start.4 = (bf16[88,640]{1,0:T(8,128)(2,1)S(1)}, bf16[88,640]{1,0:T(8,128)(2,1)S(1)}, u32[]{:S(2)}, u32[]{:S(2)}) collective-permute-start(bf16[88,640]{1,0:T(8,128)(2,1)S(1)} %shard_map.63.text), channel_id=1, source_target_pairs={{0,2},{2,0},{1,3},{3,1},{4,6},{6,4},{5,7},{7,5},{8,10},{10,8},{9,1... | collective-permute-start | bytes 337928 | tf_op jit(solution)/shard_map/ppermute | solution.py:43
  8.6 2.0 %collective-permute-start.12 = (bf16[88,640]{1,0:T(8,128)(2,1)S(1)}, bf16[88,640]{1,0:T(8,128)(2,1)S(1)}, u32[]{:S(2)}, u32[]{:S(2)}) collective-permute-start(bf16[88,640]{1,0:T(8,128)(2,1)S(1)} %shard_map.63.text), channel_id=1, source_target_pairs={{0,128},{64,192},{128,0},{192,64},{1,129},{65,193},{129,1},{193,65... | collective-permute-start | bytes 337928 | tf_op jit(solution)/shard_map/ppermute | solution.py:43
  11.3 6.8 %collective-permute-start.2 = (bf16[88,640]{1,0:T(8,128)(2,1)S(1)}, bf16[88,640]{1,0:T(8,128)(2,1)S(1)}, u32[]{:S(2)}, u32[]{:S(2)}) collective-permute-start(bf16[88,640]{1,0:T(8,128)(2,1)S(1)} %shard_map.60.refs_0_), channel_id=1, source_target_pairs={{0,40},{8,48},{16,56},{24,0},{32,8},{40,16},{48,24},{56,32},{1,41}... | collective-permute-start | bytes 337928 | tf_op jit(solution)/shard_map/ppermute | solution.py:48
  19.4 1.7 %collective-permute-start.7 = (bf16[88,640]{1,0:T(8,128)(2,1)S(1)}, bf16[88,640]{1,0:T(8,128)(2,1)S(1)}, u32[]{:S(2)}, u32[]{:S(2)}) collective-permute-start(bf16[88,640]{1,0:T(8,128)(2,1)S(1)} %collective-permute-done.4.refs_0_), channel_id=1, source_target_pairs={{0,192},{64,128},{128,64},{192,0},{1,193},{65,129},{129,65},{193,1... | collective-permute-start | bytes 337928 | tf_op jit(solution)/shard_map/ppermute | solution.py:43
  21.1 1.9 %collective-permute-start.6 = (bf16[88,640]{1,0:T(8,128)(2,1)S(1)}, bf16[88,640]{1,0:T(8,128)(2,1)S(1)}, u32[]{:S(2)}, u32[]{:S(2)}) collective-permute-start(bf16[88,640]{1,0:T(8,128)(2,1)S(1)} %collective-permute-done.4.refs_0_), channel_id=1, source_target_pairs={{0,128},{64,192},{128,0},{192,64},{1,129},{65,193},{129,1},{193,65... | collective-permute-start | bytes 337928 | tf_op jit(solution)/shard_map/ppermute | solution.py:43
  23.0 1.2 %collective-permute-start.5 = (bf16[88,640]{1,0:T(8,128)(2,1)S(1)}, bf16[88,640]{1,0:T(8,128)(2,1)S(1)}, u32[]{:S(2)}, u32[]{:S(2)}) collective-permute-start(bf16[88,640]{1,0:T(8,128)(2,1)S(1)} %collective-permute-done.4.refs_0_), channel_id=1, source_target_pairs={{0,64},{64,0},{128,192},{192,128},{1,65},{65,1},{129,193},{193,129... | collective-permute-start | bytes 337928 | tf_op jit(solution)/shard_map/ppermute | solution.py:43
  24.5 2.1 %collective-permute-start.15 = (bf16[4,88,640]{2,1,0:T(8,128)(2,1)S(1)}, bf16[4,88,640]{2,1,0:T(8,128)(2,1)S(1)}, u32[]{:S(2)}, u32[]{:S(2)}) collective-permute-start(bf16[4,88,640]{2,1,0:T(8,128)(2,1)S(1)} %get-tuple-element.57.four), channel_id=1, source_target_pairs={{0,6},{2,4},{4,2},{6,0},{1,7},{3,5},{5,3},{7,1},{8,14},{10,12},{12... | collective-permute-start | bytes 1351688 | tf_op jit(solution)/shard_map/ppermute | solution.py:43
  26.6 2.4 %collective-permute-done.1.refs_1_ = bf16[88,640]{1,0:T(8,128)(2,1)S(1)} collective-permute-done((bf16[88,640]{1,0:T(8,128)(2,1)S(1)}, bf16[88,640]{1,0:T(8,128)(2,1)S(1)}, u32[]{:S(2)}, u32[]{:S(2)}) %collective-permute-start.1) | collective-permute-done | bytes 112672 | tf_op jit(solution)/shard_map/ppermute | solution.py:48
  30.0 1.3 %collective-permute-start.9 = (bf16[3,88,640]{2,1,0:T(8,128)(2,1)S(1)}, bf16[3,88,640]{2,1,0:T(8,128)(2,1)S(1)}, u32[]{:S(2)}, u32[]{:S(2)}) collective-permute-start(bf16[3,88,640]{2,1,0:T(8,128)(2,1)S(1)} %shard_map.61.image), channel_id=1, source_target_pairs={{0,8},{8,16},{16,24},{24,32},{32,40},{40,48},{48,56},{56,0},{1,9},... | collective-permute-start | bytes 1013768 | tf_op jit(solution)/shard_map/ppermute | solution.py:48
  31.3 2.0 %collective-permute-start.10 = (bf16[2,88,640]{2,1,0:T(8,128)(2,1)S(1)}, bf16[2,88,640]{2,1,0:T(8,128)(2,1)S(1)}, u32[]{:S(2)}, u32[]{:S(2)}) collective-permute-start(bf16[2,88,640]{2,1,0:T(8,128)(2,1)S(1)} %shard_map.62), channel_id=1, source_target_pairs={{0,56},{8,0},{16,8},{24,16},{32,24},{40,32},{48,40},{56,48},{1,57}... | collective-permute-start | bytes 675848 | tf_op jit(solution)/shard_map/ppermute | solution.py:48
  33.3 4.0 %collective-permute-done.10.above = bf16[2,88,640]{2,1,0:T(8,128)(2,1)S(1)} collective-permute-done((bf16[2,88,640]{2,1,0:T(8,128)(2,1)S(1)}, bf16[2,88,640]{2,1,0:T(8,128)(2,1)S(1)}, u32[]{:S(2)}, u32[]{:S(2)}) %collective-permute-start.10) | collective-permute-done | bytes 225312 | tf_op jit(solution)/shard_map/ppermute | solution.py:48
  37.3 3.1 %collective-permute-done.9.below = bf16[3,88,640]{2,1,0:T(8,128)(2,1)S(1)} collective-permute-done((bf16[3,88,640]{2,1,0:T(8,128)(2,1)S(1)}, bf16[3,88,640]{2,1,0:T(8,128)(2,1)S(1)}, u32[]{:S(2)}, u32[]{:S(2)}) %collective-permute-start.9) | collective-permute-done | bytes 337952 | tf_op jit(solution)/shard_map/ppermute | solution.py:48
  41.3 1.4 %shard_map.66 = (f32[3,88,640]{2,1,0:T(8,128)S(1)}, bf16[288,768]{1,0:T(8,128)(2,1)S(1)}, bf16[288,1280]{1,0:T(8,128)(2,1)S(1)}, bf16[768,1280]{1,0:T(8,128)(2,1)S(1)}) custom-call(bf16[3,88,640]{2,1,0:T(8,128)(2,1)S(1)} %shard_map.61.image, bf16[3,88,640]{2,1,0:T(8,128)(2,1)S(1)} %collective-permute-done.8.swapped, ...), custom_call_target="tpu_custom_call" | custom-call | flops 570949632 | bytes 6307840 | tf_op jit(solution)/shard_map/pallas_call | solution.py:31
  42.7 1.9 %shard_map.67 = (f32[5,88,640]{2,1,0:T(8,128)S(1)}, bf16[480,768]{1,0:T(8,128)(2,1)S(1)}, bf16[480,1280]{1,0:T(8,128)(2,1)S(1)}) custom-call(bf16[3,88,640]{2,1,0:T(8,128)(2,1)S(1)} %collective-permute-done.9.below, bf16[3,88,640]{2,1,0:T(8,128)(2,1)S(1)} %collective-permute-done.16.below_swapped, bf16[2,88,640]{2,1,0:T(8,128)(2,1)S(1)} %collective-permute-done.10.above, ...), custom_call_target="tpu_custom_call" | custom-call | flops 1141899264 | bytes 6193152 | tf_op jit(solution)/shard_map/pallas_call | solution.py:31
  45.2 3.5 %shard_map.68 = (f32[3,88,640]{2,1,0:T(8,128)S(1)}, f32[5,88,640]{2,1,0:T(8,128)S(1)}, f32[4,88,577]{2,1,0:T(8,128)S(1)}, f32[4,88,577]{2,1,0:T(8,128)S(1)}, f32...) custom-call(bf16[288,768]{1,0:T(8,128)(2,1)S(1)} %get-tuple-element., ...), custom_call_target="tpu_custom_call" | custom-call | flops 1712848896 | bytes 10163712 | tf_op jit(solution)/shard_map/pallas_call | solution.py:31
  49.4 1.9 %collective-permute-start.21 = (f16[2,88,640]{2,1,0:T(8,128)(2,1)S(1)}, f16[2,88,640]{2,1,0:T(8,128)(2,1)S(1)}, u32[]{:S(2)}, u32[]{:S(2)}) collective-permute-start(f16[2,88,640]{2,1,0:T(8,128)(2,1)S(1)} %convert_element_type.80), channel_id=1, source_target_pairs={{0,8},{8,16},{16,24},{24,32},{32,40},{40,48},{48,56},{56,0},{1,9},... | collective-permute-start | bytes 675848 | tf_op jit(solution)/shard_map/ppermute | solution.py:48
  51.3 2.2 %collective-permute-start.26 = (f16[4,88,577]{2,1,0:T(8,128)(2,1)S(1)}, f16[4,88,577]{2,1,0:T(8,128)(2,1)S(1)}, u32[]{:S(2)}, u32[]{:S(2)}) collective-permute-start(f16[4,88,577]{2,1,0:T(8,128)(2,1)S(1)} %convert_element_type.88), channel_id=1, source_target_pairs={{0,6},{2,4},{4,2},{6,0},{1,7},{3,5},{5,3},{7,1},{8,14},{10,12},{12... | collective-permute-start | bytes 1218632 | tf_op jit(solution)/shard_map/ppermute | solution.py:43
  53.9 1.7 %collective-permute-start.29 = (f16[88,577]{1,0:T(8,128)(2,1)S(1)}, f16[88,577]{1,0:T(8,128)(2,1)S(1)}, u32[]{:S(2)}, u32[]{:S(2)}) collective-permute-start(f16[88,577]{1,0:T(8,128)(2,1)S(1)} %convert_element_type.94), channel_id=1, source_target_pairs={{0,192},{64,128},{128,64},{192,0},{1,193},{65,129},{129,65},{193,1... | collective-permute-start | bytes 304664 | tf_op jit(solution)/shard_map/ppermute | solution.py:43
  55.6 2.4 %collective-permute-done.21 = f16[2,88,640]{2,1,0:T(8,128)(2,1)S(1)} collective-permute-done((f16[2,88,640]{2,1,0:T(8,128)(2,1)S(1)}, f16[2,88,640]{2,1,0:T(8,128)(2,1)S(1)}, u32[]{:S(2)}, u32[]{:S(2)}) %collective-permute-start.21) | collective-permute-done | bytes 225312 | tf_op jit(solution)/shard_map/ppermute | solution.py:48
  58.1 1.7 %collective-permute-start.28 = (f16[88,577]{1,0:T(8,128)(2,1)S(1)}, f16[88,577]{1,0:T(8,128)(2,1)S(1)}, u32[]{:S(2)}, u32[]{:S(2)}) collective-permute-start(f16[88,577]{1,0:T(8,128)(2,1)S(1)} %convert_element_type.92), channel_id=1, source_target_pairs={{0,128},{64,192},{128,0},{192,64},{1,129},{65,193},{129,1},{193,65... | collective-permute-start | bytes 304664 | tf_op jit(solution)/shard_map/ppermute | solution.py:43
  60.3 2.1 %collective-permute-start.23 = (f16[88,640]{1,0:T(8,128)(2,1)S(1)}, f16[88,640]{1,0:T(8,128)(2,1)S(1)}, u32[]{:S(2)}, u32[]{:S(2)}) collective-permute-start(f16[88,640]{1,0:T(8,128)(2,1)S(1)} %convert_element_type.84), channel_id=1, source_target_pairs={{0,24},{8,32},{16,40},{24,48},{32,56},{40,0},{48,8},{56,16},{1,25}... | collective-permute-start | bytes 337928 | tf_op jit(solution)/shard_map/ppermute | solution.py:48
  63.4 0.9 %collective-permute-done.28 = f16[88,577]{1,0:T(8,128)(2,1)S(1)} collective-permute-done((f16[88,577]{1,0:T(8,128)(2,1)S(1)}, f16[88,577]{1,0:T(8,128)(2,1)S(1)}, u32[]{:S(2)}, u32[]{:S(2)}) %collective-permute-start.28) | collective-permute-done | bytes 101584 | tf_op jit(solution)/shard_map/ppermute | solution.py:43
  64.3 3.4 %collective-permute-start.22 = (f16[88,640]{1,0:T(8,128)(2,1)S(1)}, f16[88,640]{1,0:T(8,128)(2,1)S(1)}, u32[]{:S(2)}, u32[]{:S(2)}) collective-permute-start(f16[88,640]{1,0:T(8,128)(2,1)S(1)} %convert_element_type.82), channel_id=1, source_target_pairs={{0,40},{8,48},{16,56},{24,0},{32,8},{40,16},{48,24},{56,32},{1,41}... | collective-permute-start | bytes 337928 | tf_op jit(solution)/shard_map/ppermute | solution.py:48
  68.2 2.8 %collective-permute-start.30 = (f16[88,577]{1,0:T(8,128)(2,1)S(1)}, f16[88,577]{1,0:T(8,128)(2,1)S(1)}, u32[]{:S(2)}, u32[]{:S(2)}) collective-permute-start(f16[88,577]{1,0:T(8,128)(2,1)S(1)} %convert_element_type.96), channel_id=1, source_target_pairs={{0,2},{2,0},{1,3},{3,1},{4,6},{6,4},{5,7},{7,5},{8,10},{10,8},{9,1... | collective-permute-start | bytes 304664 | tf_op jit(solution)/shard_map/ppermute | solution.py:43
  72.2 2.3 %collective-permute-start.32 = (f16[88,577]{1,0:T(8,128)(2,1)S(1)}, f16[88,577]{1,0:T(8,128)(2,1)S(1)}, u32[]{:S(2)}, u32[]{:S(2)}) collective-permute-start(f16[88,577]{1,0:T(8,128)(2,1)S(1)} %convert_element_type.100), channel_id=1, source_target_pairs={{0,128},{64,192},{128,0},{192,64},{1,129},{65,193},{129,1},{193,65... | collective-permute-start | bytes 304664 | tf_op jit(solution)/shard_map/ppermute | solution.py:43
  74.5 1.4 %collective-permute-start.31 = (f16[88,577]{1,0:T(8,128)(2,1)S(1)}, f16[88,577]{1,0:T(8,128)(2,1)S(1)}, u32[]{:S(2)}, u32[]{:S(2)}) collective-permute-start(f16[88,577]{1,0:T(8,128)(2,1)S(1)} %convert_element_type.98), channel_id=1, source_target_pairs={{0,64},{64,0},{128,192},{192,128},{1,65},{65,1},{129,193},{193,129... | collective-permute-start | bytes 304664 | tf_op jit(solution)/shard_map/ppermute | solution.py:43
  77.1 1.4 %collective-permute-done.32 = f16[88,577]{1,0:T(8,128)(2,1)S(1)} collective-permute-done((f16[88,577]{1,0:T(8,128)(2,1)S(1)}, f16[88,577]{1,0:T(8,128)(2,1)S(1)}, u32[]{:S(2)}, u32[]{:S(2)}) %collective-permute-start.32) | collective-permute-done | bytes 101584 | tf_op jit(solution)/shard_map/ppermute | solution.py:43
  78.5 1.3 %collective-permute-done.31 = f16[88,577]{1,0:T(8,128)(2,1)S(1)} collective-permute-done((f16[88,577]{1,0:T(8,128)(2,1)S(1)}, f16[88,577]{1,0:T(8,128)(2,1)S(1)}, u32[]{:S(2)}, u32[]{:S(2)}) %collective-permute-start.31) | collective-permute-done | bytes 101584 | tf_op jit(solution)/shard_map/ppermute | solution.py:43
  80.2 1.3 %collective-permute-done.34.text_recv = f32[88,288]{1,0:T(8,128)S(1)} collective-permute-done((f32[88,288]{1,0:T(8,128)S(1)}, f32[88,288]{1,0:T(8,128)S(1)}, u32[]{:S(2)}, u32[]{:S(2)}) %collective-permute-start.34) | collective-permute-done | bytes 101408 | tf_op jit(solution)/shard_map/ppermute | solution.py:43
  81.6 1.7 %collective-permute-done.24.image_recv = f32[88,512]{1,0:T(8,128)S(1)} collective-permute-done((f32[88,512]{1,0:T(8,128)S(1)}, f32[88,512]{1,0:T(8,128)S(1)}, u32[]{:S(2)}, u32[]{:S(2)}) %collective-permute-start.24) | collective-permute-done | bytes 180256 | tf_op jit(solution)/shard_map/ppermute | solution.py:43
  (85 shorter events, 12.0 us)
Async XLA Ops:
  2.5 3.2 %collective-permute-start.3 = (bf16[88,288]{1,0:T(8,128)(2,1)S(1)}, bf16[88,288]{1,0:T(8,128)(2,1)S(1)}, u32[]{:S(2)}, u32[]{:S(2)}) collective-permute-start(bf16[88,288]{1,0:T(8,128)(2,1)S(1)} %get-tuple-element.53), channel_id=1, source_target_pairs={{0,1},{1,0},{2,3},{3,2},{4,5},{5,4},{6,7},{7,6},{8,9},{9,8},{10,11... | collective-permute-start | bytes 152072 | tf_op jit(solution)/shard_map/ppermute | solution.py:43
  2.6 8.5 %collective-permute-start = (bf16[96,640]{1,0:T(8,128)(2,1)S(1)}, bf16[96,640]{1,0:T(8,128)(2,1)S(1)}, u32[]{:S(2)}, u32[]{:S(2)}) collective-permute-start(bf16[96,640]{1,0:T(8,128)(2,1)S(1)} %get-tuple-element.51), channel_id=1, source_target_pairs={{0,2},{2,0},{1,3},{3,1},{4,6},{6,4},{5,7},{7,5},{8,10},{10,8},{9,1... | collective-permute-start | bytes 368648 | tf_op jit(solution)/shard_map/ppermute | solution.py:43
  5.8 12.3 %collective-permute-start.13 = (bf16[88,640]{1,0:T(8,128)(2,1)S(1)}, bf16[88,640]{1,0:T(8,128)(2,1)S(1)}, u32[]{:S(2)}, u32[]{:S(2)}) collective-permute-start(bf16[88,640]{1,0:T(8,128)(2,1)S(1)} %shard_map.63.text), channel_id=1, source_target_pairs={{0,192},{64,128},{128,64},{192,0},{1,193},{65,129},{129,65},{193,1... | collective-permute-start | bytes 337928 | tf_op jit(solution)/shard_map/ppermute | solution.py:43
  7.5 11.9 %collective-permute-start.4 = (bf16[88,640]{1,0:T(8,128)(2,1)S(1)}, bf16[88,640]{1,0:T(8,128)(2,1)S(1)}, u32[]{:S(2)}, u32[]{:S(2)}) collective-permute-start(bf16[88,640]{1,0:T(8,128)(2,1)S(1)} %shard_map.63.text), channel_id=1, source_target_pairs={{0,2},{2,0},{1,3},{3,1},{4,6},{6,4},{5,7},{7,5},{8,10},{10,8},{9,1... | collective-permute-start | bytes 337928 | tf_op jit(solution)/shard_map/ppermute | solution.py:43
  8.6 12.4 %collective-permute-start.12 = (bf16[88,640]{1,0:T(8,128)(2,1)S(1)}, bf16[88,640]{1,0:T(8,128)(2,1)S(1)}, u32[]{:S(2)}, u32[]{:S(2)}) collective-permute-start(bf16[88,640]{1,0:T(8,128)(2,1)S(1)} %shard_map.63.text), channel_id=1, source_target_pairs={{0,128},{64,192},{128,0},{192,64},{1,129},{65,193},{129,1},{193,65... | collective-permute-start | bytes 337928 | tf_op jit(solution)/shard_map/ppermute | solution.py:43
  10.7 12.3 %collective-permute-start.11 = (bf16[88,640]{1,0:T(8,128)(2,1)S(1)}, bf16[88,640]{1,0:T(8,128)(2,1)S(1)}, u32[]{:S(2)}, u32[]{:S(2)}) collective-permute-start(bf16[88,640]{1,0:T(8,128)(2,1)S(1)} %shard_map.63.text), channel_id=1, source_target_pairs={{0,64},{64,0},{128,192},{192,128},{1,65},{65,1},{129,193},{193,129... | collective-permute-start | bytes 337928 | tf_op jit(solution)/shard_map/ppermute | solution.py:43
  11.3 13.2 %collective-permute-start.2 = (bf16[88,640]{1,0:T(8,128)(2,1)S(1)}, bf16[88,640]{1,0:T(8,128)(2,1)S(1)}, u32[]{:S(2)}, u32[]{:S(2)}) collective-permute-start(bf16[88,640]{1,0:T(8,128)(2,1)S(1)} %shard_map.60.refs_0_), channel_id=1, source_target_pairs={{0,40},{8,48},{16,56},{24,0},{32,8},{40,16},{48,24},{56,32},{1,41}... | collective-permute-start | bytes 337928 | tf_op jit(solution)/shard_map/ppermute | solution.py:48
  18.1 10.9 %collective-permute-start.1 = (bf16[88,640]{1,0:T(8,128)(2,1)S(1)}, bf16[88,640]{1,0:T(8,128)(2,1)S(1)}, u32[]{:S(2)}, u32[]{:S(2)}) collective-permute-start(bf16[88,640]{1,0:T(8,128)(2,1)S(1)} %shard_map.60.refs_0_), channel_id=1, source_target_pairs={{0,24},{8,32},{16,40},{24,48},{32,56},{40,0},{48,8},{56,16},{1,25}... | collective-permute-start | bytes 337928 | tf_op jit(solution)/shard_map/ppermute | solution.py:48
  19.4 10.5 %collective-permute-start.7 = (bf16[88,640]{1,0:T(8,128)(2,1)S(1)}, bf16[88,640]{1,0:T(8,128)(2,1)S(1)}, u32[]{:S(2)}, u32[]{:S(2)}) collective-permute-start(bf16[88,640]{1,0:T(8,128)(2,1)S(1)} %collective-permute-done.4.refs_0_), channel_id=1, source_target_pairs={{0,192},{64,128},{128,64},{192,0},{1,193},{65,129},{129,65},{193,1... | collective-permute-start | bytes 337928 | tf_op jit(solution)/shard_map/ppermute | solution.py:43
  21.1 8.8 %collective-permute-start.6 = (bf16[88,640]{1,0:T(8,128)(2,1)S(1)}, bf16[88,640]{1,0:T(8,128)(2,1)S(1)}, u32[]{:S(2)}, u32[]{:S(2)}) collective-permute-start(bf16[88,640]{1,0:T(8,128)(2,1)S(1)} %collective-permute-done.4.refs_0_), channel_id=1, source_target_pairs={{0,128},{64,192},{128,0},{192,64},{1,129},{65,193},{129,1},{193,65... | collective-permute-start | bytes 337928 | tf_op jit(solution)/shard_map/ppermute | solution.py:43
  23.0 6.9 %collective-permute-start.5 = (bf16[88,640]{1,0:T(8,128)(2,1)S(1)}, bf16[88,640]{1,0:T(8,128)(2,1)S(1)}, u32[]{:S(2)}, u32[]{:S(2)}) collective-permute-start(bf16[88,640]{1,0:T(8,128)(2,1)S(1)} %collective-permute-done.4.refs_0_), channel_id=1, source_target_pairs={{0,64},{64,0},{128,192},{192,128},{1,65},{65,1},{129,193},{193,129... | collective-permute-start | bytes 337928 | tf_op jit(solution)/shard_map/ppermute | solution.py:43
  24.5 15.8 %collective-permute-start.15 = (bf16[4,88,640]{2,1,0:T(8,128)(2,1)S(1)}, bf16[4,88,640]{2,1,0:T(8,128)(2,1)S(1)}, u32[]{:S(2)}, u32[]{:S(2)}) collective-permute-start(bf16[4,88,640]{2,1,0:T(8,128)(2,1)S(1)} %get-tuple-element.57.four), channel_id=1, source_target_pairs={{0,6},{2,4},{4,2},{6,0},{1,7},{3,5},{5,3},{7,1},{8,14},{10,12},{12... | collective-permute-start | bytes 1351688 | tf_op jit(solution)/shard_map/ppermute | solution.py:43
  29.0 11.7 %collective-permute-start.14 = (bf16[4,88,640]{2,1,0:T(8,128)(2,1)S(1)}, bf16[4,88,640]{2,1,0:T(8,128)(2,1)S(1)}, u32[]{:S(2)}, u32[]{:S(2)}) collective-permute-start(bf16[4,88,640]{2,1,0:T(8,128)(2,1)S(1)} %get-tuple-element.57.four), channel_id=1, source_target_pairs={{0,4},{2,6},{4,0},{6,2},{1,5},{3,7},{5,1},{7,3},{8,12},{10,14},{12... | collective-permute-start | bytes 1351688 | tf_op jit(solution)/shard_map/ppermute | solution.py:43
  30.0 10.3 %collective-permute-start.9 = (bf16[3,88,640]{2,1,0:T(8,128)(2,1)S(1)}, bf16[3,88,640]{2,1,0:T(8,128)(2,1)S(1)}, u32[]{:S(2)}, u32[]{:S(2)}) collective-permute-start(bf16[3,88,640]{2,1,0:T(8,128)(2,1)S(1)} %shard_map.61.image), channel_id=1, source_target_pairs={{0,8},{8,16},{16,24},{24,32},{32,40},{40,48},{48,56},{56,0},{1,9},... | collective-permute-start | bytes 1013768 | tf_op jit(solution)/shard_map/ppermute | solution.py:48
  31.3 6.0 %collective-permute-start.10 = (bf16[2,88,640]{2,1,0:T(8,128)(2,1)S(1)}, bf16[2,88,640]{2,1,0:T(8,128)(2,1)S(1)}, u32[]{:S(2)}, u32[]{:S(2)}) collective-permute-start(bf16[2,88,640]{2,1,0:T(8,128)(2,1)S(1)} %shard_map.62), channel_id=1, source_target_pairs={{0,56},{8,0},{16,8},{24,16},{32,24},{40,32},{48,40},{56,48},{1,57}... | collective-permute-start | bytes 675848 | tf_op jit(solution)/shard_map/ppermute | solution.py:48
  33.3 8.0 %collective-permute-start.8 = (bf16[3,88,640]{2,1,0:T(8,128)(2,1)S(1)}, bf16[3,88,640]{2,1,0:T(8,128)(2,1)S(1)}, u32[]{:S(2)}, u32[]{:S(2)}) collective-permute-start(bf16[3,88,640]{2,1,0:T(8,128)(2,1)S(1)} %shard_map.61.image), channel_id=1, source_target_pairs={{0,1},{1,0},{2,3},{3,2},{4,5},{5,4},{6,7},{7,6},{8,9},{9,8},{10,11... | collective-permute-start | bytes 1013768 | tf_op jit(solution)/shard_map/ppermute | solution.py:43
  44.6 4.1 %collective-permute-start.19 = (f32[5,88,640]{2,1,0:T(8,128)S(1)}, f32[5,88,640]{2,1,0:T(8,128)S(1)}, u32[]{:S(2)}, u32[]{:S(2)}) collective-permute-start(f32[5,88,640]{2,1,0:T(8,128)S(1)} %get-tuple-element.72), channel_id=1, source_target_pairs={{0,1},{1,0},{2,3},{3,2},{4,5},{5,4},{6,7},{7,6},{8,9},{9,8},{10,11... | collective-permute-start | bytes 3379208 | tf_op jit(solution)/shard_map/ppermute | solution.py:43
  44.8 3.8 %collective-permute-start.18 = (f32[3,88,640]{2,1,0:T(8,128)S(1)}, f32[3,88,640]{2,1,0:T(8,128)S(1)}, u32[]{:S(2)}, u32[]{:S(2)}) collective-permute-start(f32[3,88,640]{2,1,0:T(8,128)S(1)} %get-tuple-element.70), channel_id=1, source_target_pairs={{0,1},{1,0},{2,3},{3,2},{4,5},{5,4},{6,7},{7,6},{8,9},{9,8},{10,11... | collective-permute-start | bytes 2027528 | tf_op jit(solution)/shard_map/ppermute | solution.py:43
  49.1 10.8 %collective-permute-start.20 = (f16[3,88,640]{2,1,0:T(8,128)(2,1)S(1)}, f16[3,88,640]{2,1,0:T(8,128)(2,1)S(1)}, u32[]{:S(2)}, u32[]{:S(2)}) collective-permute-start(f16[3,88,640]{2,1,0:T(8,128)(2,1)S(1)} %convert_element_type.78), channel_id=1, source_target_pairs={{0,56},{8,0},{16,8},{24,16},{32,24},{40,32},{48,40},{56,48},{1,57}... | collective-permute-start | bytes 1013768 | tf_op jit(solution)/shard_map/ppermute | solution.py:48
  49.4 8.7 %collective-permute-start.21 = (f16[2,88,640]{2,1,0:T(8,128)(2,1)S(1)}, f16[2,88,640]{2,1,0:T(8,128)(2,1)S(1)}, u32[]{:S(2)}, u32[]{:S(2)}) collective-permute-start(f16[2,88,640]{2,1,0:T(8,128)(2,1)S(1)} %convert_element_type.80), channel_id=1, source_target_pairs={{0,8},{8,16},{16,24},{24,32},{32,40},{40,48},{48,56},{56,0},{1,9},... | collective-permute-start | bytes 675848 | tf_op jit(solution)/shard_map/ppermute | solution.py:48
  51.3 19.6 %collective-permute-start.26 = (f16[4,88,577]{2,1,0:T(8,128)(2,1)S(1)}, f16[4,88,577]{2,1,0:T(8,128)(2,1)S(1)}, u32[]{:S(2)}, u32[]{:S(2)}) collective-permute-start(f16[4,88,577]{2,1,0:T(8,128)(2,1)S(1)} %convert_element_type.88), channel_id=1, source_target_pairs={{0,6},{2,4},{4,2},{6,0},{1,7},{3,5},{5,3},{7,1},{8,14},{10,12},{12... | collective-permute-start | bytes 1218632 | tf_op jit(solution)/shard_map/ppermute | solution.py:43
  53.6 17.5 %collective-permute-start.25 = (f16[4,88,577]{2,1,0:T(8,128)(2,1)S(1)}, f16[4,88,577]{2,1,0:T(8,128)(2,1)S(1)}, u32[]{:S(2)}, u32[]{:S(2)}) collective-permute-start(f16[4,88,577]{2,1,0:T(8,128)(2,1)S(1)} %convert_element_type.86), channel_id=1, source_target_pairs={{0,4},{2,6},{4,0},{6,2},{1,5},{3,7},{5,1},{7,3},{8,12},{10,14},{12... | collective-permute-start | bytes 1218632 | tf_op jit(solution)/shard_map/ppermute | solution.py:43
  53.9 8.5 %collective-permute-start.29 = (f16[88,577]{1,0:T(8,128)(2,1)S(1)}, f16[88,577]{1,0:T(8,128)(2,1)S(1)}, u32[]{:S(2)}, u32[]{:S(2)}) collective-permute-start(f16[88,577]{1,0:T(8,128)(2,1)S(1)} %convert_element_type.94), channel_id=1, source_target_pairs={{0,192},{64,128},{128,64},{192,0},{1,193},{65,129},{129,65},{193,1... | collective-permute-start | bytes 304664 | tf_op jit(solution)/shard_map/ppermute | solution.py:43
  58.1 6.3 %collective-permute-start.28 = (f16[88,577]{1,0:T(8,128)(2,1)S(1)}, f16[88,577]{1,0:T(8,128)(2,1)S(1)}, u32[]{:S(2)}, u32[]{:S(2)}) collective-permute-start(f16[88,577]{1,0:T(8,128)(2,1)S(1)} %convert_element_type.92), channel_id=1, source_target_pairs={{0,128},{64,192},{128,0},{192,64},{1,129},{65,193},{129,1},{193,65... | collective-permute-start | bytes 304664 | tf_op jit(solution)/shard_map/ppermute | solution.py:43
  60.3 14.2 %collective-permute-start.23 = (f16[88,640]{1,0:T(8,128)(2,1)S(1)}, f16[88,640]{1,0:T(8,128)(2,1)S(1)}, u32[]{:S(2)}, u32[]{:S(2)}) collective-permute-start(f16[88,640]{1,0:T(8,128)(2,1)S(1)} %convert_element_type.84), channel_id=1, source_target_pairs={{0,24},{8,32},{16,40},{24,48},{32,56},{40,0},{48,8},{56,16},{1,25}... | collective-permute-start | bytes 337928 | tf_op jit(solution)/shard_map/ppermute | solution.py:48
  62.4 5.4 %collective-permute-start.27 = (f16[88,577]{1,0:T(8,128)(2,1)S(1)}, f16[88,577]{1,0:T(8,128)(2,1)S(1)}, u32[]{:S(2)}, u32[]{:S(2)}) collective-permute-start(f16[88,577]{1,0:T(8,128)(2,1)S(1)} %convert_element_type.90), channel_id=1, source_target_pairs={{0,64},{64,0},{128,192},{192,128},{1,65},{65,1},{129,193},{193,129... | collective-permute-start | bytes 304664 | tf_op jit(solution)/shard_map/ppermute | solution.py:43
  64.3 11.6 %collective-permute-start.22 = (f16[88,640]{1,0:T(8,128)(2,1)S(1)}, f16[88,640]{1,0:T(8,128)(2,1)S(1)}, u32[]{:S(2)}, u32[]{:S(2)}) collective-permute-start(f16[88,640]{1,0:T(8,128)(2,1)S(1)} %convert_element_type.82), channel_id=1, source_target_pairs={{0,40},{8,48},{16,56},{24,0},{32,8},{40,16},{48,24},{56,32},{1,41}... | collective-permute-start | bytes 337928 | tf_op jit(solution)/shard_map/ppermute | solution.py:48
  68.2 8.9 %collective-permute-start.30 = (f16[88,577]{1,0:T(8,128)(2,1)S(1)}, f16[88,577]{1,0:T(8,128)(2,1)S(1)}, u32[]{:S(2)}, u32[]{:S(2)}) collective-permute-start(f16[88,577]{1,0:T(8,128)(2,1)S(1)} %convert_element_type.96), channel_id=1, source_target_pairs={{0,2},{2,0},{1,3},{3,1},{4,6},{6,4},{5,7},{7,5},{8,10},{10,8},{9,1... | collective-permute-start | bytes 304664 | tf_op jit(solution)/shard_map/ppermute | solution.py:43
  71.6 5.5 %collective-permute-start.33 = (f16[88,577]{1,0:T(8,128)(2,1)S(1)}, f16[88,577]{1,0:T(8,128)(2,1)S(1)}, u32[]{:S(2)}, u32[]{:S(2)}) collective-permute-start(f16[88,577]{1,0:T(8,128)(2,1)S(1)} %convert_element_type.102), channel_id=1, source_target_pairs={{0,192},{64,128},{128,64},{192,0},{1,193},{65,129},{129,65},{193,1... | collective-permute-start | bytes 304664 | tf_op jit(solution)/shard_map/ppermute | solution.py:43
  72.2 6.4 %collective-permute-start.32 = (f16[88,577]{1,0:T(8,128)(2,1)S(1)}, f16[88,577]{1,0:T(8,128)(2,1)S(1)}, u32[]{:S(2)}, u32[]{:S(2)}) collective-permute-start(f16[88,577]{1,0:T(8,128)(2,1)S(1)} %convert_element_type.100), channel_id=1, source_target_pairs={{0,128},{64,192},{128,0},{192,64},{1,129},{65,193},{129,1},{193,65... | collective-permute-start | bytes 304664 | tf_op jit(solution)/shard_map/ppermute | solution.py:43
  74.5 5.4 %collective-permute-start.31 = (f16[88,577]{1,0:T(8,128)(2,1)S(1)}, f16[88,577]{1,0:T(8,128)(2,1)S(1)}, u32[]{:S(2)}, u32[]{:S(2)}) collective-permute-start(f16[88,577]{1,0:T(8,128)(2,1)S(1)} %convert_element_type.98), channel_id=1, source_target_pairs={{0,64},{64,0},{128,192},{192,128},{1,65},{65,1},{129,193},{193,129... | collective-permute-start | bytes 304664 | tf_op jit(solution)/shard_map/ppermute | solution.py:43
  76.2 7.1 %collective-permute-start.24 = (f32[88,512]{1,0:T(8,128)S(1)}, f32[88,512]{1,0:T(8,128)S(1)}, u32[]{:S(2)}, u32[]{:S(2)}) collective-permute-start(f32[88,512]{1,0:T(8,128)S(1)} %get-tuple-element.84), channel_id=1, source_target_pairs={{0,2},{2,0},{1,3},{3,1},{4,6},{6,4},{5,7},{7,5},{8,10},{10,8},{9,1... | collective-permute-start | bytes 540680 | tf_op jit(solution)/shard_map/ppermute | solution.py:43
  (5 other events, 7.2 us)

commit v6 on v5

--- a/solution.py
+++ b/solution.py
@@ -64,7 +64,6 @@
         sent = jnp.where(low, second, first)
         if send is image_send:
             sent = jnp.concatenate([sent, jnp.zeros((ROWS, WIDE - QUART), F32)], axis=1)
-            sent = jnp.concatenate([sent, jnp.zeros((SLOT - ROWS, WIDE), F32)], axis=0)
         send[...] = sent.astype(BF16)
 
 
@@ -224,7 +223,7 @@
 def shards(image, text, scale, bias):
     half = shape((ROWS, QUART), BF16)
     image_keep, image_send, text_keep, text_send = call(
-        split_kernel, [half, shape((SLOT, WIDE), BF16), half, half], image, text, mib=4
+        split_kernel, [half, shape((ROWS, WIDE), BF16), half, half], image, text, mib=4
     )
     image_recv = flip(image_send, "h", 1)
     text_recv = flip(text_send, "c", 1)
@@ -304,7 +303,6 @@
     image_own, below, above = call(
         image_first_kernel, [three, three, two], keep, recv, far_keep, far_recv, mib=12
     )
-    below, above, *text_out = together(below, above, *text_out)
 
     def moved(x, move, axis, n):
         return move(x.astype(F16), axis, n).astype(F32)

time: 84.3 us -> 84.3 us (level)
  no operation moved by 1% of the time
where the time goes in v6:
time: 84.3 us; the launch traced here: 84.1 us
  starting transfers between devices  50.1 us (59%)
  waiting for transfers between devices  19.4 us (23%)
  Pallas kernels  9.84 us (12%)
  between operations  2.32 us (3%)
  local copies, waits for them, and re-layouts  1.8 us (2%)
    ppermute x27, starting transfers between devices, flip(): return lax.ppermute(x, axis, [(i, i ^ mask) for i in range(count)])  32.3 us
    ppermute x8, starting transfers between devices, behind(): lax.ppermute(x, axis, [(i, (i + distance) % count) for i in range(count)])  17.8 us
    ppermute x8, waiting for transfers between devices, behind(): lax.ppermute(x, axis, [(i, (i + distance) % count) for i in range(count)])  12.2 us
    pallas_call x17, Pallas kernels, call(): pl.pallas_call(kernel, out_shape=outs, in_specs=[VMEM] * (len(args) - sme...  9.84 us
    ppermute x27, waiting for transfers between devices, flip(): return lax.ppermute(x, axis, [(i, i ^ mask) for i in range(count)])  7.22 us
    unnamed x4, local copies, waits for them, and re-layouts  1.8 us
  transfers between devices with their start and end apart: 35, of which 12 were waited for; matrix products, arithmetic and copies ran while one was open for 1% of the time, Pallas kernels for 8%

profile of v6, /device:TPU:8, one launch (start us, length us, event | category | flops | bytes accessed | tf_op | source)
XLA Modules:
  0.0 84.1 jit_solution(10134501657606623482)
XLA Ops:
  2.6 3.1 %collective-permute-start = (bf16[88,640]{1,0:T(8,128)(2,1)S(1)}, bf16[88,640]{1,0:T(8,128)(2,1)S(1)}, u32[]{:S(2)}, u32[]{:S(2)}) collective-permute-start(bf16[88,640]{1,0:T(8,128)(2,1)S(1)} %get-tuple-element.47), channel_id=1, source_target_pairs={{0,2},{2,0},{1,3},{3,1},{4,6},{6,4},{5,7},{7,5},{8,10},{10,8},{9,1... | collective-permute-start | bytes 337928 | tf_op jit(solution)/shard_map/ppermute | solution.py:43
  5.8 1.7 %collective-permute-start.13 = (bf16[88,640]{1,0:T(8,128)(2,1)S(1)}, bf16[88,640]{1,0:T(8,128)(2,1)S(1)}, u32[]{:S(2)}, u32[]{:S(2)}) collective-permute-start(bf16[88,640]{1,0:T(8,128)(2,1)S(1)} %shard_map.63.text), channel_id=1, source_target_pairs={{0,192},{64,128},{128,64},{192,0},{1,193},{65,129},{129,65},{193,1... | collective-permute-start | bytes 337928 | tf_op jit(solution)/shard_map/ppermute | solution.py:43
  7.5 1.2 %collective-permute-start.4 = (bf16[88,640]{1,0:T(8,128)(2,1)S(1)}, bf16[88,640]{1,0:T(8,128)(2,1)S(1)}, u32[]{:S(2)}, u32[]{:S(2)}) collective-permute-start(bf16[88,640]{1,0:T(8,128)(2,1)S(1)} %shard_map.63.text), channel_id=1, source_target_pairs={{0,2},{2,0},{1,3},{3,1},{4,6},{6,4},{5,7},{7,5},{8,10},{10,8},{9,1... | collective-permute-start | bytes 337928 | tf_op jit(solution)/shard_map/ppermute | solution.py:43
  8.6 2.0 %collective-permute-start.12 = (bf16[88,640]{1,0:T(8,128)(2,1)S(1)}, bf16[88,640]{1,0:T(8,128)(2,1)S(1)}, u32[]{:S(2)}, u32[]{:S(2)}) collective-permute-start(bf16[88,640]{1,0:T(8,128)(2,1)S(1)} %shard_map.63.text), channel_id=1, source_target_pairs={{0,128},{64,192},{128,0},{192,64},{1,129},{65,193},{129,1},{193,65... | collective-permute-start | bytes 337928 | tf_op jit(solution)/shard_map/ppermute | solution.py:43
  11.3 6.8 %collective-permute-start.2 = (bf16[88,640]{1,0:T(8,128)(2,1)S(1)}, bf16[88,640]{1,0:T(8,128)(2,1)S(1)}, u32[]{:S(2)}, u32[]{:S(2)}) collective-permute-start(bf16[88,640]{1,0:T(8,128)(2,1)S(1)} %shard_map.60.refs_0_), channel_id=1, source_target_pairs={{0,40},{8,48},{16,56},{24,0},{32,8},{40,16},{48,24},{56,32},{1,41}... | collective-permute-start | bytes 337928 | tf_op jit(solution)/shard_map/ppermute | solution.py:48
  19.4 1.7 %collective-permute-start.7 = (bf16[88,640]{1,0:T(8,128)(2,1)S(1)}, bf16[88,640]{1,0:T(8,128)(2,1)S(1)}, u32[]{:S(2)}, u32[]{:S(2)}) collective-permute-start(bf16[88,640]{1,0:T(8,128)(2,1)S(1)} %collective-permute-done.4.refs_0_), channel_id=1, source_target_pairs={{0,192},{64,128},{128,64},{192,0},{1,193},{65,129},{129,65},{193,1... | collective-permute-start | bytes 337928 | tf_op jit(solution)/shard_map/ppermute | solution.py:43
  21.1 1.9 %collective-permute-start.6 = (bf16[88,640]{1,0:T(8,128)(2,1)S(1)}, bf16[88,640]{1,0:T(8,128)(2,1)S(1)}, u32[]{:S(2)}, u32[]{:S(2)}) collective-permute-start(bf16[88,640]{1,0:T(8,128)(2,1)S(1)} %collective-permute-done.4.refs_0_), channel_id=1, source_target_pairs={{0,128},{64,192},{128,0},{192,64},{1,129},{65,193},{129,1},{193,65... | collective-permute-start | bytes 337928 | tf_op jit(solution)/shard_map/ppermute | solution.py:43
  23.0 1.2 %collective-permute-start.5 = (bf16[88,640]{1,0:T(8,128)(2,1)S(1)}, bf16[88,640]{1,0:T(8,128)(2,1)S(1)}, u32[]{:S(2)}, u32[]{:S(2)}) collective-permute-start(bf16[88,640]{1,0:T(8,128)(2,1)S(1)} %collective-permute-done.4.refs_0_), channel_id=1, source_target_pairs={{0,64},{64,0},{128,192},{192,128},{1,65},{65,1},{129,193},{193,129... | collective-permute-start | bytes 337928 | tf_op jit(solution)/shard_map/ppermute | solution.py:43
  24.5 2.1 %collective-permute-start.15 = (bf16[4,88,640]{2,1,0:T(8,128)(2,1)S(1)}, bf16[4,88,640]{2,1,0:T(8,128)(2,1)S(1)}, u32[]{:S(2)}, u32[]{:S(2)}) collective-permute-start(bf16[4,88,640]{2,1,0:T(8,128)(2,1)S(1)} %get-tuple-element.53.four), channel_id=1, source_target_pairs={{0,6},{2,4},{4,2},{6,0},{1,7},{3,5},{5,3},{7,1},{8,14},{10,12},{12... | collective-permute-start | bytes 1351688 | tf_op jit(solution)/shard_map/ppermute | solution.py:43
  26.6 2.4 %collective-permute-done.1.refs_1_ = bf16[88,640]{1,0:T(8,128)(2,1)S(1)} collective-permute-done((bf16[88,640]{1,0:T(8,128)(2,1)S(1)}, bf16[88,640]{1,0:T(8,128)(2,1)S(1)}, u32[]{:S(2)}, u32[]{:S(2)}) %collective-permute-start.1) | collective-permute-done | bytes 112672 | tf_op jit(solution)/shard_map/ppermute | solution.py:48
  30.0 1.3 %collective-permute-start.9 = (bf16[3,88,640]{2,1,0:T(8,128)(2,1)S(1)}, bf16[3,88,640]{2,1,0:T(8,128)(2,1)S(1)}, u32[]{:S(2)}, u32[]{:S(2)}) collective-permute-start(bf16[3,88,640]{2,1,0:T(8,128)(2,1)S(1)} %shard_map.61.image), channel_id=1, source_target_pairs={{0,8},{8,16},{16,24},{24,32},{32,40},{40,48},{48,56},{56,0},{1,9},... | collective-permute-start | bytes 1013768 | tf_op jit(solution)/shard_map/ppermute | solution.py:48
  31.3 2.0 %collective-permute-start.10 = (bf16[2,88,640]{2,1,0:T(8,128)(2,1)S(1)}, bf16[2,88,640]{2,1,0:T(8,128)(2,1)S(1)}, u32[]{:S(2)}, u32[]{:S(2)}) collective-permute-start(bf16[2,88,640]{2,1,0:T(8,128)(2,1)S(1)} %shard_map.62), channel_id=1, source_target_pairs={{0,56},{8,0},{16,8},{24,16},{32,24},{40,32},{48,40},{56,48},{1,57}... | collective-permute-start | bytes 675848 | tf_op jit(solution)/shard_map/ppermute | solution.py:48
  33.3 4.0 %collective-permute-done.10.above = bf16[2,88,640]{2,1,0:T(8,128)(2,1)S(1)} collective-permute-done((bf16[2,88,640]{2,1,0:T(8,128)(2,1)S(1)}, bf16[2,88,640]{2,1,0:T(8,128)(2,1)S(1)}, u32[]{:S(2)}, u32[]{:S(2)}) %collective-permute-start.10) | collective-permute-done | bytes 225312 | tf_op jit(solution)/shard_map/ppermute | solution.py:48
  37.3 3.1 %collective-permute-done.9.below = bf16[3,88,640]{2,1,0:T(8,128)(2,1)S(1)} collective-permute-done((bf16[3,88,640]{2,1,0:T(8,128)(2,1)S(1)}, bf16[3,88,640]{2,1,0:T(8,128)(2,1)S(1)}, u32[]{:S(2)}, u32[]{:S(2)}) %collective-permute-start.9) | collective-permute-done | bytes 337952 | tf_op jit(solution)/shard_map/ppermute | solution.py:48
  41.3 1.4 %shard_map.66 = (f32[3,88,640]{2,1,0:T(8,128)S(1)}, bf16[288,768]{1,0:T(8,128)(2,1)S(1)}, bf16[288,1280]{1,0:T(8,128)(2,1)S(1)}, bf16[768,1280]{1,0:T(8,128)(2,1)S(1)}) custom-call(bf16[3,88,640]{2,1,0:T(8,128)(2,1)S(1)} %shard_map.61.image, bf16[3,88,640]{2,1,0:T(8,128)(2,1)S(1)} %collective-permute-done.8.swapped, ...), custom_call_target="tpu_custom_call" | custom-call | flops 570949632 | bytes 6307840 | tf_op jit(solution)/shard_map/pallas_call | solution.py:31
  42.7 1.9 %shard_map.67 = (f32[5,88,640]{2,1,0:T(8,128)S(1)}, bf16[480,768]{1,0:T(8,128)(2,1)S(1)}, bf16[480,1280]{1,0:T(8,128)(2,1)S(1)}) custom-call(bf16[3,88,640]{2,1,0:T(8,128)(2,1)S(1)} %collective-permute-done.9.below, bf16[3,88,640]{2,1,0:T(8,128)(2,1)S(1)} %collective-permute-done.16.below_swapped, bf16[2,88,640]{2,1,0:T(8,128)(2,1)S(1)} %collective-permute-done.10.above, ...), custom_call_target="tpu_custom_call" | custom-call | flops 1141899264 | bytes 6193152 | tf_op jit(solution)/shard_map/pallas_call | solution.py:31
  45.2 3.5 %shard_map.68 = (f32[3,88,640]{2,1,0:T(8,128)S(1)}, f32[5,88,640]{2,1,0:T(8,128)S(1)}, f32[4,88,577]{2,1,0:T(8,128)S(1)}, f32[4,88,577]{2,1,0:T(8,128)S(1)}, f32...) custom-call(bf16[288,768]{1,0:T(8,128)(2,1)S(1)} %get-tuple-element., ...), custom_call_target="tpu_custom_call" | custom-call | flops 1712848896 | bytes 10163712 | tf_op jit(solution)/shard_map/pallas_call | solution.py:31
  49.4 1.9 %collective-permute-start.21 = (f16[2,88,640]{2,1,0:T(8,128)(2,1)S(1)}, f16[2,88,640]{2,1,0:T(8,128)(2,1)S(1)}, u32[]{:S(2)}, u32[]{:S(2)}) collective-permute-start(f16[2,88,640]{2,1,0:T(8,128)(2,1)S(1)} %convert_element_type.80), channel_id=1, source_target_pairs={{0,8},{8,16},{16,24},{24,32},{32,40},{40,48},{48,56},{56,0},{1,9},... | collective-permute-start | bytes 675848 | tf_op jit(solution)/shard_map/ppermute | solution.py:48
  51.3 2.2 %collective-permute-start.26 = (f16[4,88,577]{2,1,0:T(8,128)(2,1)S(1)}, f16[4,88,577]{2,1,0:T(8,128)(2,1)S(1)}, u32[]{:S(2)}, u32[]{:S(2)}) collective-permute-start(f16[4,88,577]{2,1,0:T(8,128)(2,1)S(1)} %convert_element_type.88), channel_id=1, source_target_pairs={{0,6},{2,4},{4,2},{6,0},{1,7},{3,5},{5,3},{7,1},{8,14},{10,12},{12... | collective-permute-start | bytes 1218632 | tf_op jit(solution)/shard_map/ppermute | solution.py:43
  53.9 1.7 %collective-permute-start.29 = (f16[88,577]{1,0:T(8,128)(2,1)S(1)}, f16[88,577]{1,0:T(8,128)(2,1)S(1)}, u32[]{:S(2)}, u32[]{:S(2)}) collective-permute-start(f16[88,577]{1,0:T(8,128)(2,1)S(1)} %convert_element_type.94), channel_id=1, source_target_pairs={{0,192},{64,128},{128,64},{192,0},{1,193},{65,129},{129,65},{193,1... | collective-permute-start | bytes 304664 | tf_op jit(solution)/shard_map/ppermute | solution.py:43
  55.6 2.4 %collective-permute-done.21 = f16[2,88,640]{2,1,0:T(8,128)(2,1)S(1)} collective-permute-done((f16[2,88,640]{2,1,0:T(8,128)(2,1)S(1)}, f16[2,88,640]{2,1,0:T(8,128)(2,1)S(1)}, u32[]{:S(2)}, u32[]{:S(2)}) %collective-permute-start.21) | collective-permute-done | bytes 225312 | tf_op jit(solution)/shard_map/ppermute | solution.py:48
  58.1 1.7 %collective-permute-start.28 = (f16[88,577]{1,0:T(8,128)(2,1)S(1)}, f16[88,577]{1,0:T(8,128)(2,1)S(1)}, u32[]{:S(2)}, u32[]{:S(2)}) collective-permute-start(f16[88,577]{1,0:T(8,128)(2,1)S(1)} %convert_element_type.92), channel_id=1, source_target_pairs={{0,128},{64,192},{128,0},{192,64},{1,129},{65,193},{129,1},{193,65... | collective-permute-start | bytes 304664 | tf_op jit(solution)/shard_map/ppermute | solution.py:43
  60.3 2.1 %collective-permute-start.23 = (f16[88,640]{1,0:T(8,128)(2,1)S(1)}, f16[88,640]{1,0:T(8,128)(2,1)S(1)}, u32[]{:S(2)}, u32[]{:S(2)}) collective-permute-start(f16[88,640]{1,0:T(8,128)(2,1)S(1)} %convert_element_type.84), channel_id=1, source_target_pairs={{0,24},{8,32},{16,40},{24,48},{32,56},{40,0},{48,8},{56,16},{1,25}... | collective-permute-start | bytes 337928 | tf_op jit(solution)/shard_map/ppermute | solution.py:48
  63.4 0.9 %collective-permute-done.28 = f16[88,577]{1,0:T(8,128)(2,1)S(1)} collective-permute-done((f16[88,577]{1,0:T(8,128)(2,1)S(1)}, f16[88,577]{1,0:T(8,128)(2,1)S(1)}, u32[]{:S(2)}, u32[]{:S(2)}) %collective-permute-start.28) | collective-permute-done | bytes 101584 | tf_op jit(solution)/shard_map/ppermute | solution.py:43
  64.3 3.4 %collective-permute-start.22 = (f16[88,640]{1,0:T(8,128)(2,1)S(1)}, f16[88,640]{1,0:T(8,128)(2,1)S(1)}, u32[]{:S(2)}, u32[]{:S(2)}) collective-permute-start(f16[88,640]{1,0:T(8,128)(2,1)S(1)} %convert_element_type.82), channel_id=1, source_target_pairs={{0,40},{8,48},{16,56},{24,0},{32,8},{40,16},{48,24},{56,32},{1,41}... | collective-permute-start | bytes 337928 | tf_op jit(solution)/shard_map/ppermute | solution.py:48
  68.2 2.8 %collective-permute-start.30 = (f16[88,577]{1,0:T(8,128)(2,1)S(1)}, f16[88,577]{1,0:T(8,128)(2,1)S(1)}, u32[]{:S(2)}, u32[]{:S(2)}) collective-permute-start(f16[88,577]{1,0:T(8,128)(2,1)S(1)} %convert_element_type.96), channel_id=1, source_target_pairs={{0,2},{2,0},{1,3},{3,1},{4,6},{6,4},{5,7},{7,5},{8,10},{10,8},{9,1... | collective-permute-start | bytes 304664 | tf_op jit(solution)/shard_map/ppermute | solution.py:43
  72.2 2.3 %collective-permute-start.32 = (f16[88,577]{1,0:T(8,128)(2,1)S(1)}, f16[88,577]{1,0:T(8,128)(2,1)S(1)}, u32[]{:S(2)}, u32[]{:S(2)}) collective-permute-start(f16[88,577]{1,0:T(8,128)(2,1)S(1)} %convert_element_type.100), channel_id=1, source_target_pairs={{0,128},{64,192},{128,0},{192,64},{1,129},{65,193},{129,1},{193,65... | collective-permute-start | bytes 304664 | tf_op jit(solution)/shard_map/ppermute | solution.py:43
  74.5 1.4 %collective-permute-start.31 = (f16[88,577]{1,0:T(8,128)(2,1)S(1)}, f16[88,577]{1,0:T(8,128)(2,1)S(1)}, u32[]{:S(2)}, u32[]{:S(2)}) collective-permute-start(f16[88,577]{1,0:T(8,128)(2,1)S(1)} %convert_element_type.98), channel_id=1, source_target_pairs={{0,64},{64,0},{128,192},{192,128},{1,65},{65,1},{129,193},{193,129... | collective-permute-start | bytes 304664 | tf_op jit(solution)/shard_map/ppermute | solution.py:43
  77.1 1.4 %collective-permute-done.32 = f16[88,577]{1,0:T(8,128)(2,1)S(1)} collective-permute-done((f16[88,577]{1,0:T(8,128)(2,1)S(1)}, f16[88,577]{1,0:T(8,128)(2,1)S(1)}, u32[]{:S(2)}, u32[]{:S(2)}) %collective-permute-start.32) | collective-permute-done | bytes 101584 | tf_op jit(solution)/shard_map/ppermute | solution.py:43
  78.5 1.3 %collective-permute-done.31 = f16[88,577]{1,0:T(8,128)(2,1)S(1)} collective-permute-done((f16[88,577]{1,0:T(8,128)(2,1)S(1)}, f16[88,577]{1,0:T(8,128)(2,1)S(1)}, u32[]{:S(2)}, u32[]{:S(2)}) %collective-permute-start.31) | collective-permute-done | bytes 101584 | tf_op jit(solution)/shard_map/ppermute | solution.py:43
  80.2 1.3 %collective-permute-done.34.text_recv = f32[88,288]{1,0:T(8,128)S(1)} collective-permute-done((f32[88,288]{1,0:T(8,128)S(1)}, f32[88,288]{1,0:T(8,128)S(1)}, u32[]{:S(2)}, u32[]{:S(2)}) %collective-permute-start.34) | collective-permute-done | bytes 101408 | tf_op jit(solution)/shard_map/ppermute | solution.py:43
  81.6 1.7 %collective-permute-done.24.image_recv = f32[88,512]{1,0:T(8,128)S(1)} collective-permute-done((f32[88,512]{1,0:T(8,128)S(1)}, f32[88,512]{1,0:T(8,128)S(1)}, u32[]{:S(2)}, u32[]{:S(2)}) %collective-permute-start.24) | collective-permute-done | bytes 180256 | tf_op jit(solution)/shard_map/ppermute | solution.py:43
  (85 shorter events, 12.0 us)
Async XLA Ops:
  2.5 3.2 %collective-permute-start.3 = (bf16[88,288]{1,0:T(8,128)(2,1)S(1)}, bf16[88,288]{1,0:T(8,128)(2,1)S(1)}, u32[]{:S(2)}, u32[]{:S(2)}) collective-permute-start(bf16[88,288]{1,0:T(8,128)(2,1)S(1)} %get-tuple-element.49), channel_id=1, source_target_pairs={{0,1},{1,0},{2,3},{3,2},{4,5},{5,4},{6,7},{7,6},{8,9},{9,8},{10,11... | collective-permute-start | bytes 152072 | tf_op jit(solution)/shard_map/ppermute | solution.py:43
  2.6 8.5 %collective-permute-start = (bf16[88,640]{1,0:T(8,128)(2,1)S(1)}, bf16[88,640]{1,0:T(8,128)(2,1)S(1)}, u32[]{:S(2)}, u32[]{:S(2)}) collective-permute-start(bf16[88,640]{1,0:T(8,128)(2,1)S(1)} %get-tuple-element.47), channel_id=1, source_target_pairs={{0,2},{2,0},{1,3},{3,1},{4,6},{6,4},{5,7},{7,5},{8,10},{10,8},{9,1... | collective-permute-start | bytes 337928 | tf_op jit(solution)/shard_map/ppermute | solution.py:43
  5.8 12.3 %collective-permute-start.13 = (bf16[88,640]{1,0:T(8,128)(2,1)S(1)}, bf16[88,640]{1,0:T(8,128)(2,1)S(1)}, u32[]{:S(2)}, u32[]{:S(2)}) collective-permute-start(bf16[88,640]{1,0:T(8,128)(2,1)S(1)} %shard_map.63.text), channel_id=1, source_target_pairs={{0,192},{64,128},{128,64},{192,0},{1,193},{65,129},{129,65},{193,1... | collective-permute-start | bytes 337928 | tf_op jit(solution)/shard_map/ppermute | solution.py:43
  7.5 11.9 %collective-permute-start.4 = (bf16[88,640]{1,0:T(8,128)(2,1)S(1)}, bf16[88,640]{1,0:T(8,128)(2,1)S(1)}, u32[]{:S(2)}, u32[]{:S(2)}) collective-permute-start(bf16[88,640]{1,0:T(8,128)(2,1)S(1)} %shard_map.63.text), channel_id=1, source_target_pairs={{0,2},{2,0},{1,3},{3,1},{4,6},{6,4},{5,7},{7,5},{8,10},{10,8},{9,1... | collective-permute-start | bytes 337928 | tf_op jit(solution)/shard_map/ppermute | solution.py:43
  8.6 12.4 %collective-permute-start.12 = (bf16[88,640]{1,0:T(8,128)(2,1)S(1)}, bf16[88,640]{1,0:T(8,128)(2,1)S(1)}, u32[]{:S(2)}, u32[]{:S(2)}) collective-permute-start(bf16[88,640]{1,0:T(8,128)(2,1)S(1)} %shard_map.63.text), channel_id=1, source_target_pairs={{0,128},{64,192},{128,0},{192,64},{1,129},{65,193},{129,1},{193,65... | collective-permute-start | bytes 337928 | tf_op jit(solution)/shard_map/ppermute | solution.py:43
  10.7 12.3 %collective-permute-start.11 = (bf16[88,640]{1,0:T(8,128)(2,1)S(1)}, bf16[88,640]{1,0:T(8,128)(2,1)S(1)}, u32[]{:S(2)}, u32[]{:S(2)}) collective-permute-start(bf16[88,640]{1,0:T(8,128)(2,1)S(1)} %shard_map.63.text), channel_id=1, source_target_pairs={{0,64},{64,0},{128,192},{192,128},{1,65},{65,1},{129,193},{193,129... | collective-permute-start | bytes 337928 | tf_op jit(solution)/shard_map/ppermute | solution.py:43
  11.3 13.2 %collective-permute-start.2 = (bf16[88,640]{1,0:T(8,128)(2,1)S(1)}, bf16[88,640]{1,0:T(8,128)(2,1)S(1)}, u32[]{:S(2)}, u32[]{:S(2)}) collective-permute-start(bf16[88,640]{1,0:T(8,128)(2,1)S(1)} %shard_map.60.refs_0_), channel_id=1, source_target_pairs={{0,40},{8,48},{16,56},{24,0},{32,8},{40,16},{48,24},{56,32},{1,41}... | collective-permute-start | bytes 337928 | tf_op jit(solution)/shard_map/ppermute | solution.py:48
  18.1 10.9 %collective-permute-start.1 = (bf16[88,640]{1,0:T(8,128)(2,1)S(1)}, bf16[88,640]{1,0:T(8,128)(2,1)S(1)}, u32[]{:S(2)}, u32[]{:S(2)}) collective-permute-start(bf16[88,640]{1,0:T(8,128)(2,1)S(1)} %shard_map.60.refs_0_), channel_id=1, source_target_pairs={{0,24},{8,32},{16,40},{24,48},{32,56},{40,0},{48,8},{56,16},{1,25}... | collective-permute-start | bytes 337928 | tf_op jit(solution)/shard_map/ppermute | solution.py:48
  19.4 10.5 %collective-permute-start.7 = (bf16[88,640]{1,0:T(8,128)(2,1)S(1)}, bf16[88,640]{1,0:T(8,128)(2,1)S(1)}, u32[]{:S(2)}, u32[]{:S(2)}) collective-permute-start(bf16[88,640]{1,0:T(8,128)(2,1)S(1)} %collective-permute-done.4.refs_0_), channel_id=1, source_target_pairs={{0,192},{64,128},{128,64},{192,0},{1,193},{65,129},{129,65},{193,1... | collective-permute-start | bytes 337928 | tf_op jit(solution)/shard_map/ppermute | solution.py:43
  21.1 8.8 %collective-permute-start.6 = (bf16[88,640]{1,0:T(8,128)(2,1)S(1)}, bf16[88,640]{1,0:T(8,128)(2,1)S(1)}, u32[]{:S(2)}, u32[]{:S(2)}) collective-permute-start(bf16[88,640]{1,0:T(8,128)(2,1)S(1)} %collective-permute-done.4.refs_0_), channel_id=1, source_target_pairs={{0,128},{64,192},{128,0},{192,64},{1,129},{65,193},{129,1},{193,65... | collective-permute-start | bytes 337928 | tf_op jit(solution)/shard_map/ppermute | solution.py:43
  23.0 6.9 %collective-permute-start.5 = (bf16[88,640]{1,0:T(8,128)(2,1)S(1)}, bf16[88,640]{1,0:T(8,128)(2,1)S(1)}, u32[]{:S(2)}, u32[]{:S(2)}) collective-permute-start(bf16[88,640]{1,0:T(8,128)(2,1)S(1)} %collective-permute-done.4.refs_0_), channel_id=1, source_target_pairs={{0,64},{64,0},{128,192},{192,128},{1,65},{65,1},{129,193},{193,129... | collective-permute-start | bytes 337928 | tf_op jit(solution)/shard_map/ppermute | solution.py:43
  24.5 15.8 %collective-permute-start.15 = (bf16[4,88,640]{2,1,0:T(8,128)(2,1)S(1)}, bf16[4,88,640]{2,1,0:T(8,128)(2,1)S(1)}, u32[]{:S(2)}, u32[]{:S(2)}) collective-permute-start(bf16[4,88,640]{2,1,0:T(8,128)(2,1)S(1)} %get-tuple-element.53.four), channel_id=1, source_target_pairs={{0,6},{2,4},{4,2},{6,0},{1,7},{3,5},{5,3},{7,1},{8,14},{10,12},{12... | collective-permute-start | bytes 1351688 | tf_op jit(solution)/shard_map/ppermute | solution.py:43
  29.0 11.7 %collective-permute-start.14 = (bf16[4,88,640]{2,1,0:T(8,128)(2,1)S(1)}, bf16[4,88,640]{2,1,0:T(8,128)(2,1)S(1)}, u32[]{:S(2)}, u32[]{:S(2)}) collective-permute-start(bf16[4,88,640]{2,1,0:T(8,128)(2,1)S(1)} %get-tuple-element.53.four), channel_id=1, source_target_pairs={{0,4},{2,6},{4,0},{6,2},{1,5},{3,7},{5,1},{7,3},{8,12},{10,14},{12... | collective-permute-start | bytes 1351688 | tf_op jit(solution)/shard_map/ppermute | solution.py:43
  30.0 10.3 %collective-permute-start.9 = (bf16[3,88,640]{2,1,0:T(8,128)(2,1)S(1)}, bf16[3,88,640]{2,1,0:T(8,128)(2,1)S(1)}, u32[]{:S(2)}, u32[]{:S(2)}) collective-permute-start(bf16[3,88,640]{2,1,0:T(8,128)(2,1)S(1)} %shard_map.61.image), channel_id=1, source_target_pairs={{0,8},{8,16},{16,24},{24,32},{32,40},{40,48},{48,56},{56,0},{1,9},... | collective-permute-start | bytes 1013768 | tf_op jit(solution)/shard_map/ppermute | solution.py:48
  31.3 6.0 %collective-permute-start.10 = (bf16[2,88,640]{2,1,0:T(8,128)(2,1)S(1)}, bf16[2,88,640]{2,1,0:T(8,128)(2,1)S(1)}, u32[]{:S(2)}, u32[]{:S(2)}) collective-permute-start(bf16[2,88,640]{2,1,0:T(8,128)(2,1)S(1)} %shard_map.62), channel_id=1, source_target_pairs={{0,56},{8,0},{16,8},{24,16},{32,24},{40,32},{48,40},{56,48},{1,57}... | collective-permute-start | bytes 675848 | tf_op jit(solution)/shard_map/ppermute | solution.py:48
  33.3 8.0 %collective-permute-start.8 = (bf16[3,88,640]{2,1,0:T(8,128)(2,1)S(1)}, bf16[3,88,640]{2,1,0:T(8,128)(2,1)S(1)}, u32[]{:S(2)}, u32[]{:S(2)}) collective-permute-start(bf16[3,88,640]{2,1,0:T(8,128)(2,1)S(1)} %shard_map.61.image), channel_id=1, source_target_pairs={{0,1},{1,0},{2,3},{3,2},{4,5},{5,4},{6,7},{7,6},{8,9},{9,8},{10,11... | collective-permute-start | bytes 1013768 | tf_op jit(solution)/shard_map/ppermute | solution.py:43
  44.6 4.1 %collective-permute-start.19 = (f32[5,88,640]{2,1,0:T(8,128)S(1)}, f32[5,88,640]{2,1,0:T(8,128)S(1)}, u32[]{:S(2)}, u32[]{:S(2)}) collective-permute-start(f32[5,88,640]{2,1,0:T(8,128)S(1)} %get-tuple-element.68), channel_id=1, source_target_pairs={{0,1},{1,0},{2,3},{3,2},{4,5},{5,4},{6,7},{7,6},{8,9},{9,8},{10,11... | collective-permute-start | bytes 3379208 | tf_op jit(solution)/shard_map/ppermute | solution.py:43
  44.8 3.8 %collective-permute-start.18 = (f32[3,88,640]{2,1,0:T(8,128)S(1)}, f32[3,88,640]{2,1,0:T(8,128)S(1)}, u32[]{:S(2)}, u32[]{:S(2)}) collective-permute-start(f32[3,88,640]{2,1,0:T(8,128)S(1)} %get-tuple-element.66), channel_id=1, source_target_pairs={{0,1},{1,0},{2,3},{3,2},{4,5},{5,4},{6,7},{7,6},{8,9},{9,8},{10,11... | collective-permute-start | bytes 2027528 | tf_op jit(solution)/shard_map/ppermute | solution.py:43
  49.1 10.8 %collective-permute-start.20 = (f16[3,88,640]{2,1,0:T(8,128)(2,1)S(1)}, f16[3,88,640]{2,1,0:T(8,128)(2,1)S(1)}, u32[]{:S(2)}, u32[]{:S(2)}) collective-permute-start(f16[3,88,640]{2,1,0:T(8,128)(2,1)S(1)} %convert_element_type.78), channel_id=1, source_target_pairs={{0,56},{8,0},{16,8},{24,16},{32,24},{40,32},{48,40},{56,48},{1,57}... | collective-permute-start | bytes 1013768 | tf_op jit(solution)/shard_map/ppermute | solution.py:48
  49.4 8.7 %collective-permute-start.21 = (f16[2,88,640]{2,1,0:T(8,128)(2,1)S(1)}, f16[2,88,640]{2,1,0:T(8,128)(2,1)S(1)}, u32[]{:S(2)}, u32[]{:S(2)}) collective-permute-start(f16[2,88,640]{2,1,0:T(8,128)(2,1)S(1)} %convert_element_type.80), channel_id=1, source_target_pairs={{0,8},{8,16},{16,24},{24,32},{32,40},{40,48},{48,56},{56,0},{1,9},... | collective-permute-start | bytes 675848 | tf_op jit(solution)/shard_map/ppermute | solution.py:48
  51.3 19.6 %collective-permute-start.26 = (f16[4,88,577]{2,1,0:T(8,128)(2,1)S(1)}, f16[4,88,577]{2,1,0:T(8,128)(2,1)S(1)}, u32[]{:S(2)}, u32[]{:S(2)}) collective-permute-start(f16[4,88,577]{2,1,0:T(8,128)(2,1)S(1)} %convert_element_type.88), channel_id=1, source_target_pairs={{0,6},{2,4},{4,2},{6,0},{1,7},{3,5},{5,3},{7,1},{8,14},{10,12},{12... | collective-permute-start | bytes 1218632 | tf_op jit(solution)/shard_map/ppermute | solution.py:43
  53.6 17.5 %collective-permute-start.25 = (f16[4,88,577]{2,1,0:T(8,128)(2,1)S(1)}, f16[4,88,577]{2,1,0:T(8,128)(2,1)S(1)}, u32[]{:S(2)}, u32[]{:S(2)}) collective-permute-start(f16[4,88,577]{2,1,0:T(8,128)(2,1)S(1)} %convert_element_type.86), channel_id=1, source_target_pairs={{0,4},{2,6},{4,0},{6,2},{1,5},{3,7},{5,1},{7,3},{8,12},{10,14},{12... | collective-permute-start | bytes 1218632 | tf_op jit(solution)/shard_map/ppermute | solution.py:43
  53.9 8.5 %collective-permute-start.29 = (f16[88,577]{1,0:T(8,128)(2,1)S(1)}, f16[88,577]{1,0:T(8,128)(2,1)S(1)}, u32[]{:S(2)}, u32[]{:S(2)}) collective-permute-start(f16[88,577]{1,0:T(8,128)(2,1)S(1)} %convert_element_type.94), channel_id=1, source_target_pairs={{0,192},{64,128},{128,64},{192,0},{1,193},{65,129},{129,65},{193,1... | collective-permute-start | bytes 304664 | tf_op jit(solution)/shard_map/ppermute | solution.py:43
  58.1 6.3 %collective-permute-start.28 = (f16[88,577]{1,0:T(8,128)(2,1)S(1)}, f16[88,577]{1,0:T(8,128)(2,1)S(1)}, u32[]{:S(2)}, u32[]{:S(2)}) collective-permute-start(f16[88,577]{1,0:T(8,128)(2,1)S(1)} %convert_element_type.92), channel_id=1, source_target_pairs={{0,128},{64,192},{128,0},{192,64},{1,129},{65,193},{129,1},{193,65... | collective-permute-start | bytes 304664 | tf_op jit(solution)/shard_map/ppermute | solution.py:43
  60.3 14.2 %collective-permute-start.23 = (f16[88,640]{1,0:T(8,128)(2,1)S(1)}, f16[88,640]{1,0:T(8,128)(2,1)S(1)}, u32[]{:S(2)}, u32[]{:S(2)}) collective-permute-start(f16[88,640]{1,0:T(8,128)(2,1)S(1)} %convert_element_type.84), channel_id=1, source_target_pairs={{0,24},{8,32},{16,40},{24,48},{32,56},{40,0},{48,8},{56,16},{1,25}... | collective-permute-start | bytes 337928 | tf_op jit(solution)/shard_map/ppermute | solution.py:48
  62.4 5.4 %collective-permute-start.27 = (f16[88,577]{1,0:T(8,128)(2,1)S(1)}, f16[88,577]{1,0:T(8,128)(2,1)S(1)}, u32[]{:S(2)}, u32[]{:S(2)}) collective-permute-start(f16[88,577]{1,0:T(8,128)(2,1)S(1)} %convert_element_type.90), channel_id=1, source_target_pairs={{0,64},{64,0},{128,192},{192,128},{1,65},{65,1},{129,193},{193,129... | collective-permute-start | bytes 304664 | tf_op jit(solution)/shard_map/ppermute | solution.py:43
  64.3 11.6 %collective-permute-start.22 = (f16[88,640]{1,0:T(8,128)(2,1)S(1)}, f16[88,640]{1,0:T(8,128)(2,1)S(1)}, u32[]{:S(2)}, u32[]{:S(2)}) collective-permute-start(f16[88,640]{1,0:T(8,128)(2,1)S(1)} %convert_element_type.82), channel_id=1, source_target_pairs={{0,40},{8,48},{16,56},{24,0},{32,8},{40,16},{48,24},{56,32},{1,41}... | collective-permute-start | bytes 337928 | tf_op jit(solution)/shard_map/ppermute | solution.py:48
  68.2 8.9 %collective-permute-start.30 = (f16[88,577]{1,0:T(8,128)(2,1)S(1)}, f16[88,577]{1,0:T(8,128)(2,1)S(1)}, u32[]{:S(2)}, u32[]{:S(2)}) collective-permute-start(f16[88,577]{1,0:T(8,128)(2,1)S(1)} %convert_element_type.96), channel_id=1, source_target_pairs={{0,2},{2,0},{1,3},{3,1},{4,6},{6,4},{5,7},{7,5},{8,10},{10,8},{9,1... | collective-permute-start | bytes 304664 | tf_op jit(solution)/shard_map/ppermute | solution.py:43
  71.6 5.5 %collective-permute-start.33 = (f16[88,577]{1,0:T(8,128)(2,1)S(1)}, f16[88,577]{1,0:T(8,128)(2,1)S(1)}, u32[]{:S(2)}, u32[]{:S(2)}) collective-permute-start(f16[88,577]{1,0:T(8,128)(2,1)S(1)} %convert_element_type.102), channel_id=1, source_target_pairs={{0,192},{64,128},{128,64},{192,0},{1,193},{65,129},{129,65},{193,1... | collective-permute-start | bytes 304664 | tf_op jit(solution)/shard_map/ppermute | solution.py:43
  72.2 6.4 %collective-permute-start.32 = (f16[88,577]{1,0:T(8,128)(2,1)S(1)}, f16[88,577]{1,0:T(8,128)(2,1)S(1)}, u32[]{:S(2)}, u32[]{:S(2)}) collective-permute-start(f16[88,577]{1,0:T(8,128)(2,1)S(1)} %convert_element_type.100), channel_id=1, source_target_pairs={{0,128},{64,192},{128,0},{192,64},{1,129},{65,193},{129,1},{193,65... | collective-permute-start | bytes 304664 | tf_op jit(solution)/shard_map/ppermute | solution.py:43
  74.5 5.4 %collective-permute-start.31 = (f16[88,577]{1,0:T(8,128)(2,1)S(1)}, f16[88,577]{1,0:T(8,128)(2,1)S(1)}, u32[]{:S(2)}, u32[]{:S(2)}) collective-permute-start(f16[88,577]{1,0:T(8,128)(2,1)S(1)} %convert_element_type.98), channel_id=1, source_target_pairs={{0,64},{64,0},{128,192},{192,128},{1,65},{65,1},{129,193},{193,129... | collective-permute-start | bytes 304664 | tf_op jit(solution)/shard_map/ppermute | solution.py:43
  76.2 7.1 %collective-permute-start.24 = (f32[88,512]{1,0:T(8,128)S(1)}, f32[88,512]{1,0:T(8,128)S(1)}, u32[]{:S(2)}, u32[]{:S(2)}) collective-permute-start(f32[88,512]{1,0:T(8,128)S(1)} %get-tuple-element.76), channel_id=1, source_target_pairs={{0,2},{2,0},{1,3},{3,1},{4,6},{6,4},{5,7},{7,5},{8,10},{10,8},{9,1... | collective-permute-start | bytes 540680 | tf_op jit(solution)/shard_map/ppermute | solution.py:43
  (5 other events, 7.2 us)
